TPU v7x, 128 devices: a whole 4x4x4 slice. The times are simulated.
128 devices in a mesh: gx: 8 (over x_lo, y), gy: 4 (over x_hi, core), gz: 4 (over z).
Axes of the slice: x: 4 (x_hi: 2, x_lo: 2; x = x_hi * 2 + x_lo), y: 4, z: 4, core: 2. Of those that a mesh axis runs over, the one named last changes fastest.
Arguments:
- velocity: float32 [3, 80, 80, 2560], P(None, 'gx', 'gy', 'gz'), may hold values from -6 to 6
- obstacle_element_mask: int32 [16, 16, 512], P('gx', 'gy', 'gz'), may hold values 0 or 1
- element_metric_scale: float32 [16, 16, 512], P('gx', 'gy', 'gz'), may hold values from 0.5 to 8
Outputs:
- smoothed: float32 [80, 80, 2560], P('gx', 'gy', 'gz')
- coarse: float32 [16, 16, 512], P('gx', 'gy', 'gz')
All inputs are finite; a program needn't handle non-finite values. No bound on the sum of `obstacle_element_mask` on one device may be relied on, other than what follows from the above.
Results may differ from a plain program's by a relative error of at most 0.00012.
Values sent between devices are 32-bit elements; how exact they have to be, the bound alone decides.
No kernel may reach another device: no remote copies, remote signals or barrier semaphores. Data moves between devices by JAX's collectives and lax.ppermute only.
A program may use at most 384 MiB of HBM per device.

v0:
```python
import functools
import math

import jax
import jax.numpy as jnp
import ml_dtypes
import numpy as np
from jax import lax
from jax.experimental import pallas as pl
from jax.experimental.pallas import tpu as pltpu
from jax.sharding import PartitionSpec as P

LIFT = 10.0
STEP = 0.05
PENALTY = 4.0

BX, BY, BZ = 10, 20, 640
EX, EY, EZ = 2, 4, 128
PY = 24
ROWS = BX * PY
TILES = BZ // 128
WINDOWS = ((0, 256, 0, 384), (256, 512, 128, 640), (512, 640, 384, 640))
ZEDGE = 16

F32 = jnp.float32
BF16 = jnp.bfloat16


def lobatto_points():
    return np.array([-1.0, -math.sqrt(3.0 / 7.0), 0.0, math.sqrt(3.0 / 7.0), 1.0])


def lobatto_weights():
    return np.array([0.1, 49.0 / 90.0, 32.0 / 45.0, 49.0 / 90.0, 0.1])


def derivative_matrix():
    points = lobatto_points()
    scales = np.array(
        [np.prod([points[i] - points[k] for k in range(5) if k != i]) for i in range(5)]
    )
    result = np.zeros((5, 5))
    for i in range(5):
        for j in range(5):
            if i != j:
                result[i, j] = scales[i] / (scales[j] * (points[i] - points[j]))
        result[i, i] = -np.sum(result[i])
    return result


def eigen_basis_table():
    return np.array(
        [
            [
                math.sqrt((1.0 if k == 0 else 2.0) / 5.0) * math.cos(math.pi * (i + 0.5) * k / 5.0)
                for k in range(5)
            ]
            for i in range(5)
        ]
    )


def eigen_value_table():
    return np.array([4.0 * math.sin(math.pi * k / 10.0) ** 2 for k in range(5)])


def hat_weight_table():
    points = lobatto_points()
    weights = lobatto_weights()
    return np.array([weights * (1.0 - points) / 2.0, weights * (1.0 + points) / 2.0])


def inner_matrix():
    result = derivative_matrix()
    result[0, 0] += 0.5 * LIFT
    result[4, 4] -= 0.5 * LIFT
    return result


def line_operator(elements, coupled):
    inner = inner_matrix()
    size = 5 * elements
    m = np.zeros((size, size))
    for e in range(elements):
        m[5 * e : 5 * e + 5, 5 * e : 5 * e + 5] = inner
        if coupled and e > 0:
            m[5 * e, 5 * e - 1] = -0.5 * LIFT
        if coupled and e < elements - 1:
            m[5 * e + 4, 5 * e + 5] = 0.5 * LIFT
    return m


def hats_line(elements):
    h = hat_weight_table()
    m = np.zeros((elements + 1, 5 * elements))
    for e in range(elements):
        m[e, 5 * e : 5 * e + 5] += h[0]
        m[e + 1, 5 * e : 5 * e + 5] += h[1]
    return m


def slopes_line(elements):
    h = hat_weight_table()
    d = derivative_matrix()
    g = h @ d
    g[0, 0] += LIFT * h[0, 0]
    g[1, 4] -= LIFT * h[1, 4]
    m = np.zeros((elements + 1, 5 * elements))
    for e in range(elements):
        m[e, 5 * e : 5 * e + 5] += g[0]
        m[e + 1, 5 * e : 5 * e + 5] += g[1]
    return m


def pad_rows(m):
    out = np.zeros((m.shape[0], BX, PY))
    out[:, :, :BY] = m.reshape(m.shape[0], BX, BY)
    return out.reshape(m.shape[0], ROWS)


def pad_both(m):
    return pad_rows(pad_rows(m).T).T


def pad_to(m, rows, columns):
    out = np.zeros((rows, columns))
    out[: m.shape[0], : m.shape[1]] = m
    return out


class Packed:

    def __init__(self):
        self.parts = []
        self.places = {}
        self.rows = 0

    def add(self, name, m, parts=2):
        m = np.asarray(m, np.float64)
        hi = m.astype(np.float32).astype(ml_dtypes.bfloat16)
        lo = (m - hi.astype(np.float64)).astype(np.float32).astype(ml_dtypes.bfloat16)
        places = []
        for part in (hi, lo)[:parts]:
            wide = np.zeros((part.shape[0], 256), ml_dtypes.bfloat16)
            wide[:, : part.shape[1]] = part
            places.append((self.rows, part.shape[0], part.shape[1]))
            self.parts.append(wide)
            self.rows += part.shape[0]
        self.places[name] = places

    def add_windows(self, name, m):
        for i, (n0, n1, k0, k1) in enumerate(WINDOWS):
            self.add(name + str(i), m[k0:k1, n0:n1])

    def array(self):
        return jnp.asarray(np.concatenate(self.parts))

    def get(self, ref, name):
        out = [ref[r : r + n, 0:c] for r, n, c in self.places[name]]
        return out[0] if len(out) == 1 else out


def split(x):
    hi = x.astype(BF16)
    return hi, (x - hi.astype(F32)).astype(BF16)


def dot(a, b):
    return jnp.dot(a, b, preferred_element_type=F32)


def left_dot(m, hi, lo):
    return dot(m[0], hi) + dot(m[1], hi) + dot(m[0], lo)


def right_dot(hi, lo, m):
    return dot(hi, m[0]) + dot(lo, m[0]) + dot(hi, m[1])


def flag(name, low):
    edge = 0 if low else lax.axis_size(name) - 1
    return jnp.where(lax.axis_index(name) == edge, 0.0, 1.0)


def pack_kernel(v, mask, x_lo, x_hi, y_lo, y_hi, z_lo, z_hi, solid):
    solid[...] = mask[...].astype(F32).reshape(8, EZ)
    x_lo[...] = v[:, 0] * flag("gx", True)
    x_hi[...] = v[:, BX - 1] * flag("gx", False)
    y_low, y_high = flag("gy", True), flag("gy", False)
    lane = lax.broadcasted_iota(jnp.int32, (BY, 128), 1)
    low = jnp.zeros((BY, 128), F32)
    high = jnp.zeros((BY, 128), F32)
    for c in range(3):
        for x in range(BX):
            y_lo[c, x : x + 1, :] = v[c, x, 0:1, :] * y_low
            y_hi[c, x : x + 1, :] = v[c, x, BY - 1 : BY, :] * y_high
            here = lane == 16 * c + x
            low = jnp.where(here, jnp.broadcast_to(v[c, x, :, 0:1], (BY, 128)), low)
            high = jnp.where(here, jnp.broadcast_to(v[c, x, :, BZ - 1 : BZ], (BY, 128)), high)
    z_lo[0:BY, :] = low * flag("gz", True)
    z_hi[0:BY, :] = high * flag("gz", False)
    z_lo[BY:PY, :] = jnp.zeros((PY - BY, 128), F32)
    z_hi[BY:PY, :] = jnp.zeros((PY - BY, 128), F32)


def plane_sums(planes, scale):
    d = inner_matrix() * scale
    outs = []
    for i in range(5):
        total = None
        for j in range(5):
            if abs(d[i, j]) < 1e-12:
                continue
            term = float(d[i, j]) * planes[j]
            total = term if total is None else total + term
        outs.append(total)
    return outs


def step_kernel(
    packed, v, hx_lo, hx_hi, hy_lo, hy_hi, hz_lo, hz_hi, solid, weights,
    rhs, xp, xm, yp, ym, zp, zm, own,
    V, FH, FL, conv, prov, PH, PL,
):
    for c in range(3):
        V[c, 0, 0:BY, 128:768] = hx_lo[c]
        V[c, BX + 1, 0:BY, 128:768] = hx_hi[c]
        V[c, 0, BY:PY, 128:768] = jnp.zeros((PY - BY, BZ), F32)
        V[c, BX + 1, BY:PY, 128:768] = jnp.zeros((PY - BY, BZ), F32)
        for x in range(BX):
            V[c, x + 1, 0:BY, 128:768] = v[c, x]
            V[c, x + 1, 20:22, 128:768] = jnp.broadcast_to(hy_hi[c, x : x + 1, :], (2, BZ))
            V[c, x + 1, 22:24, 128:768] = jnp.broadcast_to(hy_lo[c, x : x + 1, :], (2, BZ))
            k = 16 * c + x
            V[c, x + 1, :, 0:128] = jnp.broadcast_to(hz_lo[:, k : k + 1], (PY, 128))
            V[c, x + 1, :, 768:896] = jnp.broadcast_to(hz_hi[:, k : k + 1], (PY, 128))

    def products(t, carry):
        src = pl.ds(pl.multiple_of(128 + 128 * t, 128), 128)
        dst = pl.ds(pl.multiple_of(128 * t, 128), 128)
        for q in range(BX // 2):
            a = [V[c, 1 + 2 * q : 3 + 2 * q, :, src].reshape(2 * PY, 128) for c in range(3)]
            pairs = (a[0] * a[1], a[1] * a[1], a[1] * a[2], a[0] * a[2], a[2] * a[2])
            for f, value in enumerate(pairs):
                hi, lo = split(value)
                FH[f, 2 * PY * q : 2 * PY * (q + 1), dst] = hi
                FL[f, 2 * PY * q : 2 * PY * (q + 1), dst] = lo
        return carry

    lax.fori_loop(0, TILES, products, 0)

    my = packed.get(weights, "my")
    for i, (n0, n1, k0, k1) in enumerate(WINDOWS):
        b = packed.get(weights, "bz" + str(i))
        for c in range(3):
            along_z = (3, 2, 4)[c]
            y = left_dot(my, FH[c, :, n0:n1], FL[c, :, n0:n1])
            z = right_dot(FH[along_z, :, k0:k1], FL[along_z, :, k0:k1], b)
            conv[c, :, :, n0:n1] = (y + z).reshape(BX, PY, n1 - n0)

    def along_x(t, carry):
        src = pl.ds(pl.multiple_of(128 + 128 * t, 128), 128)
        dst = pl.ds(pl.multiple_of(128 * t, 128), 128)
        for e in range(EX):
            v0 = [V[0, 1 + 5 * e + i, :, src] for i in range(5)]
            for c in range(3):
                flux = [v0[i] * V[c, 1 + 5 * e + i, :, src] for i in range(5)]
                for i, total in enumerate(plane_sums(flux, -STEP)):
                    conv[c, 5 * e + i, :, dst] = conv[c, 5 * e + i, :, dst] + total
        return carry

    lax.fori_loop(0, TILES, along_x, 0)

    solid = spread_out(packed, weights, [solid[...].astype(BF16)])
    conv_scale = -0.5 * LIFT * STEP
    lane = lax.broadcasted_iota(jnp.int32, (PY, 128), 1)
    row = lax.broadcasted_iota(jnp.int32, (PY, 128), 0)
    row_left = (lax.rem(row, 5) == 0) & (row < BY)
    row_right = (lax.rem(row, 5) == 4) & (row < BY)
    y_face = jnp.where(row_left | row_right, conv_scale, 0.0)
    y_sign = jnp.where(row_left, conv_scale, jnp.where(row_right, -conv_scale, 0.0))
    damp = [1.0 / (1.0 + PENALTY * solid[PY * e : PY * (e + 1)]) for e in range(EX)]
    for t in range(TILES):
        point = lax.rem(lane + 128 * t, 5)
        z_left = point == 0
        z_face = jnp.where(z_left | (point == 4), conv_scale, 0.0)
        z_sign = jnp.where(z_left, conv_scale, jnp.where(point == 4, -conv_scale, 0.0))
        here = slice(128 + 128 * t, 256 + 128 * t)
        before = slice(128 * t, 128 + 128 * t)
        after = slice(256 + 128 * t, 384 + 128 * t)
        out = slice(128 * t, 128 + 128 * t)
        for x in range(BX):
            a = [V[c, x + 1, :, here] for c in range(3)]
            total = [conv[c, x, :, out] for c in range(3)]
            w = []
            for c in range(3):
                lo = pltpu.roll(jnp.where(lane == 127, V[c, x + 1, :, before], a[c]), 1, 1)
                hi = pltpu.roll(jnp.where(lane == 0, V[c, x + 1, :, after], a[c]), 127, 1)
                w.append(jnp.where(z_left, lo, hi))
            p = z_face * jnp.maximum(jnp.abs(a[2]), jnp.abs(w[2]))
            q = p + z_sign * w[2]
            total = [total[c] + (p * a[c] - q * w[c]) for c in range(3)]
            w = [
                jnp.where(row_left, pltpu.roll(a[c], 1, 0), pltpu.roll(a[c], PY - 1, 0))
                for c in range(3)
            ]
            p = y_face * jnp.maximum(jnp.abs(a[1]), jnp.abs(w[1]))
            q = p + y_sign * w[1]
            total = [total[c] + (p * a[c] - q * w[c]) for c in range(3)]
            if x % 5 in (0, 4):
                other = x if x % 5 == 0 else x + 2
                sign = 1.0 if x % 5 == 0 else -1.0
                w = [V[c, other, :, here] for c in range(3)]
                p = conv_scale * jnp.maximum(jnp.abs(a[0]), jnp.abs(w[0]))
                q = p + (sign * conv_scale) * w[0]
                total = [total[c] + (p * a[c] - q * w[c]) for c in range(3)]
            factor = damp[x // 5][:, out]
            for c in range(3):
                prov[c, x, :, out] = (a[c] + total[c]) * factor

    for q in range(BX // 2):
        for c in range(3):
            hi, lo = split(prov[c, 2 * q : 2 * q + 2].reshape(2 * PY, BZ))
            PH[c, 2 * PY * q : 2 * PY * (q + 1), :] = hi
            PL[c, 2 * PY * q : 2 * PY * (q + 1), :] = lo
    ry = packed.get(weights, "ry")
    for i, (n0, n1, k0, k1) in enumerate(WINDOWS):
        b = packed.get(weights, "rz" + str(i))
        y = left_dot(ry, PH[1, :, n0:n1], PL[1, :, n0:n1])
        z = right_dot(PH[2, :, k0:k1], PL[2, :, k0:k1], b)
        rhs[:, :, n0:n1] = (y + z).reshape(BX, PY, n1 - n0)

    def right_x(t, carry):
        dst = pl.ds(pl.multiple_of(128 * t, 128), 128)
        planes = [prov[0, x, :, dst] for x in range(BX)]
        outs = plane_sums(planes[:5], -1.0) + plane_sums(planes[5:], -1.0)
        outs[4] = outs[4] - 0.5 * LIFT * planes[5]
        outs[5] = outs[5] + 0.5 * LIFT * planes[4]
        for x in range(BX):
            rhs[x, :, dst] = rhs[x, :, dst] + outs[x]
        return carry

    lax.fori_loop(0, TILES, right_x, 0)

    first = [1.0 - flag(name, True) for name in ("gx", "gy", "gz")]
    x_low, y_low, z_low = (flag(name, True) for name in ("gx", "gy", "gz"))
    x_high, y_high, z_high = (flag(name, False) for name in ("gx", "gy", "gz"))
    parts = []
    c0, c1, c2, d0, d1 = (
        sum(part.astype(F32) for part in packed.get(weights, n)) for n in ("c0", "c1", "c2", "d0", "d1")
    )
    for c, m in enumerate((c0 + first[0] * d0, c1 + first[1] * d1, c2)):
        hi, lo = split(m)
        parts.append(dot(hi, PH[c]) + dot(lo, PH[c]) + dot(hi, PL[c]))
    hi, lo = split(parts[0] + parts[1])
    coarse = right_dot(hi, lo, packed.get(weights, "hz"))
    hi, lo = split(parts[2])
    coarse = coarse + right_dot(hi, lo, packed.get(weights, "gz"))
    lane16 = lax.broadcasted_iota(jnp.int32, (16, 128), 1)
    vertices = coarse[:, 0:128] - jnp.where(
        lane16 == 0, (0.5 * LIFT * 0.1) * first[2] * parts[2][:, 0:128], 0.0
    )
    row16 = lax.broadcasted_iota(jnp.int32, (16, 128), 0)
    there = jnp.where(row16 >= 10, x_high, 1.0) * jnp.where(lax.rem(row16, 5) == 4, y_high, 1.0)
    vertices = vertices * there
    edge = coarse[:, 128:256] * (there * z_high)
    edge_next = pltpu.roll(edge, 1, 1)
    own[...] = vertices

    xp[0:PY, :] = prov[0, BX - 1] * x_high
    xm[...] = prov[0, 0] * x_low
    xp[24:32, :] = jnp.zeros((8, BZ), F32)
    xp[24:29, 0:128] = vertices[10:15]
    xp[24:29, 128:256] = edge[10:15]
    yp[8:24, :] = jnp.zeros((16, BZ), F32)
    ym[8:16, :] = jnp.zeros((8, BZ), F32)
    lane24 = lax.broadcasted_iota(jnp.int32, (PY, 128), 1)
    low = jnp.zeros((PY, 128), F32)
    high = jnp.zeros((PY, 128), F32)
    for x in range(BX):
        yp[x : x + 1, :] = prov[1, x, BY - 1 : BY, :] * y_high
        ym[x : x + 1, :] = prov[1, x, 0:1, :] * y_low
        low = jnp.where(lane24 == x, jnp.broadcast_to(prov[2, x, :, 0:1], (PY, 128)), low)
        high = jnp.where(lane24 == x, jnp.broadcast_to(prov[2, x, :, BZ - 1 : BZ], (PY, 128)), high)
    yp[16:17, 0:128] = vertices[4:5]
    yp[17:18, 0:128] = vertices[9:10]
    yp[16:17, 128:256] = edge[4:5] + edge_next[9:10]
    zm[...] = low * z_low
    zp[...] = high * z_high
    zp[0:4, :] = zp[0:4, :] + (edge[0:4] + edge_next[5:9])


def spread_out(packed, weights, parts):
    rows_of = packed.get(weights, "rows_of")
    wide = []
    for i in range(3):
        m = packed.get(weights, "spread" + str(i))
        wide.append(sum(dot(part, m) for part in parts))
    return sum(dot(rows_of, part) for part in split(jnp.concatenate(wide, axis=1))[: len(parts)])


def smooth_kernel(
    packed, rhs, hx_lo, hx_hi, hy_lo, hy_hi, hz_lo, hz_hi, own, scale, weights, modes,
    smoothed, coarse, AH, AL, BH, BL,
):
    lift = 0.5 * LIFT
    lane = lax.broadcasted_iota(jnp.int32, (PY, 128), 1)
    row = lax.broadcasted_iota(jnp.int32, (PY, BZ), 0)
    for q in range(BX // 2):
        planes = []
        for x in (2 * q, 2 * q + 1):
            r = rhs[x]
            if x == 0:
                r = r + lift * hx_lo[0:PY, :]
            if x == BX - 1:
                r = r - lift * hx_hi[...]
            r = r + jnp.where(row == 0, lift * jnp.broadcast_to(hy_lo[x : x + 1, :], (PY, BZ)), 0.0)
            r = r - jnp.where(
                row == BY - 1, lift * jnp.broadcast_to(hy_hi[x : x + 1, :], (PY, BZ)), 0.0
            )
            left = r[:, 0:128] + jnp.where(
                lane == 0, lift * jnp.broadcast_to(hz_lo[:, x : x + 1], (PY, 128)), 0.0
            )
            right = r[:, BZ - 128 : BZ] - jnp.where(
                lane == 127, lift * jnp.broadcast_to(hz_hi[:, x : x + 1], (PY, 128)), 0.0
            )
            planes.append(jnp.concatenate([left, r[:, 128 : BZ - 128], right], axis=1))
        hi, lo = split(jnp.concatenate(planes, axis=0))
        AH[2 * PY * q : 2 * PY * (q + 1), :] = hi
        AL[2 * PY * q : 2 * PY * (q + 1), :] = lo

    for n0, n1, _, _ in WINDOWS:
        hi, lo = split(left_dot(packed.get(weights, "tf"), AH[:, n0:n1], AL[:, n0:n1]))
        BH[:, n0:n1] = hi
        BL[:, n0:n1] = lo

    factor = spread_out(packed, weights, split(scale[...].reshape(8, EZ)))
    values = eigen_value_table()
    for i, (n0, n1, k0, k1) in enumerate(WINDOWS):
        m = packed.get(weights, "sf" + str(i))
        c = right_dot(BH[:, k0:k1], BL[:, k0:k1], m).reshape(BX, PY, n1 - n0)
        done = []
        for x in range(BX):
            f = factor[PY * (x // 5) : PY * (x // 5 + 1), n0:n1]
            done.append(c[x] / (f * (modes[:, n0:n1] + float(values[x % 5])) + 1.0))
        hi, lo = split(jnp.concatenate(done, axis=0))
        AH[:, n0:n1] = hi
        AL[:, n0:n1] = lo

    for i, (n0, n1, k0, k1) in enumerate(WINDOWS):
        m = packed.get(weights, "sb" + str(i))
        hi, lo = split(right_dot(AH[:, k0:k1], AL[:, k0:k1], m))
        BH[:, n0:n1] = hi
        BL[:, n0:n1] = lo

    for n0, n1, _, _ in WINDOWS:
        c = left_dot(packed.get(weights, "tb"), BH[:, n0:n1], BL[:, n0:n1]).reshape(BX, PY, n1 - n0)
        smoothed[:, :, n0:n1] = c[:, 0:BY]

    lane4 = lax.broadcasted_iota(jnp.int32, (4, 128), 1)
    row4 = lax.broadcasted_iota(jnp.int32, (4, 128), 0)
    for vx in range(EX):
        total = own[5 * vx : 5 * vx + 4, :]
        if vx == 0:
            total = total + hx_lo[24:28, 0:128]
        total = total + jnp.where(
            row4 == 0, jnp.broadcast_to(hy_lo[16 + vx : 17 + vx, 0:128], (4, 128)), 0.0
        )
        k = ZEDGE + vx
        total = total + jnp.where(
            lane4 == 0, jnp.broadcast_to(hz_lo[0:4, k : k + 1], (4, 128)), 0.0
        )
        coarse[vx] = total


def constants():
    step, smooth = Packed(), Packed()
    eye_x = np.eye(BX)
    step.add("my", pad_both(np.kron(eye_x, -STEP * line_operator(EY, False))))
    step.add("ry", pad_both(np.kron(eye_x, -line_operator(EY, True))))
    step.add_windows("bz", -STEP * line_operator(EZ, False).T)
    step.add_windows("rz", -line_operator(EZ, True).T)
    basis = eigen_basis_table()
    sx = np.kron(np.eye(EX), basis)
    sy = np.kron(np.eye(EY), basis)
    sz = np.kron(np.eye(EZ), basis)
    t = np.kron(sx, sy)
    smooth.add("tf", pad_both(t.T))
    smooth.add("tb", pad_both(t))
    smooth.add_windows("sf", sz)
    smooth.add_windows("sb", sz.T)
    spread = np.kron(np.eye(EZ), np.ones((1, 5)))
    rows_of = np.zeros((EX * PY, 8))
    for e in range(EX):
        for y in range(BY):
            rows_of[PY * e + y, EY * e + y // 5] = 1.0
    for packed in (step, smooth):
        packed.add("rows_of", rows_of, 1)
        for i, (n0, n1, _, _) in enumerate(WINDOWS):
            packed.add("spread" + str(i), spread[:, n0:n1], 1)
    values = eigen_value_table()
    modes = np.zeros((PY, BZ))
    for y in range(BY):
        modes[y] = values[y % 5] + np.tile(values, EZ)
    hx, hy, hz = hats_line(EX), hats_line(EY), hats_line(EZ)
    gx, gy, gz = slopes_line(EX), slopes_line(EY), slopes_line(EZ)
    for name, m in (("hz", hz), ("gz", gz)):
        wide = np.zeros((BZ, 256))
        wide[:, 0:EZ] = m[:EZ].T
        wide[:, 128 + ZEDGE] = m[EZ]
        step.add(name, wide)
    half = 0.5 * LIFT * hat_weight_table()[0, 0]
    ex, ey = np.zeros_like(gx), np.zeros_like(gy)
    ex[0, 0] = -half
    ey[0, 0] = -half
    for name, m in (
        ("c0", np.kron(gx, hy)),
        ("c1", np.kron(hx, gy)),
        ("c2", np.kron(hx, hy)),
        ("d0", np.kron(ex, hy)),
        ("d1", np.kron(hx, ey)),
    ):
        step.add(name, pad_to(pad_rows(-m), 16, ROWS))
    return step, smooth, modes.astype(np.float32)


def shift(x, axis, by):
    size = lax.axis_size(axis)
    return lax.ppermute(x, axis, [(i, (i + by) % size) for i in range(size)])


def like(*shape):
    return jax.ShapeDtypeStruct(shape, F32)


def run(kernel, outs, operands, scratch=(), name=None, flops=0, moved=0):
    vmem = pl.BlockSpec(memory_space=pltpu.VMEM)
    return pl.pallas_call(
        kernel,
        out_shape=outs,
        in_specs=[vmem] * len(operands),
        out_specs=[vmem] * len(outs),
        scratch_shapes=list(scratch),
        compiler_params=pltpu.CompilerParams(vmem_limit_bytes=40 * 2**20),
        cost_estimate=pl.CostEstimate(flops=flops, bytes_accessed=moved, transcendentals=0),
        name=name,
    )(*operands)


def shards(velocity, obstacle_element_mask, element_metric_scale):
    step, smooth, modes = constants()
    faces = run(
        pack_kernel,
        [like(3, BY, BZ)] * 2 + [like(3, BX, BZ)] * 2 + [like(PY, 128)] * 2 + [like(8, EZ)],
        [velocity, obstacle_element_mask],
        name="pack",
        flops=10**10,
        moved=4 << 20,
    )
    halo = [
        shift(faces[1], "gx", 1),
        shift(faces[0], "gx", -1),
        shift(faces[3], "gy", 1),
        shift(faces[2], "gy", -1),
        shift(faces[5], "gz", 1),
    ]
    halo[0], last = lax.optimization_barrier((halo[0], faces[4]))
    halo.append(shift(last, "gz", -1))
    rhs, xp, xm, yp, ym, zp, zm, own = run(
        functools.partial(step_kernel, step),
        [
            like(BX, PY, BZ),
            like(32, BZ),
            like(PY, BZ),
            like(24, BZ),
            like(16, BZ),
            like(PY, 128),
            like(PY, 128),
            like(16, 128),
        ],
        [velocity, *halo, faces[6], step.array()],
        scratch=[
            pltpu.VMEM((3, BX + 2, PY, 896), F32),
            pltpu.VMEM((5, ROWS, BZ), BF16),
            pltpu.VMEM((5, ROWS, BZ), BF16),
            pltpu.VMEM((3, BX, PY, BZ), F32),
            pltpu.VMEM((3, BX, PY, BZ), F32),
            pltpu.VMEM((3, ROWS, BZ), BF16),
            pltpu.VMEM((3, ROWS, BZ), BF16),
        ],
        name="step",
        flops=4 * 10**9,
        moved=8 << 20,
    )
    gx_lo = shift(xp, "gx", 1)
    gx_hi = shift(xm, "gx", -1)
    yp = yp + jnp.pad(gx_lo[28:29, 0:256], ((16, 7), (0, BZ - 256)))
    gy_lo = shift(yp, "gy", 1)
    gy_hi = shift(ym, "gy", -1)
    zp = zp + jnp.pad(gx_lo[24:28, 128:256], ((0, 20), (0, 0)))
    zp = zp + jnp.pad(gy_lo[16:17, 128:256], ((0, 23), (0, 0)))
    gz_lo = shift(zp, "gz", 1)
    gz_hi = shift(zm, "gz", -1)
    smoothed, coarse = run(
        functools.partial(smooth_kernel, smooth),
        [like(BX, BY, BZ), like(EX, EY, EZ)],
        [rhs, gx_lo, gx_hi, gy_lo, gy_hi, gz_lo, gz_hi, own, element_metric_scale]
        + [smooth.array(), jnp.asarray(modes)],
        scratch=[pltpu.VMEM((ROWS, BZ), BF16)] * 4,
        name="smooth",
        flops=3 * 10**9,
        moved=6 << 20,
    )
    return (smoothed, coarse)


def solution(mesh):
    return jax.shard_map(
        shards,
        mesh=mesh,
        in_specs=(P(None, "gx", "gy", "gz"), P("gx", "gy", "gz"), P("gx", "gy", "gz")),
        out_specs=(P("gx", "gy", "gz"), P("gx", "gy", "gz")),
        check_vma=False,
    )
```

profile of v0, /device:TPU:14, one launch (start us, length us, event | category | flops | bytes accessed | tf_op | source)
XLA Modules:
  0.0 48.3 jit_solution(7762757923674888739)
XLA Ops:
  0.6 0.0 copy-start
  0.6 1.5 %copy-done = f32[3,10,20,640]{3,2,1,0:T(8,128)S(1)} copy-done((f32[3,10,20,640]{3,2,1,0:T(8,128)S(1)}, f32[3,10,20,640]{3,2,1,0:T(8,128)}, u32[]{:S(2)}) %copy-start) | copy-done | bytes 1536024
  2.1 0.0 copy-start.1
  2.1 0.7 %copy-done.1 = s32[2,4,128]{2,1,0:T(4,128)S(1)} copy-done((s32[2,4,128]{2,1,0:T(4,128)S(1)}, s32[2,4,128]{2,1,0:T(4,128)}, u32[]{:S(2)}) %copy-start.1) | copy-done | bytes 4120
  2.8 0.0 copy-start.3
  2.8 0.4 pack.1
  3.2 1.6 %collective-permute-start = (f32[3,20,640]{2,1,0:T(8,128)S(1)}, f32[3,20,640]{2,1,0:T(8,128)S(1)}, u32[]{:S(2)}, u32[]{:S(2)}) collective-permute-start(f32[3,20,640]{2,1,0:T(8,128)S(1)} %get-tuple-element.19), channel_id=1, source_target_pairs={{0,16},{16,32},{32,48},{48,64},{64,80},{80,96},{96,112},{112,0},{1... | collective-permute-start | bytes 460808 | tf_op jit(solution)/shard_map/ppermute | solution.py:529
  4.9 0.4 collective-permute-start.1
  5.3 0.0 collective-permute-start.2
  5.3 3.2 %collective-permute-start.3 = (f32[3,10,640]{2,1,0:T(8,128)S(1)}, f32[3,10,640]{2,1,0:T(8,128)S(1)}, u32[]{:S(2)}, u32[]{:S(2)}) collective-permute-start(f32[3,10,640]{2,1,0:T(8,128)S(1)} %get-tuple-element.24), channel_id=1, source_target_pairs={{0,12},{4,0},{8,4},{12,8},{1,13},{5,1},{9,5},{13,9},{2,14},{6,2},{... | collective-permute-start | bytes 230408 | tf_op jit(solution)/shard_map/ppermute | solution.py:529
  8.6 1.9 %collective-permute-start.4 = (f32[24,128]{1,0:T(8,128)S(1)}, f32[24,128]{1,0:T(8,128)S(1)}, u32[]{:S(2)}, u32[]{:S(2)}) collective-permute-start(f32[24,128]{1,0:T(8,128)S(1)} %get-tuple-element.25), channel_id=1, source_target_pairs={{0,1},{1,2},{2,3},{3,0},{4,5},{5,6},{6,7},{7,4},{8,9},{9,10},{10,1... | collective-permute-start | bytes 36872 | tf_op jit(solution)/shard_map/ppermute | solution.py:529
  10.5 0.0 collective-permute-done.hx_lo
  10.5 3.2 %collective-permute-start.5 = (f32[24,128]{1,0:T(8,128)S(1)}, f32[24,128]{1,0:T(8,128)S(1)}, u32[]{:S(2)}, u32[]{:S(2)}) collective-permute-start(f32[24,128]{1,0:T(8,128)S(1)} %get-tuple-element.26), channel_id=1, source_target_pairs={{0,3},{1,0},{2,1},{3,2},{4,7},{5,4},{6,5},{7,6},{8,11},{9,8},{10,9... | collective-permute-start | bytes 36872 | tf_op jit(solution)/shard_map/ppermute | solution.py:529
  13.7 0.6 %collective-permute-done.4.hz_lo = f32[24,128]{1,0:T(8,128)S(1)} collective-permute-done((f32[24,128]{1,0:T(8,128)S(1)}, f32[24,128]{1,0:T(8,128)S(1)}, u32[]{:S(2)}, u32[]{:S(2)}) %collective-permute-start.4) | collective-permute-done | bytes 12320 | tf_op jit(solution)/shard_map/ppermute | solution.py:529
  14.3 0.0 collective-permute-done.2.hy_lo
  14.3 0.0 collective-permute-done.3.hy_hi
  14.3 0.0 collective-permute-done.1.hx_hi
  14.3 0.8 %collective-permute-done.5.hz_hi = f32[24,128]{1,0:T(8,128)S(1)} collective-permute-done((f32[24,128]{1,0:T(8,128)S(1)}, f32[24,128]{1,0:T(8,128)S(1)}, u32[]{:S(2)}, u32[]{:S(2)}) %collective-permute-start.5) | collective-permute-done | bytes 12320 | tf_op jit(solution)/shard_map/ppermute | solution.py:529
  15.1 0.0 copy-done.3
  15.1 0.0 copy-start.2
  15.1 0.0 copy-start.4
  15.1 0.0 copy-start.5
  15.1 8.4 %step.1 = (f32[10,24,640]{2,1,0:T(8,128)S(1)}, f32[32,640]{1,0:T(8,128)S(1)}, f32[24,640]{1,0:T(8,128)S(1)}, f32[24,640]{1,0:T(8,128)S(1)}, f32[16,640]{1,0:T(8,...) custom-call(f32[3,10,20,640]{3,2,1,0:T(8,128)S(1)} %copy-done, ...), custom_call_target="tpu_custom_call" | custom-call | flops 4000000000 | bytes 8388608 | tf_op jit(solution)/shard_map/step/pallas_call | solution.py:538
  23.5 1.6 %collective-permute-start.6 = (f32[32,640]{1,0:T(8,128)S(1)}, f32[32,640]{1,0:T(8,128)S(1)}, u32[]{:S(2)}, u32[]{:S(2)}) collective-permute-start(f32[32,640]{1,0:T(8,128)S(1)} %get-tuple-element.29), channel_id=1, source_target_pairs={{0,16},{16,32},{32,48},{48,64},{64,80},{80,96},{96,112},{112,0},{1... | collective-permute-start | bytes 245768 | tf_op jit(solution)/shard_map/ppermute | solution.py:529
  25.1 4.6 %collective-permute-done.6.hx_lo = f32[32,640]{1,0:T(8,128)S(1)} collective-permute-done((f32[32,640]{1,0:T(8,128)S(1)}, f32[32,640]{1,0:T(8,128)S(1)}, u32[]{:S(2)}, u32[]{:S(2)}) %collective-permute-start.6) | collective-permute-done | bytes 81952 | tf_op jit(solution)/shard_map/ppermute | solution.py:529
  29.7 0.1 collective-permute-start.8
  29.8 3.6 %collective-permute-start.11 = (f32[24,128]{1,0:T(8,128)S(1)}, f32[24,128]{1,0:T(8,128)S(1)}, u32[]{:S(2)}, u32[]{:S(2)}) collective-permute-start(f32[24,128]{1,0:T(8,128)S(1)} %get-tuple-element.34), channel_id=1, source_target_pairs={{0,3},{1,0},{2,1},{3,2},{4,7},{5,4},{6,5},{7,6},{8,11},{9,8},{10,9... | collective-permute-start | bytes 36872 | tf_op jit(solution)/shard_map/ppermute | solution.py:529
  33.3 2.9 %collective-permute-start.9 = (f32[16,640]{1,0:T(8,128)S(1)}, f32[16,640]{1,0:T(8,128)S(1)}, u32[]{:S(2)}, u32[]{:S(2)}) collective-permute-start(f32[16,640]{1,0:T(8,128)S(1)} %get-tuple-element.32), channel_id=1, source_target_pairs={{0,12},{4,0},{8,4},{12,8},{1,13},{5,1},{9,5},{13,9},{2,14},{6,2},{... | collective-permute-start | bytes 122888 | tf_op jit(solution)/shard_map/ppermute | solution.py:529
  36.2 4.1 %collective-permute-start.7 = (f32[24,640]{1,0:T(8,128)S(1)}, f32[24,640]{1,0:T(8,128)S(1)}, u32[]{:S(2)}, u32[]{:S(2)}) collective-permute-start(f32[24,640]{1,0:T(8,128)S(1)} %get-tuple-element.30), channel_id=1, source_target_pairs={{0,112},{16,0},{32,16},{48,32},{64,48},{80,64},{96,80},{112,96},{1... | collective-permute-start | bytes 184328 | tf_op jit(solution)/shard_map/ppermute | solution.py:529
  40.4 0.0 collective-permute-done.8.hy_lo
  40.4 0.1 collective-permute-start.10
  40.5 0.0 collective-permute-done.11.hz_hi
  40.5 0.0 collective-permute-done.9.hy_hi
  40.5 1.7 %collective-permute-done.7.hx_hi = f32[24,640]{1,0:T(8,128)S(1)} collective-permute-done((f32[24,640]{1,0:T(8,128)S(1)}, f32[24,640]{1,0:T(8,128)S(1)}, u32[]{:S(2)}, u32[]{:S(2)}) %collective-permute-start.7) | collective-permute-done | bytes 61472 | tf_op jit(solution)/shard_map/ppermute | solution.py:529
  42.2 3.1 %collective-permute-done.10.hz_lo = f32[24,128]{1,0:T(8,128)S(1)} collective-permute-done((f32[24,128]{1,0:T(8,128)S(1)}, f32[24,128]{1,0:T(8,128)S(1)}, u32[]{:S(2)}, u32[]{:S(2)}) %collective-permute-start.10) | collective-permute-done | bytes 12320 | tf_op jit(solution)/shard_map/ppermute | solution.py:529
  45.4 0.0 copy-done.2
  45.4 0.0 copy-done.4
  45.4 0.0 copy-done.5
  45.4 2.9 %smooth.1 = (f32[10,20,640]{2,1,0:T(8,128)}, f32[2,4,128]{2,1,0:T(4,128)}) custom-call(f32[10,24,640]{2,1,0:T(8,128)S(1)} %get-tuple-element.28.rhs, f32[32,640]{1,0:T(8,128)S(1)} %collective-permute-done.6.hx_lo, f32[24,640]{1,0:T(8,128)S(1)} %collective-permute-done.7.hx_hi, f32[24,640]{1,0:T(8,128)S(1)} %collective-permute-done.8.hy_lo, ...), custom_call_target="tpu_custom_call" | custom-call | flops 3000000000 | bytes 6291456 | tf_op jit(solution)/shard_map/smooth/pallas_call | solution.py:538
  (5 shorter events, 0.0 us)
Async XLA Ops:
  0.6 1.5 %copy-start = (f32[3,10,20,640]{3,2,1,0:T(8,128)S(1)}, f32[3,10,20,640]{3,2,1,0:T(8,128)}, u32[]{:S(2)}) copy-start(f32[3,10,20,640]{3,2,1,0:T(8,128)} %v.3) | copy-start | bytes 4608004
  2.1 0.7 %copy-start.1 = (s32[2,4,128]{2,1,0:T(4,128)S(1)}, s32[2,4,128]{2,1,0:T(4,128)}, u32[]{:S(2)}) copy-start(s32[2,4,128]{2,1,0:T(4,128)} %mask.1) | copy-start | bytes 12292
  2.8 12.3 %copy-start.3 = (bf16[8720,256]{1,0:T(8,128)(2,1)S(1)}, bf16[8720,256]{1,0:T(8,128)(2,1)}, u32[]{:S(2)}) copy-start(bf16[8720,256]{1,0:T(8,128)(2,1)} %constant.9.clone.weights) | copy-start | bytes 13393924
  3.2 7.3 %collective-permute-start = (f32[3,20,640]{2,1,0:T(8,128)S(1)}, f32[3,20,640]{2,1,0:T(8,128)S(1)}, u32[]{:S(2)}, u32[]{:S(2)}) collective-permute-start(f32[3,20,640]{2,1,0:T(8,128)S(1)} %get-tuple-element.19), channel_id=1, source_target_pairs={{0,16},{16,32},{32,48},{48,64},{64,80},{80,96},{96,112},{112,0},{1... | collective-permute-start | bytes 460808 | tf_op jit(solution)/shard_map/ppermute | solution.py:529
  4.9 9.4 %collective-permute-start.1 = (f32[3,20,640]{2,1,0:T(8,128)S(1)}, f32[3,20,640]{2,1,0:T(8,128)S(1)}, u32[]{:S(2)}, u32[]{:S(2)}) collective-permute-start(f32[3,20,640]{2,1,0:T(8,128)S(1)} %get-tuple-element.22), channel_id=1, source_target_pairs={{0,112},{16,0},{32,16},{48,32},{64,48},{80,64},{96,80},{112,96},{1... | collective-permute-start | bytes 460808 | tf_op jit(solution)/shard_map/ppermute | solution.py:529
  5.3 9.0 %collective-permute-start.2 = (f32[3,10,640]{2,1,0:T(8,128)S(1)}, f32[3,10,640]{2,1,0:T(8,128)S(1)}, u32[]{:S(2)}, u32[]{:S(2)}) collective-permute-start(f32[3,10,640]{2,1,0:T(8,128)S(1)} %get-tuple-element.23), channel_id=1, source_target_pairs={{0,4},{4,8},{8,12},{12,0},{1,5},{5,9},{9,13},{13,1},{2,6},{6,10},{... | collective-permute-start | bytes 230408 | tf_op jit(solution)/shard_map/ppermute | solution.py:529
  5.3 9.0 %collective-permute-start.3 = (f32[3,10,640]{2,1,0:T(8,128)S(1)}, f32[3,10,640]{2,1,0:T(8,128)S(1)}, u32[]{:S(2)}, u32[]{:S(2)}) collective-permute-start(f32[3,10,640]{2,1,0:T(8,128)S(1)} %get-tuple-element.24), channel_id=1, source_target_pairs={{0,12},{4,0},{8,4},{12,8},{1,13},{5,1},{9,5},{13,9},{2,14},{6,2},{... | collective-permute-start | bytes 230408 | tf_op jit(solution)/shard_map/ppermute | solution.py:529
  8.6 5.7 %collective-permute-start.4 = (f32[24,128]{1,0:T(8,128)S(1)}, f32[24,128]{1,0:T(8,128)S(1)}, u32[]{:S(2)}, u32[]{:S(2)}) collective-permute-start(f32[24,128]{1,0:T(8,128)S(1)} %get-tuple-element.25), channel_id=1, source_target_pairs={{0,1},{1,2},{2,3},{3,0},{4,5},{5,6},{6,7},{7,4},{8,9},{9,10},{10,1... | collective-permute-start | bytes 36872 | tf_op jit(solution)/shard_map/ppermute | solution.py:529
  10.5 4.6 %collective-permute-start.5 = (f32[24,128]{1,0:T(8,128)S(1)}, f32[24,128]{1,0:T(8,128)S(1)}, u32[]{:S(2)}, u32[]{:S(2)}) collective-permute-start(f32[24,128]{1,0:T(8,128)S(1)} %get-tuple-element.26), channel_id=1, source_target_pairs={{0,3},{1,0},{2,1},{3,2},{4,7},{5,4},{6,5},{7,6},{8,11},{9,8},{10,9... | collective-permute-start | bytes 36872 | tf_op jit(solution)/shard_map/ppermute | solution.py:529
  15.1 30.3 %copy-start.2 = (f32[2,4,128]{2,1,0:T(4,128)S(1)}, f32[2,4,128]{2,1,0:T(4,128)}, u32[]{:S(2)}) copy-start(f32[2,4,128]{2,1,0:T(4,128)} %scale.1) | copy-start | bytes 12292
  15.1 30.3 %copy-start.4 = (bf16[6000,256]{1,0:T(8,128)(2,1)S(1)}, bf16[6000,256]{1,0:T(8,128)(2,1)}, u32[]{:S(2)}) copy-start(bf16[6000,256]{1,0:T(8,128)(2,1)} %constant.10.clone.weights) | copy-start | bytes 9216004
  15.1 30.3 %copy-start.5 = (f32[24,640]{1,0:T(8,128)S(1)}, f32[24,640]{1,0:T(8,128)}, u32[]{:S(2)}) copy-start(f32[24,640]{1,0:T(8,128)} %constant.11.clone.modes) | copy-start | bytes 184324
  23.5 6.1 %collective-permute-start.6 = (f32[32,640]{1,0:T(8,128)S(1)}, f32[32,640]{1,0:T(8,128)S(1)}, u32[]{:S(2)}, u32[]{:S(2)}) collective-permute-start(f32[32,640]{1,0:T(8,128)S(1)} %get-tuple-element.29), channel_id=1, source_target_pairs={{0,16},{16,32},{32,48},{48,64},{64,80},{80,96},{96,112},{112,0},{1... | collective-permute-start | bytes 245768 | tf_op jit(solution)/shard_map/ppermute | solution.py:529
  29.7 10.7 %collective-permute-start.8 = (f32[24,640]{1,0:T(8,128)S(1)}, f32[24,640]{1,0:T(8,128)S(1)}, u32[]{:S(2)}, u32[]{:S(2)}) collective-permute-start(f32[24,640]{1,0:T(8,128)S(1)} %pad_add_fusion), channel_id=1, source_target_pairs={{0,4},{4,8},{8,12},{12,0},{1,5},{5,9},{9,13},{13,1},{2,6},{6,10},{... | collective-permute-start | bytes 184328 | tf_op jit(solution)/shard_map/ppermute | solution.py:529
  29.8 10.7 %collective-permute-start.11 = (f32[24,128]{1,0:T(8,128)S(1)}, f32[24,128]{1,0:T(8,128)S(1)}, u32[]{:S(2)}, u32[]{:S(2)}) collective-permute-start(f32[24,128]{1,0:T(8,128)S(1)} %get-tuple-element.34), channel_id=1, source_target_pairs={{0,3},{1,0},{2,1},{3,2},{4,7},{5,4},{6,5},{7,6},{8,11},{9,8},{10,9... | collective-permute-start | bytes 36872 | tf_op jit(solution)/shard_map/ppermute | solution.py:529
  33.3 7.1 %collective-permute-start.9 = (f32[16,640]{1,0:T(8,128)S(1)}, f32[16,640]{1,0:T(8,128)S(1)}, u32[]{:S(2)}, u32[]{:S(2)}) collective-permute-start(f32[16,640]{1,0:T(8,128)S(1)} %get-tuple-element.32), channel_id=1, source_target_pairs={{0,12},{4,0},{8,4},{12,8},{1,13},{5,1},{9,5},{13,9},{2,14},{6,2},{... | collective-permute-start | bytes 122888 | tf_op jit(solution)/shard_map/ppermute | solution.py:529
  36.2 6.0 %collective-permute-start.7 = (f32[24,640]{1,0:T(8,128)S(1)}, f32[24,640]{1,0:T(8,128)S(1)}, u32[]{:S(2)}, u32[]{:S(2)}) collective-permute-start(f32[24,640]{1,0:T(8,128)S(1)} %get-tuple-element.30), channel_id=1, source_target_pairs={{0,112},{16,0},{32,16},{48,32},{64,48},{80,64},{96,80},{112,96},{1... | collective-permute-start | bytes 184328 | tf_op jit(solution)/shard_map/ppermute | solution.py:529
  40.4 5.0 %collective-permute-start.10 = (f32[24,128]{1,0:T(8,128)S(1)}, f32[24,128]{1,0:T(8,128)S(1)}, u32[]{:S(2)}, u32[]{:S(2)}) collective-permute-start(f32[24,128]{1,0:T(8,128)S(1)} %pad_add_fusion.1), channel_id=1, source_target_pairs={{0,1},{1,2},{2,3},{3,0},{4,5},{5,6},{6,7},{7,4},{8,9},{9,10},{10,1... | collective-permute-start | bytes 36872 | tf_op jit(solution)/shard_map/ppermute | solution.py:529
where the time goes:
time: 48.5 us; the launch traced here: 48.3 us
  starting transfers between devices  22.8 us (47%)
  Pallas kernels  11.7 us (24%)
  waiting for transfers between devices  10.8 us (22%)
  local copies, waits for them, and re-layouts  2.2 us (5%)
  between operations  0.7 us (1%)
    ppermute x12, starting transfers between devices, shift(): return lax.ppermute(x, axis, [(i, (i + by) % size) for i in range(size)])  22.8 us
    pallas_call x3, Pallas kernels, run(): pl.pallas_call(kernel, out_shape=outs, in_specs=[vmem] * len(operands), o...  11.7 us
    ppermute x12, waiting for transfers between devices, shift(): return lax.ppermute(x, axis, [(i, (i + by) % size) for i in range(size)])  10.8 us
    unnamed x12, local copies, waits for them, and re-layouts  2.2 us
  transfers between devices with their start and end apart: 12, of which 5 were waited for; matrix products, arithmetic and copies ran while one was open for 0% of the time, Pallas kernels for 0%

commit v1 on v0

--- a/solution.py
+++ b/solution.py
@@ -182,10 +182,11 @@
     return jnp.where(lax.axis_index(name) == edge, 0.0, 1.0)
 
 
-def pack_kernel(v, mask, x_lo, x_hi, y_lo, y_hi, z_lo, z_hi, solid):
-    solid[...] = mask[...].astype(F32).reshape(8, EZ)
-    x_lo[...] = v[:, 0] * flag("gx", True)
-    x_hi[...] = v[:, BX - 1] * flag("gx", False)
+def pack_kernel(v, x_lo, x_hi, y_lo, y_hi, z_lo, z_hi):
+    x_lo[:, 0:BY, :] = v[:, 0] * flag("gx", True)
+    x_hi[:, 0:BY, :] = v[:, BX - 1] * flag("gx", False)
+    x_lo[:, BY:PY, :] = jnp.zeros((3, PY - BY, BZ), F32)
+    x_hi[:, BY:PY, :] = jnp.zeros((3, PY - BY, BZ), F32)
     y_low, y_high = flag("gy", True), flag("gy", False)
     lane = lax.broadcasted_iota(jnp.int32, (BY, 128), 1)
     low = jnp.zeros((BY, 128), F32)
@@ -217,29 +218,17 @@
     return outs
 
 
-def step_kernel(
-    packed, v, hx_lo, hx_hi, hy_lo, hy_hi, hz_lo, hz_hi, solid, weights,
-    rhs, xp, xm, yp, ym, zp, zm, own,
-    V, FH, FL, conv, prov, PH, PL,
-):
+def volume_kernel(packed, v, after, weights, conv, V, FH, FL):
+    del after
     for c in range(3):
-        V[c, 0, 0:BY, 128:768] = hx_lo[c]
-        V[c, BX + 1, 0:BY, 128:768] = hx_hi[c]
-        V[c, 0, BY:PY, 128:768] = jnp.zeros((PY - BY, BZ), F32)
-        V[c, BX + 1, BY:PY, 128:768] = jnp.zeros((PY - BY, BZ), F32)
         for x in range(BX):
-            V[c, x + 1, 0:BY, 128:768] = v[c, x]
-            V[c, x + 1, 20:22, 128:768] = jnp.broadcast_to(hy_hi[c, x : x + 1, :], (2, BZ))
-            V[c, x + 1, 22:24, 128:768] = jnp.broadcast_to(hy_lo[c, x : x + 1, :], (2, BZ))
-            k = 16 * c + x
-            V[c, x + 1, :, 0:128] = jnp.broadcast_to(hz_lo[:, k : k + 1], (PY, 128))
-            V[c, x + 1, :, 768:896] = jnp.broadcast_to(hz_hi[:, k : k + 1], (PY, 128))
+            V[c, x, 0:BY, :] = v[c, x]
+            V[c, x, BY:PY, :] = jnp.zeros((PY - BY, BZ), F32)
 
     def products(t, carry):
-        src = pl.ds(pl.multiple_of(128 + 128 * t, 128), 128)
         dst = pl.ds(pl.multiple_of(128 * t, 128), 128)
         for q in range(BX // 2):
-            a = [V[c, 1 + 2 * q : 3 + 2 * q, :, src].reshape(2 * PY, 128) for c in range(3)]
+            a = [V[c, 2 * q : 2 * q + 2, :, dst].reshape(2 * PY, 128) for c in range(3)]
             pairs = (a[0] * a[1], a[1] * a[1], a[1] * a[2], a[0] * a[2], a[2] * a[2])
             for f, value in enumerate(pairs):
                 hi, lo = split(value)
@@ -259,19 +248,34 @@
             conv[c, :, :, n0:n1] = (y + z).reshape(BX, PY, n1 - n0)
 
     def along_x(t, carry):
-        src = pl.ds(pl.multiple_of(128 + 128 * t, 128), 128)
         dst = pl.ds(pl.multiple_of(128 * t, 128), 128)
         for e in range(EX):
-            v0 = [V[0, 1 + 5 * e + i, :, src] for i in range(5)]
+            v0 = [V[0, 5 * e + i, :, dst] for i in range(5)]
             for c in range(3):
-                flux = [v0[i] * V[c, 1 + 5 * e + i, :, src] for i in range(5)]
+                flux = [v0[i] * V[c, 5 * e + i, :, dst] for i in range(5)]
                 for i, total in enumerate(plane_sums(flux, -STEP)):
                     conv[c, 5 * e + i, :, dst] = conv[c, 5 * e + i, :, dst] + total
         return carry
 
     lax.fori_loop(0, TILES, along_x, 0)
 
-    solid = spread_out(packed, weights, [solid[...].astype(BF16)])
+
+def lift_kernel(
+    packed, v, conv, hx_lo, hx_hi, hy_lo, hy_hi, hz_lo, hz_hi, mask, weights,
+    prov, PH, PL, xp, xm, yp, ym, zp, zm, own, V,
+):
+    for c in range(3):
+        V[c, 0, :, 128:768] = hx_lo[c]
+        V[c, BX + 1, :, 128:768] = hx_hi[c]
+        for x in range(BX):
+            V[c, x + 1, 0:BY, 128:768] = v[c, x]
+            V[c, x + 1, 20:22, 128:768] = jnp.broadcast_to(hy_hi[c, x : x + 1, :], (2, BZ))
+            V[c, x + 1, 22:24, 128:768] = jnp.broadcast_to(hy_lo[c, x : x + 1, :], (2, BZ))
+            k = 16 * c + x
+            V[c, x + 1, :, 0:128] = jnp.broadcast_to(hz_lo[:, k : k + 1], (PY, 128))
+            V[c, x + 1, :, 768:896] = jnp.broadcast_to(hz_hi[:, k : k + 1], (PY, 128))
+
+    solid = spread_out(packed, weights, [mask[...].astype(F32).reshape(8, EZ).astype(BF16)])
     conv_scale = -0.5 * LIFT * STEP
     lane = lax.broadcasted_iota(jnp.int32, (PY, 128), 1)
     row = lax.broadcasted_iota(jnp.int32, (PY, 128), 0)
@@ -308,9 +312,8 @@
             q = p + y_sign * w[1]
             total = [total[c] + (p * a[c] - q * w[c]) for c in range(3)]
             if x % 5 in (0, 4):
-                other = x if x % 5 == 0 else x + 2
                 sign = 1.0 if x % 5 == 0 else -1.0
-                w = [V[c, other, :, here] for c in range(3)]
+                w = [V[c, x if x % 5 == 0 else x + 2, :, here] for c in range(3)]
                 p = conv_scale * jnp.maximum(jnp.abs(a[0]), jnp.abs(w[0]))
                 q = p + (sign * conv_scale) * w[0]
                 total = [total[c] + (p * a[c] - q * w[c]) for c in range(3)]
@@ -323,25 +326,6 @@
             hi, lo = split(prov[c, 2 * q : 2 * q + 2].reshape(2 * PY, BZ))
             PH[c, 2 * PY * q : 2 * PY * (q + 1), :] = hi
             PL[c, 2 * PY * q : 2 * PY * (q + 1), :] = lo
-    ry = packed.get(weights, "ry")
-    for i, (n0, n1, k0, k1) in enumerate(WINDOWS):
-        b = packed.get(weights, "rz" + str(i))
-        y = left_dot(ry, PH[1, :, n0:n1], PL[1, :, n0:n1])
-        z = right_dot(PH[2, :, k0:k1], PL[2, :, k0:k1], b)
-        rhs[:, :, n0:n1] = (y + z).reshape(BX, PY, n1 - n0)
-
-    def right_x(t, carry):
-        dst = pl.ds(pl.multiple_of(128 * t, 128), 128)
-        planes = [prov[0, x, :, dst] for x in range(BX)]
-        outs = plane_sums(planes[:5], -1.0) + plane_sums(planes[5:], -1.0)
-        outs[4] = outs[4] - 0.5 * LIFT * planes[5]
-        outs[5] = outs[5] + 0.5 * LIFT * planes[4]
-        for x in range(BX):
-            rhs[x, :, dst] = rhs[x, :, dst] + outs[x]
-        return carry
-
-    lax.fori_loop(0, TILES, right_x, 0)
-
     first = [1.0 - flag(name, True) for name in ("gx", "gy", "gz")]
     x_low, y_low, z_low = (flag(name, True) for name in ("gx", "gy", "gz"))
     x_high, y_high, z_high = (flag(name, False) for name in ("gx", "gy", "gz"))
@@ -388,6 +372,27 @@
     zm[...] = low * z_low
     zp[...] = high * z_high
     zp[0:4, :] = zp[0:4, :] + (edge[0:4] + edge_next[5:9])
+
+
+def right_kernel(packed, prov, PH, PL, weights, rhs):
+    ry = packed.get(weights, "ry")
+    for i, (n0, n1, k0, k1) in enumerate(WINDOWS):
+        b = packed.get(weights, "rz" + str(i))
+        y = left_dot(ry, PH[1, :, n0:n1], PL[1, :, n0:n1])
+        z = right_dot(PH[2, :, k0:k1], PL[2, :, k0:k1], b)
+        rhs[:, :, n0:n1] = (y + z).reshape(BX, PY, n1 - n0)
+
+    def right_x(t, carry):
+        dst = pl.ds(pl.multiple_of(128 * t, 128), 128)
+        planes = [prov[0, x, :, dst] for x in range(BX)]
+        outs = plane_sums(planes[:5], -1.0) + plane_sums(planes[5:], -1.0)
+        outs[4] = outs[4] - 0.5 * LIFT * planes[5]
+        outs[5] = outs[5] + 0.5 * LIFT * planes[4]
+        for x in range(BX):
+            rhs[x, :, dst] = rhs[x, :, dst] + outs[x]
+        return carry
+
+    lax.fori_loop(0, TILES, right_x, 0)
 
 
 def spread_out(packed, weights, parts):
@@ -474,12 +479,12 @@
 
 
 def constants():
-    step, smooth = Packed(), Packed()
+    volume, lift, right, smooth = Packed(), Packed(), Packed(), Packed()
     eye_x = np.eye(BX)
-    step.add("my", pad_both(np.kron(eye_x, -STEP * line_operator(EY, False))))
-    step.add("ry", pad_both(np.kron(eye_x, -line_operator(EY, True))))
-    step.add_windows("bz", -STEP * line_operator(EZ, False).T)
-    step.add_windows("rz", -line_operator(EZ, True).T)
+    volume.add("my", pad_both(np.kron(eye_x, -STEP * line_operator(EY, False))))
+    right.add("ry", pad_both(np.kron(eye_x, -line_operator(EY, True))))
+    volume.add_windows("bz", -STEP * line_operator(EZ, False).T)
+    right.add_windows("rz", -line_operator(EZ, True).T)
     basis = eigen_basis_table()
     sx = np.kron(np.eye(EX), basis)
     sy = np.kron(np.eye(EY), basis)
@@ -494,7 +499,7 @@
     for e in range(EX):
         for y in range(BY):
             rows_of[PY * e + y, EY * e + y // 5] = 1.0
-    for packed in (step, smooth):
+    for packed in (lift, smooth):
         packed.add("rows_of", rows_of, 1)
         for i, (n0, n1, _, _) in enumerate(WINDOWS):
             packed.add("spread" + str(i), spread[:, n0:n1], 1)
@@ -508,7 +513,7 @@
         wide = np.zeros((BZ, 256))
         wide[:, 0:EZ] = m[:EZ].T
         wide[:, 128 + ZEDGE] = m[EZ]
-        step.add(name, wide)
+        lift.add(name, wide)
     half = 0.5 * LIFT * hat_weight_table()[0, 0]
     ex, ey = np.zeros_like(gx), np.zeros_like(gy)
     ex[0, 0] = -half
@@ -520,8 +525,8 @@
         ("d0", np.kron(ex, hy)),
         ("d1", np.kron(hx, ey)),
     ):
-        step.add(name, pad_to(pad_rows(-m), 16, ROWS))
-    return step, smooth, modes.astype(np.float32)
+        lift.add(name, pad_to(pad_rows(-m), 16, ROWS))
+    return volume, lift, right, smooth, modes.astype(np.float32)
 
 
 def shift(x, axis, by):
@@ -533,7 +538,7 @@
     return jax.ShapeDtypeStruct(shape, F32)
 
 
-def run(kernel, outs, operands, scratch=(), name=None, flops=0, moved=0):
+def run(kernel, outs, operands, scratch=(), name=None, flops=0):
     vmem = pl.BlockSpec(memory_space=pltpu.VMEM)
     return pl.pallas_call(
         kernel,
@@ -541,21 +546,20 @@
         in_specs=[vmem] * len(operands),
         out_specs=[vmem] * len(outs),
         scratch_shapes=list(scratch),
-        compiler_params=pltpu.CompilerParams(vmem_limit_bytes=40 * 2**20),
-        cost_estimate=pl.CostEstimate(flops=flops, bytes_accessed=moved, transcendentals=0),
+        compiler_params=pltpu.CompilerParams(vmem_limit_bytes=32 * 2**20),
+        cost_estimate=pl.CostEstimate(flops=flops, bytes_accessed=4 << 20, transcendentals=0),
         name=name,
     )(*operands)
 
 
 def shards(velocity, obstacle_element_mask, element_metric_scale):
-    step, smooth, modes = constants()
+    volume, lift, right, smooth, modes = constants()
     faces = run(
         pack_kernel,
-        [like(3, BY, BZ)] * 2 + [like(3, BX, BZ)] * 2 + [like(PY, 128)] * 2 + [like(8, EZ)],
-        [velocity, obstacle_element_mask],
+        [like(3, PY, BZ)] * 2 + [like(3, BX, BZ)] * 2 + [like(PY, 128)] * 2,
+        [velocity],
         name="pack",
         flops=10**10,
-        moved=4 << 20,
     )
     halo = [
         shift(faces[1], "gx", 1),
@@ -566,31 +570,32 @@
     ]
     halo[0], last = lax.optimization_barrier((halo[0], faces[4]))
     halo.append(shift(last, "gz", -1))
-    rhs, xp, xm, yp, ym, zp, zm, own = run(
-        functools.partial(step_kernel, step),
-        [
-            like(BX, PY, BZ),
-            like(32, BZ),
-            like(PY, BZ),
-            like(24, BZ),
-            like(16, BZ),
-            like(PY, 128),
-            like(PY, 128),
-            like(16, 128),
-        ],
-        [velocity, *halo, faces[6], step.array()],
-        scratch=[
-            pltpu.VMEM((3, BX + 2, PY, 896), F32),
-            pltpu.VMEM((5, ROWS, BZ), BF16),
-            pltpu.VMEM((5, ROWS, BZ), BF16),
-            pltpu.VMEM((3, BX, PY, BZ), F32),
-            pltpu.VMEM((3, BX, PY, BZ), F32),
-            pltpu.VMEM((3, ROWS, BZ), BF16),
-            pltpu.VMEM((3, ROWS, BZ), BF16),
-        ],
-        name="step",
+    field = like(3, BX, PY, BZ)
+    half = jax.ShapeDtypeStruct((3, ROWS, BZ), BF16)
+    (conv,) = run(
+        functools.partial(volume_kernel, volume),
+        [field],
+        [velocity, faces[4], volume.array()],
+        scratch=[pltpu.VMEM((3, BX, PY, BZ), F32)] + [pltpu.VMEM((5, ROWS, BZ), BF16)] * 2,
+        name="volume",
         flops=4 * 10**9,
-        moved=8 << 20,
+    )
+    prov, ph, plo, xp, xm, yp, ym, zp, zm, own = run(
+        functools.partial(lift_kernel, lift),
+        [field, half, half]
+        + [like(32, BZ), like(PY, BZ), like(24, BZ), like(16, BZ), like(PY, 128), like(PY, 128)]
+        + [like(16, 128)],
+        [velocity, conv, *halo, obstacle_element_mask, lift.array()],
+        scratch=[pltpu.VMEM((3, BX + 2, PY, 896), F32)],
+        name="lift",
+        flops=4 * 10**9,
+    )
+    (rhs,) = run(
+        functools.partial(right_kernel, right),
+        [like(BX, PY, BZ)],
+        [prov, ph, plo, right.array()],
+        name="right",
+        flops=2 * 10**9,
     )
     gx_lo = shift(xp, "gx", 1)
     gx_hi = shift(xm, "gx", -1)
@@ -609,7 +614,6 @@
         scratch=[pltpu.VMEM((ROWS, BZ), BF16)] * 4,
         name="smooth",
         flops=3 * 10**9,
-        moved=6 << 20,
     )
     return (smoothed, coarse)
 

time: 48.5 us -> 43.7 us (0.901)
  the two profiles are of different devices: /device:TPU:14 before, /device:TPU:0 now
where the time goes in v1:
time: 43.7 us; the launch traced here: 43.5 us
  starting transfers between devices  17.9 us (41%)
  Pallas kernels  11.8 us (27%)
  waiting for transfers between devices  11.5 us (26%)
  local copies, waits for them, and re-layouts  1.54 us (4%)
  between operations  0.81 us (2%)
    ppermute x12, starting transfers between devices, shift(): return lax.ppermute(x, axis, [(i, (i + by) % size) for i in range(size)])  17.9 us
    pallas_call x5, Pallas kernels, run(): pl.pallas_call(kernel, out_shape=outs, in_specs=[vmem] * len(operands), o...  11.8 us
    ppermute x12, waiting for transfers between devices, shift(): return lax.ppermute(x, axis, [(i, (i + by) % size) for i in range(size)])  11.5 us
    unnamed x16, local copies, waits for them, and re-layouts  1.53 us
  transfers between devices with their start and end apart: 12, of which 4 were waited for; matrix products, arithmetic and copies ran while one was open for 0% of the time, Pallas kernels for 11%

profile of v1, /device:TPU:0, one launch (start us, length us, event | category | flops | bytes accessed | tf_op | source)
XLA Modules:
  0.0 43.5 jit_solution(11152409949620936879)
XLA Ops:
  0.6 0.0 copy-start
  0.6 1.5 %copy-done = f32[3,10,20,640]{3,2,1,0:T(8,128)S(1)} copy-done((f32[3,10,20,640]{3,2,1,0:T(8,128)S(1)}, f32[3,10,20,640]{3,2,1,0:T(8,128)}, u32[]{:S(2)}) %copy-start) | copy-done | bytes 1536024
  2.1 0.0 copy-start.6
  2.1 0.4 pack.1
  2.5 1.7 %collective-permute-start = (f32[3,24,640]{2,1,0:T(8,128)S(1)}, f32[3,24,640]{2,1,0:T(8,128)S(1)}, u32[]{:S(2)}, u32[]{:S(2)}) collective-permute-start(f32[3,24,640]{2,1,0:T(8,128)S(1)} %get-tuple-element.21), channel_id=1, source_target_pairs={{0,16},{16,32},{32,48},{48,64},{64,80},{80,96},{96,112},{112,0},{1... | collective-permute-start | bytes 552968 | tf_op jit(solution)/shard_map/ppermute | solution.py:534
  4.2 1.9 %collective-permute-start.4 = (f32[24,128]{1,0:T(8,128)S(1)}, f32[24,128]{1,0:T(8,128)S(1)}, u32[]{:S(2)}, u32[]{:S(2)}) collective-permute-start(f32[24,128]{1,0:T(8,128)S(1)} %get-tuple-element.26), channel_id=1, source_target_pairs={{0,1},{1,2},{2,3},{3,0},{4,5},{5,6},{6,7},{7,4},{8,9},{9,10},{10,1... | collective-permute-start | bytes 36872 | tf_op jit(solution)/shard_map/ppermute | solution.py:534
  6.2 0.0 collective-permute-start.2
  6.2 3.2 %collective-permute-start.3 = (f32[3,10,640]{2,1,0:T(8,128)S(1)}, f32[3,10,640]{2,1,0:T(8,128)S(1)}, u32[]{:S(2)}, u32[]{:S(2)}) collective-permute-start(f32[3,10,640]{2,1,0:T(8,128)S(1)} %get-tuple-element.25), channel_id=1, source_target_pairs={{0,12},{4,0},{8,4},{12,8},{1,13},{5,1},{9,5},{13,9},{2,14},{6,2},{... | collective-permute-start | bytes 230408 | tf_op jit(solution)/shard_map/ppermute | solution.py:534
  9.4 2.6 %collective-permute-start.1 = (f32[3,24,640]{2,1,0:T(8,128)S(1)}, f32[3,24,640]{2,1,0:T(8,128)S(1)}, u32[]{:S(2)}, u32[]{:S(2)}) collective-permute-start(f32[3,24,640]{2,1,0:T(8,128)S(1)} %get-tuple-element.23), channel_id=1, source_target_pairs={{0,112},{16,0},{32,16},{48,32},{64,48},{80,64},{96,80},{112,96},{1... | collective-permute-start | bytes 552968 | tf_op jit(solution)/shard_map/ppermute | solution.py:534
  12.0 0.0 collective-permute-done.hx_lo
  12.0 0.0 copy-start.1
  12.0 0.0 copy-start.4
  12.0 4.4 %collective-permute-start.5 = (f32[24,128]{1,0:T(8,128)S(1)}, f32[24,128]{1,0:T(8,128)S(1)}, u32[]{:S(2)}, u32[]{:S(2)}) collective-permute-start(f32[24,128]{1,0:T(8,128)S(1)} %get-tuple-element.27.after), channel_id=1, source_target_pairs={{0,3},{1,0},{2,1},{3,2},{4,7},{5,4},{6,5},{7,6},{8,11},{9,8},{10,9... | collective-permute-start | bytes 36872 | tf_op jit(solution)/shard_map/ppermute | solution.py:534
  16.3 0.0 copy-done.6
  16.3 3.8 %volume.1.conv = f32[3,10,24,640]{3,2,1,0:T(8,128)S(1)} custom-call(f32[3,10,20,640]{3,2,1,0:T(8,128)S(1)} %copy-done, f32[24,128]{1,0:T(8,128)S(1)} %get-tuple-element.27.after, bf16[2784,256]{1,0:T(8,128)(2,1)S(1)} %copy-done.6), custom_call_target="tpu_custom_call" | custom-call | flops 4000000000 | bytes 4194304 | tf_op jit(solution)/shard_map/volume/pallas_call | solution.py:543
  20.2 0.0 copy-start.5
  20.2 0.0 collective-permute-done.4.hz_lo
  20.2 0.0 collective-permute-done.2.hy_lo
  20.2 0.0 collective-permute-done.3.hy_hi
  20.2 0.0 collective-permute-done.1.hx_hi
  20.2 0.0 collective-permute-done.5.hz_hi
  20.3 0.0 copy-done.1
  20.3 0.0 copy-done.4
  20.3 3.5 %lift.1 = (f32[3,10,24,640]{3,2,1,0:T(8,128)S(1)}, bf16[3,240,640]{2,1,0:T(8,128)(2,1)S(1)}, bf16[3,240,640]{2,1,0:T(8,128)(2,1)S(1)}, f32[32,640]{1,0:T(8,128)S...) custom-call(f32[3,10,20,640]{3,2,1,0:T(8,128)S(1)} %copy-done, ...), custom_call_target="tpu_custom_call" | custom-call | flops 4000000000 | bytes 4194304 | tf_op jit(solution)/shard_map/lift/pallas_call | solution.py:543
  23.8 0.1 collective-permute-start.6
  23.9 6.5 %collective-permute-done.6.hx_lo = f32[32,640]{1,0:T(8,128)S(1)} collective-permute-done((f32[32,640]{1,0:T(8,128)S(1)}, f32[32,640]{1,0:T(8,128)S(1)}, u32[]{:S(2)}, u32[]{:S(2)}) %collective-permute-start.6) | collective-permute-done | bytes 81952 | tf_op jit(solution)/shard_map/ppermute | solution.py:534
  30.4 0.1 collective-permute-start.8
  30.5 1.0 %collective-permute-start.11 = (f32[24,128]{1,0:T(8,128)S(1)}, f32[24,128]{1,0:T(8,128)S(1)}, u32[]{:S(2)}, u32[]{:S(2)}) collective-permute-start(f32[24,128]{1,0:T(8,128)S(1)} %get-tuple-element.36), channel_id=1, source_target_pairs={{0,3},{1,0},{2,1},{3,2},{4,7},{5,4},{6,5},{7,6},{8,11},{9,8},{10,9... | collective-permute-start | bytes 36872 | tf_op jit(solution)/shard_map/ppermute | solution.py:534
  31.5 2.9 %collective-permute-start.9 = (f32[16,640]{1,0:T(8,128)S(1)}, f32[16,640]{1,0:T(8,128)S(1)}, u32[]{:S(2)}, u32[]{:S(2)}) collective-permute-start(f32[16,640]{1,0:T(8,128)S(1)} %get-tuple-element.34), channel_id=1, source_target_pairs={{0,12},{4,0},{8,4},{12,8},{1,13},{5,1},{9,5},{13,9},{2,14},{6,2},{... | collective-permute-start | bytes 122888 | tf_op jit(solution)/shard_map/ppermute | solution.py:534
  34.4 0.0 collective-permute-start.7
  34.4 1.2 %collective-permute-done.8.hy_lo = f32[24,640]{1,0:T(8,128)S(1)} collective-permute-done((f32[24,640]{1,0:T(8,128)S(1)}, f32[24,640]{1,0:T(8,128)S(1)}, u32[]{:S(2)}, u32[]{:S(2)}) %collective-permute-start.8) | collective-permute-done | bytes 61472 | tf_op jit(solution)/shard_map/ppermute | solution.py:534
  35.6 0.0 collective-permute-start.10
  35.6 0.0 copy-done.5
  35.7 0.0 copy-start.2
  35.7 0.0 copy-start.3
  35.7 0.0 copy-start.7
  35.7 1.1 %right.1.rhs = f32[10,24,640]{2,1,0:T(8,128)S(1)} custom-call(f32[3,10,24,640]{3,2,1,0:T(8,128)S(1)} %get-tuple-element.28.prov, bf16[3,240,640]{2,1,0:T(8,128)(2,1)S(1)} %get-tuple-element.29.PH, bf16[3,240,640]{2,1,0:T(8,128)(2,1)S(1)} %get-tuple-element.30.PL, bf16[2784,256]{1,0:T(8,128)(2,1)S(1)} %copy-done.5), custom_call_target="tpu_custom_call" | custom-call | flops 2000000000 | bytes 4194304 | tf_op jit(solution)/shard_map/right/pallas_call | solution.py:543
  36.8 0.0 collective-permute-done.11.hz_hi
  36.8 0.0 collective-permute-done.9.hy_hi
  36.9 1.8 %collective-permute-done.7.hx_hi = f32[24,640]{1,0:T(8,128)S(1)} collective-permute-done((f32[24,640]{1,0:T(8,128)S(1)}, f32[24,640]{1,0:T(8,128)S(1)}, u32[]{:S(2)}, u32[]{:S(2)}) %collective-permute-start.7) | collective-permute-done | bytes 61472 | tf_op jit(solution)/shard_map/ppermute | solution.py:534
  38.6 1.9 %collective-permute-done.10.hz_lo = f32[24,128]{1,0:T(8,128)S(1)} collective-permute-done((f32[24,128]{1,0:T(8,128)S(1)}, f32[24,128]{1,0:T(8,128)S(1)}, u32[]{:S(2)}, u32[]{:S(2)}) %collective-permute-start.10) | collective-permute-done | bytes 12320 | tf_op jit(solution)/shard_map/ppermute | solution.py:534
  40.5 0.0 copy-done.2
  40.6 0.0 copy-done.3
  40.6 0.0 copy-done.7
  40.6 3.0 %smooth.1 = (f32[10,20,640]{2,1,0:T(8,128)}, f32[2,4,128]{2,1,0:T(4,128)}) custom-call(f32[10,24,640]{2,1,0:T(8,128)S(1)} %right.1.rhs, f32[32,640]{1,0:T(8,128)S(1)} %collective-permute-done.6.hx_lo, f32[24,640]{1,0:T(8,128)S(1)} %collective-permute-done.7.hx_hi, f32[24,640]{1,0:T(8,128)S(1)} %collective-permute-done.8.hy_lo, ...), custom_call_target="tpu_custom_call" | custom-call | flops 3000000000 | bytes 4194304 | tf_op jit(solution)/shard_map/smooth/pallas_call | solution.py:543
  (5 shorter events, 0.0 us)
Async XLA Ops:
  0.6 1.5 %copy-start = (f32[3,10,20,640]{3,2,1,0:T(8,128)S(1)}, f32[3,10,20,640]{3,2,1,0:T(8,128)}, u32[]{:S(2)}) copy-start(f32[3,10,20,640]{3,2,1,0:T(8,128)} %v.5) | copy-start | bytes 4608004
  2.1 14.2 %copy-start.6 = (bf16[2784,256]{1,0:T(8,128)(2,1)S(1)}, bf16[2784,256]{1,0:T(8,128)(2,1)}, u32[]{:S(2)}) copy-start(bf16[2784,256]{1,0:T(8,128)(2,1)} %constant.13.clone.weights) | copy-start | bytes 4276228
  2.5 9.5 %collective-permute-start = (f32[3,24,640]{2,1,0:T(8,128)S(1)}, f32[3,24,640]{2,1,0:T(8,128)S(1)}, u32[]{:S(2)}, u32[]{:S(2)}) collective-permute-start(f32[3,24,640]{2,1,0:T(8,128)S(1)} %get-tuple-element.21), channel_id=1, source_target_pairs={{0,16},{16,32},{32,48},{48,64},{64,80},{80,96},{96,112},{112,0},{1... | collective-permute-start | bytes 552968 | tf_op jit(solution)/shard_map/ppermute | solution.py:534
  4.2 16.0 %collective-permute-start.4 = (f32[24,128]{1,0:T(8,128)S(1)}, f32[24,128]{1,0:T(8,128)S(1)}, u32[]{:S(2)}, u32[]{:S(2)}) collective-permute-start(f32[24,128]{1,0:T(8,128)S(1)} %get-tuple-element.26), channel_id=1, source_target_pairs={{0,1},{1,2},{2,3},{3,0},{4,5},{5,6},{6,7},{7,4},{8,9},{9,10},{10,1... | collective-permute-start | bytes 36872 | tf_op jit(solution)/shard_map/ppermute | solution.py:534
  6.2 14.0 %collective-permute-start.2 = (f32[3,10,640]{2,1,0:T(8,128)S(1)}, f32[3,10,640]{2,1,0:T(8,128)S(1)}, u32[]{:S(2)}, u32[]{:S(2)}) collective-permute-start(f32[3,10,640]{2,1,0:T(8,128)S(1)} %get-tuple-element.24), channel_id=1, source_target_pairs={{0,4},{4,8},{8,12},{12,0},{1,5},{5,9},{9,13},{13,1},{2,6},{6,10},{... | collective-permute-start | bytes 230408 | tf_op jit(solution)/shard_map/ppermute | solution.py:534
  6.2 14.1 %collective-permute-start.3 = (f32[3,10,640]{2,1,0:T(8,128)S(1)}, f32[3,10,640]{2,1,0:T(8,128)S(1)}, u32[]{:S(2)}, u32[]{:S(2)}) collective-permute-start(f32[3,10,640]{2,1,0:T(8,128)S(1)} %get-tuple-element.25), channel_id=1, source_target_pairs={{0,12},{4,0},{8,4},{12,8},{1,13},{5,1},{9,5},{13,9},{2,14},{6,2},{... | collective-permute-start | bytes 230408 | tf_op jit(solution)/shard_map/ppermute | solution.py:534
  9.4 10.8 %collective-permute-start.1 = (f32[3,24,640]{2,1,0:T(8,128)S(1)}, f32[3,24,640]{2,1,0:T(8,128)S(1)}, u32[]{:S(2)}, u32[]{:S(2)}) collective-permute-start(f32[3,24,640]{2,1,0:T(8,128)S(1)} %get-tuple-element.23), channel_id=1, source_target_pairs={{0,112},{16,0},{32,16},{48,32},{64,48},{80,64},{96,80},{112,96},{1... | collective-permute-start | bytes 552968 | tf_op jit(solution)/shard_map/ppermute | solution.py:534
  12.0 8.3 %copy-start.1 = (s32[2,4,128]{2,1,0:T(4,128)S(1)}, s32[2,4,128]{2,1,0:T(4,128)}, u32[]{:S(2)}) copy-start(s32[2,4,128]{2,1,0:T(4,128)} %mask.1) | copy-start | bytes 12292
  12.0 8.3 %copy-start.4 = (bf16[3152,256]{1,0:T(8,128)(2,1)S(1)}, bf16[3152,256]{1,0:T(8,128)(2,1)}, u32[]{:S(2)}) copy-start(bf16[3152,256]{1,0:T(8,128)(2,1)} %constant.14.clone.weights) | copy-start | bytes 4841476
  12.0 8.3 %collective-permute-start.5 = (f32[24,128]{1,0:T(8,128)S(1)}, f32[24,128]{1,0:T(8,128)S(1)}, u32[]{:S(2)}, u32[]{:S(2)}) collective-permute-start(f32[24,128]{1,0:T(8,128)S(1)} %get-tuple-element.27.after), channel_id=1, source_target_pairs={{0,3},{1,0},{2,1},{3,2},{4,7},{5,4},{6,5},{7,6},{8,11},{9,8},{10,9... | collective-permute-start | bytes 36872 | tf_op jit(solution)/shard_map/ppermute | solution.py:534
  20.2 15.5 %copy-start.5 = (bf16[2784,256]{1,0:T(8,128)(2,1)S(1)}, bf16[2784,256]{1,0:T(8,128)(2,1)}, u32[]{:S(2)}) copy-start(bf16[2784,256]{1,0:T(8,128)(2,1)} %constant.15.clone.weights) | copy-start | bytes 4276228
  23.8 6.6 %collective-permute-start.6 = (f32[32,640]{1,0:T(8,128)S(1)}, f32[32,640]{1,0:T(8,128)S(1)}, u32[]{:S(2)}, u32[]{:S(2)}) collective-permute-start(f32[32,640]{1,0:T(8,128)S(1)} %get-tuple-element.31), channel_id=1, source_target_pairs={{0,16},{16,32},{32,48},{48,64},{64,80},{80,96},{96,112},{112,0},{1... | collective-permute-start | bytes 245768 | tf_op jit(solution)/shard_map/ppermute | solution.py:534
  30.4 5.2 %collective-permute-start.8 = (f32[24,640]{1,0:T(8,128)S(1)}, f32[24,640]{1,0:T(8,128)S(1)}, u32[]{:S(2)}, u32[]{:S(2)}) collective-permute-start(f32[24,640]{1,0:T(8,128)S(1)} %pad_add_fusion), channel_id=1, source_target_pairs={{0,4},{4,8},{8,12},{12,0},{1,5},{5,9},{9,13},{13,1},{2,6},{6,10},{... | collective-permute-start | bytes 184328 | tf_op jit(solution)/shard_map/ppermute | solution.py:534
  30.5 6.3 %collective-permute-start.11 = (f32[24,128]{1,0:T(8,128)S(1)}, f32[24,128]{1,0:T(8,128)S(1)}, u32[]{:S(2)}, u32[]{:S(2)}) collective-permute-start(f32[24,128]{1,0:T(8,128)S(1)} %get-tuple-element.36), channel_id=1, source_target_pairs={{0,3},{1,0},{2,1},{3,2},{4,7},{5,4},{6,5},{7,6},{8,11},{9,8},{10,9... | collective-permute-start | bytes 36872 | tf_op jit(solution)/shard_map/ppermute | solution.py:534
  31.5 5.3 %collective-permute-start.9 = (f32[16,640]{1,0:T(8,128)S(1)}, f32[16,640]{1,0:T(8,128)S(1)}, u32[]{:S(2)}, u32[]{:S(2)}) collective-permute-start(f32[16,640]{1,0:T(8,128)S(1)} %get-tuple-element.34), channel_id=1, source_target_pairs={{0,12},{4,0},{8,4},{12,8},{1,13},{5,1},{9,5},{13,9},{2,14},{6,2},{... | collective-permute-start | bytes 122888 | tf_op jit(solution)/shard_map/ppermute | solution.py:534
  34.4 4.2 %collective-permute-start.7 = (f32[24,640]{1,0:T(8,128)S(1)}, f32[24,640]{1,0:T(8,128)S(1)}, u32[]{:S(2)}, u32[]{:S(2)}) collective-permute-start(f32[24,640]{1,0:T(8,128)S(1)} %get-tuple-element.32), channel_id=1, source_target_pairs={{0,112},{16,0},{32,16},{48,32},{64,48},{80,64},{96,80},{112,96},{1... | collective-permute-start | bytes 184328 | tf_op jit(solution)/shard_map/ppermute | solution.py:534
  35.6 4.9 %collective-permute-start.10 = (f32[24,128]{1,0:T(8,128)S(1)}, f32[24,128]{1,0:T(8,128)S(1)}, u32[]{:S(2)}, u32[]{:S(2)}) collective-permute-start(f32[24,128]{1,0:T(8,128)S(1)} %pad_add_fusion.1), channel_id=1, source_target_pairs={{0,1},{1,2},{2,3},{3,0},{4,5},{5,6},{6,7},{7,4},{8,9},{9,10},{10,1... | collective-permute-start | bytes 36872 | tf_op jit(solution)/shard_map/ppermute | solution.py:534
  35.7 4.9 %copy-start.2 = (f32[2,4,128]{2,1,0:T(4,128)S(1)}, f32[2,4,128]{2,1,0:T(4,128)}, u32[]{:S(2)}) copy-start(f32[2,4,128]{2,1,0:T(4,128)} %scale.1) | copy-start | bytes 12292
  35.7 4.9 %copy-start.3 = (bf16[6000,256]{1,0:T(8,128)(2,1)S(1)}, bf16[6000,256]{1,0:T(8,128)(2,1)}, u32[]{:S(2)}) copy-start(bf16[6000,256]{1,0:T(8,128)(2,1)} %constant.16.clone.weights) | copy-start | bytes 9216004
  35.7 4.9 %copy-start.7 = (f32[24,640]{1,0:T(8,128)S(1)}, f32[24,640]{1,0:T(8,128)}, u32[]{:S(2)}) copy-start(f32[24,640]{1,0:T(8,128)} %constant.17.clone.modes) | copy-start | bytes 184324

commit v2 on v1

--- a/solution.py
+++ b/solution.py
@@ -155,6 +155,10 @@
     def array(self):
         return jnp.asarray(np.concatenate(self.parts))
 
+    def both(self, ref, name):
+        r, n, c = self.places[name][0]
+        return ref[r : r + 2 * n, 0:c]
+
     def get(self, ref, name):
         out = [ref[r : r + n, 0:c] for r, n, c in self.places[name]]
         return out[0] if len(out) == 1 else out
@@ -165,16 +169,28 @@
     return hi, (x - hi.astype(F32)).astype(BF16)
 
 
+def stacked(x):
+    return jnp.concatenate(split(x), axis=0)
+
+
 def dot(a, b):
     return jnp.dot(a, b, preferred_element_type=F32)
 
 
 def left_dot(m, hi, lo):
-    return dot(m[0], hi) + dot(m[1], hi) + dot(m[0], lo)
+    rows = m.shape[0] // 2
+    both = dot(m, hi)
+    return both[:rows] + both[rows:] + dot(m[:rows], lo)
 
 
 def right_dot(hi, lo, m):
     return dot(hi, m[0]) + dot(lo, m[0]) + dot(hi, m[1])
+
+
+def stack_dot(x, m):
+    rows = x.shape[0] // 2
+    both = dot(x, m[0])
+    return both[:rows] + both[rows:] + dot(x[:rows], m[1])
 
 
 def flag(name, low):
@@ -182,19 +198,15 @@
     return jnp.where(lax.axis_index(name) == edge, 0.0, 1.0)
 
 
-def pack_kernel(v, x_lo, x_hi, y_lo, y_hi, z_lo, z_hi):
-    x_lo[:, 0:BY, :] = v[:, 0] * flag("gx", True)
-    x_hi[:, 0:BY, :] = v[:, BX - 1] * flag("gx", False)
-    x_lo[:, BY:PY, :] = jnp.zeros((3, PY - BY, BZ), F32)
-    x_hi[:, BY:PY, :] = jnp.zeros((3, PY - BY, BZ), F32)
+def pack_kernel(v, y_lo, y_hi, z_lo, z_hi):
     y_low, y_high = flag("gy", True), flag("gy", False)
     lane = lax.broadcasted_iota(jnp.int32, (BY, 128), 1)
     low = jnp.zeros((BY, 128), F32)
     high = jnp.zeros((BY, 128), F32)
     for c in range(3):
         for x in range(BX):
-            y_lo[c, x : x + 1, :] = v[c, x, 0:1, :] * y_low
-            y_hi[c, x : x + 1, :] = v[c, x, BY - 1 : BY, :] * y_high
+            y_lo[BX * c + x : BX * c + x + 1, :] = v[c, x, 0:1, :] * y_low
+            y_hi[BX * c + x : BX * c + x + 1, :] = v[c, x, BY - 1 : BY, :] * y_high
             here = lane == 16 * c + x
             low = jnp.where(here, jnp.broadcast_to(v[c, x, :, 0:1], (BY, 128)), low)
             high = jnp.where(here, jnp.broadcast_to(v[c, x, :, BZ - 1 : BZ], (BY, 128)), high)
@@ -238,14 +250,16 @@
 
     lax.fori_loop(0, TILES, products, 0)
 
-    my = packed.get(weights, "my")
+    my = packed.both(weights, "my")
     for i, (n0, n1, k0, k1) in enumerate(WINDOWS):
-        b = packed.get(weights, "bz" + str(i))
+        high = FH[2:5, :, k0:k1].reshape(3 * ROWS, k1 - k0)
+        low = FL[2:5, :, k0:k1].reshape(3 * ROWS, k1 - k0)
+        z = right_dot(high, low, packed.get(weights, "bz" + str(i)))
         for c in range(3):
-            along_z = (3, 2, 4)[c]
+            along_z = ROWS * (1, 0, 2)[c]
             y = left_dot(my, FH[c, :, n0:n1], FL[c, :, n0:n1])
-            z = right_dot(FH[along_z, :, k0:k1], FL[along_z, :, k0:k1], b)
-            conv[c, :, :, n0:n1] = (y + z).reshape(BX, PY, n1 - n0)
+            total = y + z[along_z : along_z + ROWS]
+            conv[c, :, :, n0:n1] = total.reshape(BX, PY, n1 - n0)
 
     def along_x(t, carry):
         dst = pl.ds(pl.multiple_of(128 * t, 128), 128)
@@ -265,12 +279,15 @@
     prov, PH, PL, xp, xm, yp, ym, zp, zm, own, V,
 ):
     for c in range(3):
-        V[c, 0, :, 128:768] = hx_lo[c]
-        V[c, BX + 1, :, 128:768] = hx_hi[c]
+        V[c, 0, 0:BY, 128:768] = hx_lo[c] * flag("gx", True)
+        V[c, BX + 1, 0:BY, 128:768] = hx_hi[c] * flag("gx", False)
+        V[c, 0, BY:PY, 128:768] = jnp.zeros((PY - BY, BZ), F32)
+        V[c, BX + 1, BY:PY, 128:768] = jnp.zeros((PY - BY, BZ), F32)
         for x in range(BX):
+            r = BX * c + x
             V[c, x + 1, 0:BY, 128:768] = v[c, x]
-            V[c, x + 1, 20:22, 128:768] = jnp.broadcast_to(hy_hi[c, x : x + 1, :], (2, BZ))
-            V[c, x + 1, 22:24, 128:768] = jnp.broadcast_to(hy_lo[c, x : x + 1, :], (2, BZ))
+            V[c, x + 1, 20:22, 128:768] = jnp.broadcast_to(hy_hi[r : r + 1, :], (2, BZ))
+            V[c, x + 1, 22:24, 128:768] = jnp.broadcast_to(hy_lo[r : r + 1, :], (2, BZ))
             k = 16 * c + x
             V[c, x + 1, :, 0:128] = jnp.broadcast_to(hz_lo[:, k : k + 1], (PY, 128))
             V[c, x + 1, :, 768:896] = jnp.broadcast_to(hz_hi[:, k : k + 1], (PY, 128))
@@ -334,12 +351,9 @@
         sum(part.astype(F32) for part in packed.get(weights, n)) for n in ("c0", "c1", "c2", "d0", "d1")
     )
     for c, m in enumerate((c0 + first[0] * d0, c1 + first[1] * d1, c2)):
-        hi, lo = split(m)
-        parts.append(dot(hi, PH[c]) + dot(lo, PH[c]) + dot(hi, PL[c]))
-    hi, lo = split(parts[0] + parts[1])
-    coarse = right_dot(hi, lo, packed.get(weights, "hz"))
-    hi, lo = split(parts[2])
-    coarse = coarse + right_dot(hi, lo, packed.get(weights, "gz"))
+        parts.append(left_dot(stacked(m), PH[c], PL[c]))
+    coarse = stack_dot(stacked(parts[0] + parts[1]), packed.get(weights, "hz"))
+    coarse = coarse + stack_dot(stacked(parts[2]), packed.get(weights, "gz"))
     lane16 = lax.broadcasted_iota(jnp.int32, (16, 128), 1)
     vertices = coarse[:, 0:128] - jnp.where(
         lane16 == 0, (0.5 * LIFT * 0.1) * first[2] * parts[2][:, 0:128], 0.0
@@ -353,10 +367,12 @@
 
     xp[0:PY, :] = prov[0, BX - 1] * x_high
     xm[...] = prov[0, 0] * x_low
-    xp[24:32, :] = jnp.zeros((8, BZ), F32)
-    xp[24:29, 0:128] = vertices[10:15]
-    xp[24:29, 128:256] = edge[10:15]
-    yp[8:24, :] = jnp.zeros((16, BZ), F32)
+    xp[BY:PY, :] = jnp.zeros((PY - BY, BZ), F32)
+    xp[20:24, 0:128] = vertices[10:14]
+    xp[20:24, 128:256] = edge[10:14]
+    xp[20:21, 256:384] = vertices[14:15]
+    xp[20:21, 384:512] = edge[14:15]
+    yp[8:16, :] = jnp.zeros((8, BZ), F32)
     ym[8:16, :] = jnp.zeros((8, BZ), F32)
     lane24 = lax.broadcasted_iota(jnp.int32, (PY, 128), 1)
     low = jnp.zeros((PY, 128), F32)
@@ -366,16 +382,16 @@
         ym[x : x + 1, :] = prov[1, x, 0:1, :] * y_low
         low = jnp.where(lane24 == x, jnp.broadcast_to(prov[2, x, :, 0:1], (PY, 128)), low)
         high = jnp.where(lane24 == x, jnp.broadcast_to(prov[2, x, :, BZ - 1 : BZ], (PY, 128)), high)
-    yp[16:17, 0:128] = vertices[4:5]
-    yp[17:18, 0:128] = vertices[9:10]
-    yp[16:17, 128:256] = edge[4:5] + edge_next[9:10]
+    yp[10:11, 0:128] = vertices[4:5]
+    yp[11:12, 0:128] = vertices[9:10]
+    yp[10:11, 128:256] = edge[4:5] + edge_next[9:10]
     zm[...] = low * z_low
     zp[...] = high * z_high
     zp[0:4, :] = zp[0:4, :] + (edge[0:4] + edge_next[5:9])
 
 
 def right_kernel(packed, prov, PH, PL, weights, rhs):
-    ry = packed.get(weights, "ry")
+    ry = packed.both(weights, "ry")
     for i, (n0, n1, k0, k1) in enumerate(WINDOWS):
         b = packed.get(weights, "rz" + str(i))
         y = left_dot(ry, PH[1, :, n0:n1], PL[1, :, n0:n1])
@@ -406,7 +422,7 @@
 
 def smooth_kernel(
     packed, rhs, hx_lo, hx_hi, hy_lo, hy_hi, hz_lo, hz_hi, own, scale, weights, modes,
-    smoothed, coarse, AH, AL, BH, BL,
+    smoothed, coarse, A, B,
 ):
     lift = 0.5 * LIFT
     lane = lax.broadcasted_iota(jnp.int32, (PY, 128), 1)
@@ -416,7 +432,7 @@
         for x in (2 * q, 2 * q + 1):
             r = rhs[x]
             if x == 0:
-                r = r + lift * hx_lo[0:PY, :]
+                r = r + lift * hx_lo[...]
             if x == BX - 1:
                 r = r - lift * hx_hi[...]
             r = r + jnp.where(row == 0, lift * jnp.broadcast_to(hy_lo[x : x + 1, :], (PY, BZ)), 0.0)
@@ -431,35 +447,29 @@
             )
             planes.append(jnp.concatenate([left, r[:, 128 : BZ - 128], right], axis=1))
         hi, lo = split(jnp.concatenate(planes, axis=0))
-        AH[2 * PY * q : 2 * PY * (q + 1), :] = hi
-        AL[2 * PY * q : 2 * PY * (q + 1), :] = lo
-
+        A[2 * PY * q : 2 * PY * (q + 1), :] = hi
+        A[ROWS + 2 * PY * q : ROWS + 2 * PY * (q + 1), :] = lo
+
+    tf = packed.both(weights, "tf")
     for n0, n1, _, _ in WINDOWS:
-        hi, lo = split(left_dot(packed.get(weights, "tf"), AH[:, n0:n1], AL[:, n0:n1]))
-        BH[:, n0:n1] = hi
-        BL[:, n0:n1] = lo
+        B[:, n0:n1] = stacked(left_dot(tf, A[0:ROWS, n0:n1], A[ROWS:, n0:n1]))
 
     factor = spread_out(packed, weights, split(scale[...].reshape(8, EZ)))
     values = eigen_value_table()
     for i, (n0, n1, k0, k1) in enumerate(WINDOWS):
-        m = packed.get(weights, "sf" + str(i))
-        c = right_dot(BH[:, k0:k1], BL[:, k0:k1], m).reshape(BX, PY, n1 - n0)
+        c = stack_dot(B[:, k0:k1], packed.get(weights, "sf" + str(i))).reshape(BX, PY, n1 - n0)
         done = []
         for x in range(BX):
             f = factor[PY * (x // 5) : PY * (x // 5 + 1), n0:n1]
             done.append(c[x] / (f * (modes[:, n0:n1] + float(values[x % 5])) + 1.0))
-        hi, lo = split(jnp.concatenate(done, axis=0))
-        AH[:, n0:n1] = hi
-        AL[:, n0:n1] = lo
+        A[:, n0:n1] = stacked(jnp.concatenate(done, axis=0))
 
     for i, (n0, n1, k0, k1) in enumerate(WINDOWS):
-        m = packed.get(weights, "sb" + str(i))
-        hi, lo = split(right_dot(AH[:, k0:k1], AL[:, k0:k1], m))
-        BH[:, n0:n1] = hi
-        BL[:, n0:n1] = lo
-
+        B[:, n0:n1] = stacked(stack_dot(A[:, k0:k1], packed.get(weights, "sb" + str(i))))
+
+    tb = packed.both(weights, "tb")
     for n0, n1, _, _ in WINDOWS:
-        c = left_dot(packed.get(weights, "tb"), BH[:, n0:n1], BL[:, n0:n1]).reshape(BX, PY, n1 - n0)
+        c = left_dot(tb, B[0:ROWS, n0:n1], B[ROWS:, n0:n1]).reshape(BX, PY, n1 - n0)
         smoothed[:, :, n0:n1] = c[:, 0:BY]
 
     lane4 = lax.broadcasted_iota(jnp.int32, (4, 128), 1)
@@ -467,9 +477,9 @@
     for vx in range(EX):
         total = own[5 * vx : 5 * vx + 4, :]
         if vx == 0:
-            total = total + hx_lo[24:28, 0:128]
+            total = total + hx_lo[20:24, 0:128]
         total = total + jnp.where(
-            row4 == 0, jnp.broadcast_to(hy_lo[16 + vx : 17 + vx, 0:128], (4, 128)), 0.0
+            row4 == 0, jnp.broadcast_to(hy_lo[10 + vx : 11 + vx, 0:128], (4, 128)), 0.0
         )
         k = ZEDGE + vx
         total = total + jnp.where(
@@ -556,26 +566,26 @@
     volume, lift, right, smooth, modes = constants()
     faces = run(
         pack_kernel,
-        [like(3, PY, BZ)] * 2 + [like(3, BX, BZ)] * 2 + [like(PY, 128)] * 2,
+        [like(3 * BX, BZ)] * 2 + [like(PY, 128)] * 2,
         [velocity],
         name="pack",
         flops=10**10,
     )
     halo = [
-        shift(faces[1], "gx", 1),
-        shift(faces[0], "gx", -1),
-        shift(faces[3], "gy", 1),
-        shift(faces[2], "gy", -1),
-        shift(faces[5], "gz", 1),
+        shift(velocity[:, BX - 1], "gx", 1),
+        shift(velocity[:, 0], "gx", -1),
+        shift(faces[1], "gy", 1),
+        shift(faces[0], "gy", -1),
+        shift(faces[3], "gz", 1),
     ]
-    halo[0], last = lax.optimization_barrier((halo[0], faces[4]))
+    halo[0], last = lax.optimization_barrier((halo[0], faces[2]))
     halo.append(shift(last, "gz", -1))
     field = like(3, BX, PY, BZ)
     half = jax.ShapeDtypeStruct((3, ROWS, BZ), BF16)
     (conv,) = run(
         functools.partial(volume_kernel, volume),
         [field],
-        [velocity, faces[4], volume.array()],
+        [velocity, faces[2], volume.array()],
         scratch=[pltpu.VMEM((3, BX, PY, BZ), F32)] + [pltpu.VMEM((5, ROWS, BZ), BF16)] * 2,
         name="volume",
         flops=4 * 10**9,
@@ -583,7 +593,7 @@
     prov, ph, plo, xp, xm, yp, ym, zp, zm, own = run(
         functools.partial(lift_kernel, lift),
         [field, half, half]
-        + [like(32, BZ), like(PY, BZ), like(24, BZ), like(16, BZ), like(PY, 128), like(PY, 128)]
+        + [like(PY, BZ), like(PY, BZ), like(16, BZ), like(16, BZ), like(PY, 128), like(PY, 128)]
         + [like(16, 128)],
         [velocity, conv, *halo, obstacle_element_mask, lift.array()],
         scratch=[pltpu.VMEM((3, BX + 2, PY, 896), F32)],
@@ -598,20 +608,21 @@
         flops=2 * 10**9,
     )
     gx_lo = shift(xp, "gx", 1)
+    gz_hi = shift(zm, "gz", -1)
+    gx_lo, gz_hi = lax.optimization_barrier((gx_lo, gz_hi))
     gx_hi = shift(xm, "gx", -1)
-    yp = yp + jnp.pad(gx_lo[28:29, 0:256], ((16, 7), (0, BZ - 256)))
+    yp = yp + jnp.pad(gx_lo[20:21, 256:512], ((10, 5), (0, BZ - 256)))
     gy_lo = shift(yp, "gy", 1)
     gy_hi = shift(ym, "gy", -1)
-    zp = zp + jnp.pad(gx_lo[24:28, 128:256], ((0, 20), (0, 0)))
-    zp = zp + jnp.pad(gy_lo[16:17, 128:256], ((0, 23), (0, 0)))
+    zp = zp + jnp.pad(gx_lo[20:24, 128:256], ((0, 20), (0, 0)))
+    zp = zp + jnp.pad(gy_lo[10:11, 128:256], ((0, 23), (0, 0)))
     gz_lo = shift(zp, "gz", 1)
-    gz_hi = shift(zm, "gz", -1)
     smoothed, coarse = run(
         functools.partial(smooth_kernel, smooth),
         [like(BX, BY, BZ), like(EX, EY, EZ)],
         [rhs, gx_lo, gx_hi, gy_lo, gy_hi, gz_lo, gz_hi, own, element_metric_scale]
         + [smooth.array(), jnp.asarray(modes)],
-        scratch=[pltpu.VMEM((ROWS, BZ), BF16)] * 4,
+        scratch=[pltpu.VMEM((2 * ROWS, BZ), BF16)] * 2,
         name="smooth",
         flops=3 * 10**9,
     )

time: 43.7 us -> 41.9 us (0.959)
  waiting for transfers between devices: 11.5 us -> 8.16 us
  local copies, waits for them, and re-layouts: 1.54 us -> 2.58 us
  starting transfers between devices: 17.9 us -> 18.8 us
    ppermute x12, waiting for transfers between devices: 11.5 us -> 8.16 us  [shift(): return lax.ppermute(x, axis, [(i, (i + by) % size) for i in range(size)])]
    squeeze x0 -> x1, local copies, waits for them, and re-layouts: none -> 1.04 us  [shards(): velocity[:, 0]]
    ppermute x12, starting transfers between devices: 17.9 us -> 18.8 us  [shift(): return lax.ppermute(x, axis, [(i, (i + by) % size) for i in range(size)])]
  transfers between devices with their start and end apart: 12 -> 12, of which waited for: 4 -> 5; matrix products, arithmetic and copies ran while one was open for 0% -> 0% of each run, Pallas kernels for 11% -> 13%
where the time goes in v2:
time: 41.9 us; the launch traced here: 41.8 us
  starting transfers between devices  18.8 us (45%)
  Pallas kernels  11.5 us (27%)
  waiting for transfers between devices  8.16 us (19%)
  local copies, waits for them, and re-layouts  2.58 us (6%)
  between operations  0.77 us (2%)
    ppermute x12, starting transfers between devices, shift(): return lax.ppermute(x, axis, [(i, (i + by) % size) for i in range(size)])  18.8 us
    pallas_call x5, Pallas kernels, run(): pl.pallas_call(kernel, out_shape=outs, in_specs=[vmem] * len(operands), o...  11.5 us
    ppermute x12, waiting for transfers between devices, shift(): return lax.ppermute(x, axis, [(i, (i + by) % size) for i in range(size)])  8.16 us
    unnamed x16, local copies, waits for them, and re-layouts  1.53 us
    squeeze x1, local copies, waits for them, and re-layouts, shards(): velocity[:, 0]  1.04 us
  transfers between devices with their start and end apart: 12, of which 5 were waited for; matrix products, arithmetic and copies ran while one was open for 0% of the time, Pallas kernels for 13%

profile of v2, /device:TPU:0, one launch (start us, length us, event | category | flops | bytes accessed | tf_op | source)
XLA Modules:
  0.0 41.8 jit_solution(6322584691082277172)
XLA Ops:
  0.6 1.0 %slice_bitcast_fusion = (f32[3,20,640]{2,1,0:T(8,128)S(1)}, f32[3,20,640]{2,1,0:T(8,128)S(1)}) fusion(f32[3,10,20,640]{3,2,1,0:T(8,128)} %v.5), kind=kLoop, calls=%fused_computation | loop fusion | bytes 614400 | tf_op jit(solution)/shard_map/squeeze | solution.py:576
  1.7 1.7 %collective-permute-start = (f32[3,20,640]{2,1,0:T(8,128)S(1)}, f32[3,20,640]{2,1,0:T(8,128)S(1)}, u32[]{:S(2)}, u32[]{:S(2)}) collective-permute-start(f32[3,20,640]{2,1,0:T(8,128)S(1)} %get-tuple-element.39), channel_id=1, source_target_pairs={{0,16},{16,32},{32,48},{48,64},{64,80},{80,96},{96,112},{112,0},{1... | collective-permute-start | bytes 460808 | tf_op jit(solution)/shard_map/ppermute | solution.py:544
  3.4 0.0 copy-start
  3.4 1.5 %copy-done = f32[3,10,20,640]{3,2,1,0:T(8,128)S(1)} copy-done((f32[3,10,20,640]{3,2,1,0:T(8,128)S(1)}, f32[3,10,20,640]{3,2,1,0:T(8,128)}, u32[]{:S(2)}) %copy-start) | copy-done | bytes 1536024
  4.9 0.0 copy-start.6
  4.9 0.4 pack.1
  5.3 2.0 %collective-permute-start.4 = (f32[24,128]{1,0:T(8,128)S(1)}, f32[24,128]{1,0:T(8,128)S(1)}, u32[]{:S(2)}, u32[]{:S(2)}) collective-permute-start(f32[24,128]{1,0:T(8,128)S(1)} %get-tuple-element.24), channel_id=1, source_target_pairs={{0,1},{1,2},{2,3},{3,0},{4,5},{5,6},{6,7},{7,4},{8,9},{9,10},{10,1... | collective-permute-start | bytes 36872 | tf_op jit(solution)/shard_map/ppermute | solution.py:544
  7.3 0.0 collective-permute-start.2
  7.3 3.2 %collective-permute-start.3 = (f32[30,640]{1,0:T(8,128)S(1)}, f32[30,640]{1,0:T(8,128)S(1)}, u32[]{:S(2)}, u32[]{:S(2)}) collective-permute-start(f32[30,640]{1,0:T(8,128)S(1)} %get-tuple-element.23), channel_id=1, source_target_pairs={{0,12},{4,0},{8,4},{12,8},{1,13},{5,1},{9,5},{13,9},{2,14},{6,2},{... | collective-permute-start | bytes 230408 | tf_op jit(solution)/shard_map/ppermute | solution.py:544
  10.5 2.6 %collective-permute-start.1 = (f32[3,20,640]{2,1,0:T(8,128)S(1)}, f32[3,20,640]{2,1,0:T(8,128)S(1)}, u32[]{:S(2)}, u32[]{:S(2)}) collective-permute-start(f32[3,20,640]{2,1,0:T(8,128)S(1)} %get-tuple-element.38), channel_id=1, source_target_pairs={{0,112},{16,0},{32,16},{48,32},{64,48},{80,64},{96,80},{112,96},{1... | collective-permute-start | bytes 460808 | tf_op jit(solution)/shard_map/ppermute | solution.py:544
  13.1 0.0 collective-permute-done.hx_lo
  13.1 0.0 copy-start.1
  13.1 0.0 copy-start.4
  13.1 2.2 %collective-permute-start.5 = (f32[24,128]{1,0:T(8,128)S(1)}, f32[24,128]{1,0:T(8,128)S(1)}, u32[]{:S(2)}, u32[]{:S(2)}) collective-permute-start(f32[24,128]{1,0:T(8,128)S(1)} %get-tuple-element.25.after), channel_id=1, source_target_pairs={{0,3},{1,0},{2,1},{3,2},{4,7},{5,4},{6,5},{7,6},{8,11},{9,8},{10,9... | collective-permute-start | bytes 36872 | tf_op jit(solution)/shard_map/ppermute | solution.py:544
  15.3 0.0 copy-done.6
  15.3 3.8 %volume.1.conv = f32[3,10,24,640]{3,2,1,0:T(8,128)S(1)} custom-call(f32[3,10,20,640]{3,2,1,0:T(8,128)S(1)} %copy-done, f32[24,128]{1,0:T(8,128)S(1)} %get-tuple-element.25.after, bf16[2784,256]{1,0:T(8,128)(2,1)S(1)} %copy-done.6), custom_call_target="tpu_custom_call" | custom-call | flops 4000000000 | bytes 4194304 | tf_op jit(solution)/shard_map/volume/pallas_call | solution.py:553
  19.1 0.0 copy-start.5
  19.1 0.0 collective-permute-done.4.hz_lo
  19.1 0.0 collective-permute-done.2.hy_lo
  19.1 0.0 collective-permute-done.3.hy_hi
  19.1 0.0 collective-permute-done.1.hx_hi
  19.2 0.0 collective-permute-done.5.hz_hi
  19.2 0.0 copy-done.1
  19.2 0.0 copy-done.4
  19.2 3.2 %lift.1 = (f32[3,10,24,640]{3,2,1,0:T(8,128)S(1)}, bf16[3,240,640]{2,1,0:T(8,128)(2,1)S(1)}, bf16[3,240,640]{2,1,0:T(8,128)(2,1)S(1)}, f32[24,640]{1,0:T(8,128)S...) custom-call(f32[3,10,20,640]{3,2,1,0:T(8,128)S(1)} %copy-done, ...), custom_call_target="tpu_custom_call" | custom-call | flops 4000000000 | bytes 4194304 | tf_op jit(solution)/shard_map/lift/pallas_call | solution.py:553
  22.4 0.1 collective-permute-start.6
  22.5 2.0 %collective-permute-start.7 = (f32[24,128]{1,0:T(8,128)S(1)}, f32[24,128]{1,0:T(8,128)S(1)}, u32[]{:S(2)}, u32[]{:S(2)}) collective-permute-start(f32[24,128]{1,0:T(8,128)S(1)} %get-tuple-element.30), channel_id=1, source_target_pairs={{0,3},{1,0},{2,1},{3,2},{4,7},{5,4},{6,5},{7,6},{8,11},{9,8},{10,9... | collective-permute-start | bytes 36872 | tf_op jit(solution)/shard_map/ppermute | solution.py:544
  24.5 1.8 %collective-permute-done.7.hz_hi = f32[24,128]{1,0:T(8,128)S(1)} collective-permute-done((f32[24,128]{1,0:T(8,128)S(1)}, f32[24,128]{1,0:T(8,128)S(1)}, u32[]{:S(2)}, u32[]{:S(2)}) %collective-permute-start.7) | collective-permute-done | bytes 12320 | tf_op jit(solution)/shard_map/ppermute | solution.py:544
  26.3 2.6 %collective-permute-done.6.hx_lo = f32[24,640]{1,0:T(8,128)S(1)} collective-permute-done((f32[24,640]{1,0:T(8,128)S(1)}, f32[24,640]{1,0:T(8,128)S(1)}, u32[]{:S(2)}, u32[]{:S(2)}) %collective-permute-start.6) | collective-permute-done | bytes 61472 | tf_op jit(solution)/shard_map/ppermute | solution.py:544
  28.8 0.1 collective-permute-start.9
  28.9 3.2 %collective-permute-start.10 = (f32[16,640]{1,0:T(8,128)S(1)}, f32[16,640]{1,0:T(8,128)S(1)}, u32[]{:S(2)}, u32[]{:S(2)}) collective-permute-start(f32[16,640]{1,0:T(8,128)S(1)} %get-tuple-element.34), channel_id=1, source_target_pairs={{0,12},{4,0},{8,4},{12,8},{1,13},{5,1},{9,5},{13,9},{2,14},{6,2},{... | collective-permute-start | bytes 122888 | tf_op jit(solution)/shard_map/ppermute | solution.py:544
  32.1 1.5 %collective-permute-start.8 = (f32[24,640]{1,0:T(8,128)S(1)}, f32[24,640]{1,0:T(8,128)S(1)}, u32[]{:S(2)}, u32[]{:S(2)}) collective-permute-start(f32[24,640]{1,0:T(8,128)S(1)} %get-tuple-element.32), channel_id=1, source_target_pairs={{0,112},{16,0},{32,16},{48,32},{64,48},{80,64},{96,80},{112,96},{1... | collective-permute-start | bytes 184328 | tf_op jit(solution)/shard_map/ppermute | solution.py:544
  33.7 0.2 collective-permute-done.9.hy_lo
  33.8 0.1 collective-permute-start.11
  34.0 0.0 copy-done.5
  34.0 0.0 copy-start.2
  34.0 0.0 copy-start.3
  34.0 0.0 copy-start.7
  34.0 1.1 %right.1.rhs = f32[10,24,640]{2,1,0:T(8,128)S(1)} custom-call(f32[3,10,24,640]{3,2,1,0:T(8,128)S(1)} %get-tuple-element.26.prov, bf16[3,240,640]{2,1,0:T(8,128)(2,1)S(1)} %get-tuple-element.27.PH, bf16[3,240,640]{2,1,0:T(8,128)(2,1)S(1)} %get-tuple-element.28.PL, bf16[2784,256]{1,0:T(8,128)(2,1)S(1)} %copy-done.5), custom_call_target="tpu_custom_call" | custom-call | flops 2000000000 | bytes 4194304 | tf_op jit(solution)/shard_map/right/pallas_call | solution.py:553
  35.1 0.0 collective-permute-done.10.hy_hi
  35.1 1.2 %collective-permute-done.8.hx_hi = f32[24,640]{1,0:T(8,128)S(1)} collective-permute-done((f32[24,640]{1,0:T(8,128)S(1)}, f32[24,640]{1,0:T(8,128)S(1)}, u32[]{:S(2)}, u32[]{:S(2)}) %collective-permute-start.8) | collective-permute-done | bytes 61472 | tf_op jit(solution)/shard_map/ppermute | solution.py:544
  36.4 2.4 %collective-permute-done.11.hz_lo = f32[24,128]{1,0:T(8,128)S(1)} collective-permute-done((f32[24,128]{1,0:T(8,128)S(1)}, f32[24,128]{1,0:T(8,128)S(1)}, u32[]{:S(2)}, u32[]{:S(2)}) %collective-permute-start.11) | collective-permute-done | bytes 12320 | tf_op jit(solution)/shard_map/ppermute | solution.py:544
  38.8 0.0 copy-done.2
  38.8 0.0 copy-done.3
  38.8 0.0 copy-done.7
  38.8 3.0 %smooth.1 = (f32[10,20,640]{2,1,0:T(8,128)}, f32[2,4,128]{2,1,0:T(4,128)}) custom-call(f32[10,24,640]{2,1,0:T(8,128)S(1)} %right.1.rhs, f32[24,640]{1,0:T(8,128)S(1)} %collective-permute-done.6.hx_lo, f32[24,640]{1,0:T(8,128)S(1)} %collective-permute-done.8.hx_hi, f32[16,640]{1,0:T(8,128)S(1)} %collective-permute-done.9.hy_lo, ...), custom_call_target="tpu_custom_call" | custom-call | flops 3000000000 | bytes 4194304 | tf_op jit(solution)/shard_map/smooth/pallas_call | solution.py:553
  (5 shorter events, 0.0 us)
Async XLA Ops:
  1.7 11.4 %collective-permute-start = (f32[3,20,640]{2,1,0:T(8,128)S(1)}, f32[3,20,640]{2,1,0:T(8,128)S(1)}, u32[]{:S(2)}, u32[]{:S(2)}) collective-permute-start(f32[3,20,640]{2,1,0:T(8,128)S(1)} %get-tuple-element.39), channel_id=1, source_target_pairs={{0,16},{16,32},{32,48},{48,64},{64,80},{80,96},{96,112},{112,0},{1... | collective-permute-start | bytes 460808 | tf_op jit(solution)/shard_map/ppermute | solution.py:544
  3.4 1.5 %copy-start = (f32[3,10,20,640]{3,2,1,0:T(8,128)S(1)}, f32[3,10,20,640]{3,2,1,0:T(8,128)}, u32[]{:S(2)}) copy-start(f32[3,10,20,640]{3,2,1,0:T(8,128)} %v.5) | copy-start | bytes 4608004
  4.9 10.4 %copy-start.6 = (bf16[2784,256]{1,0:T(8,128)(2,1)S(1)}, bf16[2784,256]{1,0:T(8,128)(2,1)}, u32[]{:S(2)}) copy-start(bf16[2784,256]{1,0:T(8,128)(2,1)} %constant.13.clone.weights) | copy-start | bytes 4276228
  5.3 13.8 %collective-permute-start.4 = (f32[24,128]{1,0:T(8,128)S(1)}, f32[24,128]{1,0:T(8,128)S(1)}, u32[]{:S(2)}, u32[]{:S(2)}) collective-permute-start(f32[24,128]{1,0:T(8,128)S(1)} %get-tuple-element.24), channel_id=1, source_target_pairs={{0,1},{1,2},{2,3},{3,0},{4,5},{5,6},{6,7},{7,4},{8,9},{9,10},{10,1... | collective-permute-start | bytes 36872 | tf_op jit(solution)/shard_map/ppermute | solution.py:544
  7.3 11.9 %collective-permute-start.2 = (f32[30,640]{1,0:T(8,128)S(1)}, f32[30,640]{1,0:T(8,128)S(1)}, u32[]{:S(2)}, u32[]{:S(2)}) collective-permute-start(f32[30,640]{1,0:T(8,128)S(1)} %get-tuple-element.22), channel_id=1, source_target_pairs={{0,4},{4,8},{8,12},{12,0},{1,5},{5,9},{9,13},{13,1},{2,6},{6,10},{... | collective-permute-start | bytes 230408 | tf_op jit(solution)/shard_map/ppermute | solution.py:544
  7.3 11.9 %collective-permute-start.3 = (f32[30,640]{1,0:T(8,128)S(1)}, f32[30,640]{1,0:T(8,128)S(1)}, u32[]{:S(2)}, u32[]{:S(2)}) collective-permute-start(f32[30,640]{1,0:T(8,128)S(1)} %get-tuple-element.23), channel_id=1, source_target_pairs={{0,12},{4,0},{8,4},{12,8},{1,13},{5,1},{9,5},{13,9},{2,14},{6,2},{... | collective-permute-start | bytes 230408 | tf_op jit(solution)/shard_map/ppermute | solution.py:544
  10.5 8.6 %collective-permute-start.1 = (f32[3,20,640]{2,1,0:T(8,128)S(1)}, f32[3,20,640]{2,1,0:T(8,128)S(1)}, u32[]{:S(2)}, u32[]{:S(2)}) collective-permute-start(f32[3,20,640]{2,1,0:T(8,128)S(1)} %get-tuple-element.38), channel_id=1, source_target_pairs={{0,112},{16,0},{32,16},{48,32},{64,48},{80,64},{96,80},{112,96},{1... | collective-permute-start | bytes 460808 | tf_op jit(solution)/shard_map/ppermute | solution.py:544
  13.1 6.1 %copy-start.1 = (s32[2,4,128]{2,1,0:T(4,128)S(1)}, s32[2,4,128]{2,1,0:T(4,128)}, u32[]{:S(2)}) copy-start(s32[2,4,128]{2,1,0:T(4,128)} %mask.1) | copy-start | bytes 12292
  13.1 6.1 %copy-start.4 = (bf16[3152,256]{1,0:T(8,128)(2,1)S(1)}, bf16[3152,256]{1,0:T(8,128)(2,1)}, u32[]{:S(2)}) copy-start(bf16[3152,256]{1,0:T(8,128)(2,1)} %constant.14.clone.weights) | copy-start | bytes 4841476
  13.1 6.1 %collective-permute-start.5 = (f32[24,128]{1,0:T(8,128)S(1)}, f32[24,128]{1,0:T(8,128)S(1)}, u32[]{:S(2)}, u32[]{:S(2)}) collective-permute-start(f32[24,128]{1,0:T(8,128)S(1)} %get-tuple-element.25.after), channel_id=1, source_target_pairs={{0,3},{1,0},{2,1},{3,2},{4,7},{5,4},{6,5},{7,6},{8,11},{9,8},{10,9... | collective-permute-start | bytes 36872 | tf_op jit(solution)/shard_map/ppermute | solution.py:544
  19.1 14.9 %copy-start.5 = (bf16[2784,256]{1,0:T(8,128)(2,1)S(1)}, bf16[2784,256]{1,0:T(8,128)(2,1)}, u32[]{:S(2)}) copy-start(bf16[2784,256]{1,0:T(8,128)(2,1)} %constant.15.clone.weights) | copy-start | bytes 4276228
  22.4 6.4 %collective-permute-start.6 = (f32[24,640]{1,0:T(8,128)S(1)}, f32[24,640]{1,0:T(8,128)S(1)}, u32[]{:S(2)}, u32[]{:S(2)}) collective-permute-start(f32[24,640]{1,0:T(8,128)S(1)} %get-tuple-element.29), channel_id=1, source_target_pairs={{0,16},{16,32},{32,48},{48,64},{64,80},{80,96},{96,112},{112,0},{1... | collective-permute-start | bytes 184328 | tf_op jit(solution)/shard_map/ppermute | solution.py:544
  22.5 3.8 %collective-permute-start.7 = (f32[24,128]{1,0:T(8,128)S(1)}, f32[24,128]{1,0:T(8,128)S(1)}, u32[]{:S(2)}, u32[]{:S(2)}) collective-permute-start(f32[24,128]{1,0:T(8,128)S(1)} %get-tuple-element.30), channel_id=1, source_target_pairs={{0,3},{1,0},{2,1},{3,2},{4,7},{5,4},{6,5},{7,6},{8,11},{9,8},{10,9... | collective-permute-start | bytes 36872 | tf_op jit(solution)/shard_map/ppermute | solution.py:544
  28.8 5.0 %collective-permute-start.9 = (f32[16,640]{1,0:T(8,128)S(1)}, f32[16,640]{1,0:T(8,128)S(1)}, u32[]{:S(2)}, u32[]{:S(2)}) collective-permute-start(f32[16,640]{1,0:T(8,128)S(1)} %pad_add_fusion), channel_id=1, source_target_pairs={{0,4},{4,8},{8,12},{12,0},{1,5},{5,9},{9,13},{13,1},{2,6},{6,10},{... | collective-permute-start | bytes 122888 | tf_op jit(solution)/shard_map/ppermute | solution.py:544
  28.9 6.2 %collective-permute-start.10 = (f32[16,640]{1,0:T(8,128)S(1)}, f32[16,640]{1,0:T(8,128)S(1)}, u32[]{:S(2)}, u32[]{:S(2)}) collective-permute-start(f32[16,640]{1,0:T(8,128)S(1)} %get-tuple-element.34), channel_id=1, source_target_pairs={{0,12},{4,0},{8,4},{12,8},{1,13},{5,1},{9,5},{13,9},{2,14},{6,2},{... | collective-permute-start | bytes 122888 | tf_op jit(solution)/shard_map/ppermute | solution.py:544
  32.1 4.2 %collective-permute-start.8 = (f32[24,640]{1,0:T(8,128)S(1)}, f32[24,640]{1,0:T(8,128)S(1)}, u32[]{:S(2)}, u32[]{:S(2)}) collective-permute-start(f32[24,640]{1,0:T(8,128)S(1)} %get-tuple-element.32), channel_id=1, source_target_pairs={{0,112},{16,0},{32,16},{48,32},{64,48},{80,64},{96,80},{112,96},{1... | collective-permute-start | bytes 184328 | tf_op jit(solution)/shard_map/ppermute | solution.py:544
  33.8 5.0 %collective-permute-start.11 = (f32[24,128]{1,0:T(8,128)S(1)}, f32[24,128]{1,0:T(8,128)S(1)}, u32[]{:S(2)}, u32[]{:S(2)}) collective-permute-start(f32[24,128]{1,0:T(8,128)S(1)} %pad_add_fusion.1), channel_id=1, source_target_pairs={{0,1},{1,2},{2,3},{3,0},{4,5},{5,6},{6,7},{7,4},{8,9},{9,10},{10,1... | collective-permute-start | bytes 36872 | tf_op jit(solution)/shard_map/ppermute | solution.py:544
  34.0 4.8 %copy-start.2 = (f32[2,4,128]{2,1,0:T(4,128)S(1)}, f32[2,4,128]{2,1,0:T(4,128)}, u32[]{:S(2)}) copy-start(f32[2,4,128]{2,1,0:T(4,128)} %scale.1) | copy-start | bytes 12292
  34.0 4.8 %copy-start.3 = (bf16[6000,256]{1,0:T(8,128)(2,1)S(1)}, bf16[6000,256]{1,0:T(8,128)(2,1)}, u32[]{:S(2)}) copy-start(bf16[6000,256]{1,0:T(8,128)(2,1)} %constant.16.clone.weights) | copy-start | bytes 9216004
  34.0 4.8 %copy-start.7 = (f32[24,640]{1,0:T(8,128)S(1)}, f32[24,640]{1,0:T(8,128)}, u32[]{:S(2)}) copy-start(f32[24,640]{1,0:T(8,128)} %constant.17.clone.modes) | copy-start | bytes 184324

commit v3 on v2

--- a/solution.py
+++ b/solution.py
@@ -19,7 +19,8 @@
 PY = 24
 ROWS = BX * PY
 TILES = BZ // 128
-WINDOWS = ((0, 256, 0, 384), (256, 512, 128, 640), (512, 640, 384, 640))
+WINDOWS = ((0, 250, 0, 251), (250, 500, 249, 501), (500, 640, 499, 640))
+LANES = ((0, 256), (256, 512), (512, 640))
 ZEDGE = 16
 
 F32 = jnp.float32
@@ -148,9 +149,9 @@
             self.rows += part.shape[0]
         self.places[name] = places
 
-    def add_windows(self, name, m):
+    def add_windows(self, name, m, coupled=True):
         for i, (n0, n1, k0, k1) in enumerate(WINDOWS):
-            self.add(name + str(i), m[k0:k1, n0:n1])
+            self.add(name + str(i), m[k0:k1, n0:n1] if coupled else m[n0:n1, n0:n1])
 
     def array(self):
         return jnp.asarray(np.concatenate(self.parts))
@@ -196,6 +197,14 @@
 def flag(name, low):
     edge = 0 if low else lax.axis_size(name) - 1
     return jnp.where(lax.axis_index(name) == edge, 0.0, 1.0)
+
+
+def face_kernel(v_lo, v_hi, x_lo, x_hi):
+    for c in range(3):
+        x_lo[c, 0:BY, :] = v_lo[c] * flag("gx", True)
+        x_hi[c, 0:BY, :] = v_hi[c] * flag("gx", False)
+        x_lo[c, BY:PY, :] = jnp.zeros((PY - BY, BZ), F32)
+        x_hi[c, BY:PY, :] = jnp.zeros((PY - BY, BZ), F32)
 
 
 def pack_kernel(v, y_lo, y_hi, z_lo, z_hi):
@@ -250,16 +259,18 @@
 
     lax.fori_loop(0, TILES, products, 0)
 
-    my = packed.both(weights, "my")
     for i, (n0, n1, k0, k1) in enumerate(WINDOWS):
         high = FH[2:5, :, k0:k1].reshape(3 * ROWS, k1 - k0)
         low = FL[2:5, :, k0:k1].reshape(3 * ROWS, k1 - k0)
         z = right_dot(high, low, packed.get(weights, "bz" + str(i)))
         for c in range(3):
             along_z = ROWS * (1, 0, 2)[c]
-            y = left_dot(my, FH[c, :, n0:n1], FL[c, :, n0:n1])
-            total = y + z[along_z : along_z + ROWS]
-            conv[c, :, :, n0:n1] = total.reshape(BX, PY, n1 - n0)
+            conv[c, :, :, n0:n1] = z[along_z : along_z + ROWS].reshape(BX, PY, n1 - n0)
+    my = packed.both(weights, "my")
+    for n0, n1 in LANES:
+        for c in range(3):
+            y = left_dot(my, FH[c, :, n0:n1], FL[c, :, n0:n1]).reshape(BX, PY, n1 - n0)
+            conv[c, :, :, n0:n1] = conv[c, :, :, n0:n1] + y
 
     def along_x(t, carry):
         dst = pl.ds(pl.multiple_of(128 * t, 128), 128)
@@ -279,10 +290,8 @@
     prov, PH, PL, xp, xm, yp, ym, zp, zm, own, V,
 ):
     for c in range(3):
-        V[c, 0, 0:BY, 128:768] = hx_lo[c] * flag("gx", True)
-        V[c, BX + 1, 0:BY, 128:768] = hx_hi[c] * flag("gx", False)
-        V[c, 0, BY:PY, 128:768] = jnp.zeros((PY - BY, BZ), F32)
-        V[c, BX + 1, BY:PY, 128:768] = jnp.zeros((PY - BY, BZ), F32)
+        V[c, 0, :, 128:768] = hx_lo[c]
+        V[c, BX + 1, :, 128:768] = hx_hi[c]
         for x in range(BX):
             r = BX * c + x
             V[c, x + 1, 0:BY, 128:768] = v[c, x]
@@ -293,6 +302,7 @@
             V[c, x + 1, :, 768:896] = jnp.broadcast_to(hz_hi[:, k : k + 1], (PY, 128))
 
     solid = spread_out(packed, weights, [mask[...].astype(F32).reshape(8, EZ).astype(BF16)])
+    solid = jnp.concatenate(solid, axis=1)
     conv_scale = -0.5 * LIFT * STEP
     lane = lax.broadcasted_iota(jnp.int32, (PY, 128), 1)
     row = lax.broadcasted_iota(jnp.int32, (PY, 128), 0)
@@ -391,12 +401,13 @@
 
 
 def right_kernel(packed, prov, PH, PL, weights, rhs):
+    for i, (n0, n1, k0, k1) in enumerate(WINDOWS):
+        z = right_dot(PH[2, :, k0:k1], PL[2, :, k0:k1], packed.get(weights, "rz" + str(i)))
+        rhs[:, :, n0:n1] = z.reshape(BX, PY, n1 - n0)
     ry = packed.both(weights, "ry")
-    for i, (n0, n1, k0, k1) in enumerate(WINDOWS):
-        b = packed.get(weights, "rz" + str(i))
-        y = left_dot(ry, PH[1, :, n0:n1], PL[1, :, n0:n1])
-        z = right_dot(PH[2, :, k0:k1], PL[2, :, k0:k1], b)
-        rhs[:, :, n0:n1] = (y + z).reshape(BX, PY, n1 - n0)
+    for n0, n1 in LANES:
+        y = left_dot(ry, PH[1, :, n0:n1], PL[1, :, n0:n1]).reshape(BX, PY, n1 - n0)
+        rhs[:, :, n0:n1] = rhs[:, :, n0:n1] + y
 
     def right_x(t, carry):
         dst = pl.ds(pl.multiple_of(128 * t, 128), 128)
@@ -413,15 +424,28 @@
 
 def spread_out(packed, weights, parts):
     rows_of = packed.get(weights, "rows_of")
-    wide = []
+    nodes = []
     for i in range(3):
         m = packed.get(weights, "spread" + str(i))
-        wide.append(sum(dot(part, m) for part in parts))
-    return sum(dot(rows_of, part) for part in split(jnp.concatenate(wide, axis=1))[: len(parts)])
+        wide = sum(dot(part, m) for part in parts)
+        nodes.append(sum(dot(rows_of, part) for part in split(wide)[: len(parts)]))
+    return nodes
+
+
+def divisor_kernel(packed, scale, after, weights, modes, inverse):
+    del after
+    factor = spread_out(packed, weights, split(scale[...].reshape(8, EZ)))
+    values = eigen_value_table()
+    for i, (n0, n1, _, _) in enumerate(WINDOWS):
+        for x in range(BX):
+            f = factor[i][PY * (x // 5) : PY * (x // 5 + 1)]
+            inverse[x, :, 256 * i : 256 * i + n1 - n0] = 1.0 / (
+                f * (modes[:, 0 : n1 - n0] + float(values[x % 5])) + 1.0
+            )
 
 
 def smooth_kernel(
-    packed, rhs, hx_lo, hx_hi, hy_lo, hy_hi, hz_lo, hz_hi, own, scale, weights, modes,
+    packed, rhs, hx_lo, hx_hi, hy_lo, hy_hi, hz_lo, hz_hi, own, inverse, weights,
     smoothed, coarse, A, B,
 ):
     lift = 0.5 * LIFT
@@ -447,29 +471,24 @@
             )
             planes.append(jnp.concatenate([left, r[:, 128 : BZ - 128], right], axis=1))
         hi, lo = split(jnp.concatenate(planes, axis=0))
-        A[2 * PY * q : 2 * PY * (q + 1), :] = hi
-        A[ROWS + 2 * PY * q : ROWS + 2 * PY * (q + 1), :] = lo
+        A[2 * PY * q : 2 * PY * (q + 1), 0:BZ] = hi
+        A[ROWS + 2 * PY * q : ROWS + 2 * PY * (q + 1), 0:BZ] = lo
 
     tf = packed.both(weights, "tf")
-    for n0, n1, _, _ in WINDOWS:
+    for n0, n1 in LANES:
         B[:, n0:n1] = stacked(left_dot(tf, A[0:ROWS, n0:n1], A[ROWS:, n0:n1]))
 
-    factor = spread_out(packed, weights, split(scale[...].reshape(8, EZ)))
-    values = eigen_value_table()
-    for i, (n0, n1, k0, k1) in enumerate(WINDOWS):
-        c = stack_dot(B[:, k0:k1], packed.get(weights, "sf" + str(i))).reshape(BX, PY, n1 - n0)
-        done = []
-        for x in range(BX):
-            f = factor[PY * (x // 5) : PY * (x // 5 + 1), n0:n1]
-            done.append(c[x] / (f * (modes[:, n0:n1] + float(values[x % 5])) + 1.0))
-        A[:, n0:n1] = stacked(jnp.concatenate(done, axis=0))
-
-    for i, (n0, n1, k0, k1) in enumerate(WINDOWS):
-        B[:, n0:n1] = stacked(stack_dot(A[:, k0:k1], packed.get(weights, "sb" + str(i))))
+    for i, (n0, n1, _, _) in enumerate(WINDOWS):
+        size = n1 - n0
+        c = stack_dot(B[:, n0:n1], packed.get(weights, "sf" + str(i))).reshape(BX, PY, size)
+        c = (c * inverse[:, :, 256 * i : 256 * i + size]).reshape(ROWS, size)
+        c = stack_dot(stacked(c), packed.get(weights, "sb" + str(i)))
+        A[:, 256 * i : 256 * i + size] = stacked(c)
 
     tb = packed.both(weights, "tb")
-    for n0, n1, _, _ in WINDOWS:
-        c = left_dot(tb, B[0:ROWS, n0:n1], B[ROWS:, n0:n1]).reshape(BX, PY, n1 - n0)
+    for i, (n0, n1, _, _) in enumerate(WINDOWS):
+        here = slice(256 * i, 256 * i + n1 - n0)
+        c = left_dot(tb, A[0:ROWS, here], A[ROWS:, here]).reshape(BX, PY, n1 - n0)
         smoothed[:, :, n0:n1] = c[:, 0:BY]
 
     lane4 = lax.broadcasted_iota(jnp.int32, (4, 128), 1)
@@ -489,7 +508,7 @@
 
 
 def constants():
-    volume, lift, right, smooth = Packed(), Packed(), Packed(), Packed()
+    volume, lift, right, smooth, scales = (Packed() for _ in range(5))
     eye_x = np.eye(BX)
     volume.add("my", pad_both(np.kron(eye_x, -STEP * line_operator(EY, False))))
     right.add("ry", pad_both(np.kron(eye_x, -line_operator(EY, True))))
@@ -502,17 +521,17 @@
     t = np.kron(sx, sy)
     smooth.add("tf", pad_both(t.T))
     smooth.add("tb", pad_both(t))
-    smooth.add_windows("sf", sz)
-    smooth.add_windows("sb", sz.T)
+    smooth.add_windows("sf", sz, False)
+    smooth.add_windows("sb", sz.T, False)
     spread = np.kron(np.eye(EZ), np.ones((1, 5)))
     rows_of = np.zeros((EX * PY, 8))
     for e in range(EX):
         for y in range(BY):
             rows_of[PY * e + y, EY * e + y // 5] = 1.0
-    for packed in (lift, smooth):
+    for packed, cuts in ((lift, LANES), (scales, WINDOWS)):
         packed.add("rows_of", rows_of, 1)
-        for i, (n0, n1, _, _) in enumerate(WINDOWS):
-            packed.add("spread" + str(i), spread[:, n0:n1], 1)
+        for i, cut in enumerate(cuts):
+            packed.add("spread" + str(i), spread[:, cut[0] : cut[1]], 1)
     values = eigen_value_table()
     modes = np.zeros((PY, BZ))
     for y in range(BY):
@@ -536,7 +555,7 @@
         ("d1", np.kron(hx, ey)),
     ):
         lift.add(name, pad_to(pad_rows(-m), 16, ROWS))
-    return volume, lift, right, smooth, modes.astype(np.float32)
+    return volume, lift, right, smooth, scales, modes.astype(np.float32)
 
 
 def shift(x, axis, by):
@@ -563,7 +582,14 @@
 
 
 def shards(velocity, obstacle_element_mask, element_metric_scale):
-    volume, lift, right, smooth, modes = constants()
+    volume, lift, right, smooth, scales, modes = constants()
+    x_faces = run(
+        face_kernel,
+        [like(3, PY, BZ)] * 2,
+        [velocity[:, 0], velocity[:, BX - 1]],
+        name="face",
+        flops=10**10,
+    )
     faces = run(
         pack_kernel,
         [like(3 * BX, BZ)] * 2 + [like(PY, 128)] * 2,
@@ -572,8 +598,8 @@
         flops=10**10,
     )
     halo = [
-        shift(velocity[:, BX - 1], "gx", 1),
-        shift(velocity[:, 0], "gx", -1),
+        shift(x_faces[1], "gx", 1),
+        shift(x_faces[0], "gx", -1),
         shift(faces[1], "gy", 1),
         shift(faces[0], "gy", -1),
         shift(faces[3], "gz", 1),
@@ -617,12 +643,19 @@
     zp = zp + jnp.pad(gx_lo[20:24, 128:256], ((0, 20), (0, 0)))
     zp = zp + jnp.pad(gy_lo[10:11, 128:256], ((0, 23), (0, 0)))
     gz_lo = shift(zp, "gz", 1)
+    (inverse,) = run(
+        functools.partial(divisor_kernel, scales),
+        [like(BX, PY, 768)],
+        [element_metric_scale, gy_lo, scales.array(), jnp.asarray(modes)],
+        name="divisor",
+        flops=2 * 10**9,
+    )
     smoothed, coarse = run(
         functools.partial(smooth_kernel, smooth),
         [like(BX, BY, BZ), like(EX, EY, EZ)],
-        [rhs, gx_lo, gx_hi, gy_lo, gy_hi, gz_lo, gz_hi, own, element_metric_scale]
-        + [smooth.array(), jnp.asarray(modes)],
-        scratch=[pltpu.VMEM((2 * ROWS, BZ), BF16)] * 2,
+        [rhs, gx_lo, gx_hi, gy_lo, gy_hi, gz_lo, gz_hi, own, inverse]
+        + [smooth.array()],
+        scratch=[pltpu.VMEM((2 * ROWS, 768), BF16), pltpu.VMEM((2 * ROWS, BZ), BF16)],
         name="smooth",
         flops=3 * 10**9,
     )

time: 41.9 us -> 41.1 us (0.981)
  local copies, waits for them, and re-layouts: 2.58 us -> 1.11 us
  starting transfers between devices: 18.8 us -> 19.5 us
  Pallas kernels: 11.5 us -> 11 us
    unnamed x16 -> x18, local copies, waits for them, and re-layouts: 1.53 us -> 0.05 us
    ppermute x12, starting transfers between devices: 18.8 us -> 19.5 us  [shift(): return lax.ppermute(x, axis, [(i, (i + by) % size) for i in range(size)])]
    pallas_call x5 -> x7, Pallas kernels: 11.5 us -> 11 us  [run(): pl.pallas_call(kernel, out_shape=outs, in_specs=[vmem] * len(operands), o...]
  transfers between devices with their start and end apart: 12 -> 12, of which waited for: 5 -> 3; matrix products, arithmetic and copies ran while one was open for 0% -> 0% of each run, Pallas kernels for 13% -> 13%
where the time goes in v3:
time: 41.1 us; the launch traced here: 40.9 us
  starting transfers between devices  19.5 us (47%)
  Pallas kernels  11 us (27%)
  waiting for transfers between devices  8.48 us (21%)
  local copies, waits for them, and re-layouts  1.11 us (3%)
  between operations  0.83 us (2%)
    ppermute x12, starting transfers between devices, shift(): return lax.ppermute(x, axis, [(i, (i + by) % size) for i in range(size)])  19.5 us
    pallas_call x7, Pallas kernels, run(): pl.pallas_call(kernel, out_shape=outs, in_specs=[vmem] * len(operands), o...  11 us
    ppermute x12, waiting for transfers between devices, shift(): return lax.ppermute(x, axis, [(i, (i + by) % size) for i in range(size)])  8.48 us
    squeeze x1, local copies, waits for them, and re-layouts, shards(): velocity[:, BX - 1]  1.05 us
  transfers between devices with their start and end apart: 12, of which 3 were waited for; matrix products, arithmetic and copies ran while one was open for 0% of the time, Pallas kernels for 13%

profile of v3, /device:TPU:0, one launch (start us, length us, event | category | flops | bytes accessed | tf_op | source)
XLA Modules:
  0.0 40.9 jit_solution(12849951938926101839)
XLA Ops:
  0.6 1.0 %slice_bitcast_fusion = (f32[3,20,640]{2,1,0:T(8,128)S(1)}, f32[3,20,640]{2,1,0:T(8,128)S(1)}) fusion(f32[3,10,20,640]{3,2,1,0:T(8,128)} %v.5), kind=kLoop, calls=%fused_computation | loop fusion | bytes 614400 | tf_op jit(solution)/shard_map/squeeze | solution.py:589
  1.7 0.0 copy-start
  1.7 0.0 copy-start.6
  1.7 1.7 %collective-permute-start = (f32[3,24,640]{2,1,0:T(8,128)S(1)}, f32[3,24,640]{2,1,0:T(8,128)S(1)}, u32[]{:S(2)}, u32[]{:S(2)}) collective-permute-start(f32[3,24,640]{2,1,0:T(8,128)S(1)} %get-tuple-element.23), channel_id=1, source_target_pairs={{0,16},{16,32},{32,48},{48,64},{64,80},{80,96},{96,112},{112,0},{1... | collective-permute-start | bytes 552968 | tf_op jit(solution)/shard_map/ppermute | solution.py:563
  3.5 0.0 copy-done
  3.5 0.4 pack.1
  3.9 2.0 %collective-permute-start.4 = (f32[24,128]{1,0:T(8,128)S(1)}, f32[24,128]{1,0:T(8,128)S(1)}, u32[]{:S(2)}, u32[]{:S(2)}) collective-permute-start(f32[24,128]{1,0:T(8,128)S(1)} %get-tuple-element.28), channel_id=1, source_target_pairs={{0,1},{1,2},{2,3},{3,0},{4,5},{5,6},{6,7},{7,4},{8,9},{9,10},{10,1... | collective-permute-start | bytes 36872 | tf_op jit(solution)/shard_map/ppermute | solution.py:563
  5.8 0.0 collective-permute-start.2
  5.8 3.2 %collective-permute-start.3 = (f32[30,640]{1,0:T(8,128)S(1)}, f32[30,640]{1,0:T(8,128)S(1)}, u32[]{:S(2)}, u32[]{:S(2)}) collective-permute-start(f32[30,640]{1,0:T(8,128)S(1)} %get-tuple-element.27), channel_id=1, source_target_pairs={{0,12},{4,0},{8,4},{12,8},{1,13},{5,1},{9,5},{13,9},{2,14},{6,2},{... | collective-permute-start | bytes 230408 | tf_op jit(solution)/shard_map/ppermute | solution.py:563
  9.1 3.7 %collective-permute-start.1 = (f32[3,24,640]{2,1,0:T(8,128)S(1)}, f32[3,24,640]{2,1,0:T(8,128)S(1)}, u32[]{:S(2)}, u32[]{:S(2)}) collective-permute-start(f32[3,24,640]{2,1,0:T(8,128)S(1)} %get-tuple-element.25), channel_id=1, source_target_pairs={{0,112},{16,0},{32,16},{48,32},{64,48},{80,64},{96,80},{112,96},{1... | collective-permute-start | bytes 552968 | tf_op jit(solution)/shard_map/ppermute | solution.py:563
  12.8 0.0 collective-permute-done.hx_lo
  12.8 0.0 copy-start.1
  12.8 0.0 copy-start.4
  12.8 2.2 %collective-permute-start.5 = (f32[24,128]{1,0:T(8,128)S(1)}, f32[24,128]{1,0:T(8,128)S(1)}, u32[]{:S(2)}, u32[]{:S(2)}) collective-permute-start(f32[24,128]{1,0:T(8,128)S(1)} %get-tuple-element.29.after), channel_id=1, source_target_pairs={{0,3},{1,0},{2,1},{3,2},{4,7},{5,4},{6,5},{7,6},{8,11},{9,8},{10,9... | collective-permute-start | bytes 36872 | tf_op jit(solution)/shard_map/ppermute | solution.py:563
  15.0 0.0 copy-done.6
  15.0 3.3 %volume.1.conv = f32[3,10,24,640]{3,2,1,0:T(8,128)S(1)} custom-call(f32[3,10,20,640]{3,2,1,0:T(8,128)S(1)} %copy-done, f32[24,128]{1,0:T(8,128)S(1)} %get-tuple-element.29.after, bf16[1768,256]{1,0:T(8,128)(2,1)S(1)} %copy-done.6), custom_call_target="tpu_custom_call" | custom-call | flops 4000000000 | bytes 4194304 | tf_op jit(solution)/shard_map/volume/pallas_call | solution.py:572
  18.3 0.0 copy-start.5
  18.4 0.0 collective-permute-done.4.hz_lo
  18.4 0.0 collective-permute-done.2.hy_lo
  18.4 0.0 collective-permute-done.3.hy_hi
  18.4 0.0 collective-permute-done.1.hx_hi
  18.4 0.0 collective-permute-done.5.hz_hi
  18.4 0.0 copy-done.1
  18.4 0.0 copy-done.4
  18.4 3.2 %lift.1 = (f32[3,10,24,640]{3,2,1,0:T(8,128)S(1)}, bf16[3,240,640]{2,1,0:T(8,128)(2,1)S(1)}, bf16[3,240,640]{2,1,0:T(8,128)(2,1)S(1)}, f32[24,640]{1,0:T(8,128)S...) custom-call(f32[3,10,20,640]{3,2,1,0:T(8,128)S(1)} %copy-done, ...), custom_call_target="tpu_custom_call" | custom-call | flops 4000000000 | bytes 4194304 | tf_op jit(solution)/shard_map/lift/pallas_call | solution.py:572
  21.6 0.1 collective-permute-start.6
  21.7 2.0 %collective-permute-start.7 = (f32[24,128]{1,0:T(8,128)S(1)}, f32[24,128]{1,0:T(8,128)S(1)}, u32[]{:S(2)}, u32[]{:S(2)}) collective-permute-start(f32[24,128]{1,0:T(8,128)S(1)} %get-tuple-element.34), channel_id=1, source_target_pairs={{0,3},{1,0},{2,1},{3,2},{4,7},{5,4},{6,5},{7,6},{8,11},{9,8},{10,9... | collective-permute-start | bytes 36872 | tf_op jit(solution)/shard_map/ppermute | solution.py:563
  23.7 0.0 collective-permute-start.10
  23.7 4.1 %collective-permute-start.8 = (f32[24,640]{1,0:T(8,128)S(1)}, f32[24,640]{1,0:T(8,128)S(1)}, u32[]{:S(2)}, u32[]{:S(2)}) collective-permute-start(f32[24,640]{1,0:T(8,128)S(1)} %get-tuple-element.36), channel_id=1, source_target_pairs={{0,112},{16,0},{32,16},{48,32},{64,48},{80,64},{96,80},{112,96},{1... | collective-permute-start | bytes 184328 | tf_op jit(solution)/shard_map/ppermute | solution.py:563
  27.8 0.0 collective-permute-done.7.hz_hi
  27.8 0.2 collective-permute-done.6.hx_lo
  28.0 0.1 collective-permute-start.9
  28.1 0.0 copy-done.5
  28.1 0.0 copy-start.2
  28.1 0.0 copy-start.7
  28.1 0.0 copy-start.8
  28.2 1.0 %right.1.rhs = f32[10,24,640]{2,1,0:T(8,128)S(1)} custom-call(f32[3,10,24,640]{3,2,1,0:T(8,128)S(1)} %get-tuple-element.30.prov, bf16[3,240,640]{2,1,0:T(8,128)(2,1)S(1)} %get-tuple-element.31.PH, bf16[3,240,640]{2,1,0:T(8,128)(2,1)S(1)} %get-tuple-element.32.PL, bf16[1768,256]{1,0:T(8,128)(2,1)S(1)} %copy-done.5), custom_call_target="tpu_custom_call" | custom-call | flops 2000000000 | bytes 4194304 | tf_op jit(solution)/shard_map/right/pallas_call | solution.py:572
  29.2 4.2 %collective-permute-done.9.after.hy_lo = f32[16,640]{1,0:T(8,128)S(1)} collective-permute-done((f32[16,640]{1,0:T(8,128)S(1)}, f32[16,640]{1,0:T(8,128)S(1)}, u32[]{:S(2)}, u32[]{:S(2)}) %collective-permute-start.9) | collective-permute-done | bytes 40992 | tf_op jit(solution)/shard_map/ppermute | solution.py:563
  33.3 0.0 copy-start.3
  33.3 0.4 collective-permute-start.11
  33.7 0.0 copy-done.2
  33.7 0.0 copy-done.7
  33.7 0.0 copy-done.8
  33.7 0.5 %divisor.1.inverse = f32[10,24,768]{2,1,0:T(8,128)S(1)} custom-call(f32[2,4,128]{2,1,0:T(4,128)S(1)} %copy-done.2, f32[16,640]{1,0:T(8,128)S(1)} %collective-permute-done.9.after.hy_lo, bf16[432,256]{1,0:T(8,128)(2,1)S(1)} %copy-done.7, f32[24,640]{1,0:T(8,128)S(1)} %copy-done.8), custom_call_target="tpu_custom_call" | custom-call | flops 2000000000 | bytes 4194304 | tf_op jit(solution)/shard_map/divisor/pallas_call | solution.py:572
  34.2 0.0 collective-permute-done.10.hy_hi
  34.2 0.0 collective-permute-done.8.hx_hi
  34.3 4.1 %collective-permute-done.11.hz_lo = f32[24,128]{1,0:T(8,128)S(1)} collective-permute-done((f32[24,128]{1,0:T(8,128)S(1)}, f32[24,128]{1,0:T(8,128)S(1)}, u32[]{:S(2)}, u32[]{:S(2)}) %collective-permute-start.11) | collective-permute-done | bytes 12320 | tf_op jit(solution)/shard_map/ppermute | solution.py:563
  38.3 0.0 copy-done.3
  38.3 2.6 %smooth.1 = (f32[10,20,640]{2,1,0:T(8,128)}, f32[2,4,128]{2,1,0:T(4,128)}) custom-call(f32[10,24,640]{2,1,0:T(8,128)S(1)} %right.1.rhs, f32[24,640]{1,0:T(8,128)S(1)} %collective-permute-done.6.hx_lo, f32[24,640]{1,0:T(8,128)S(1)} %collective-permute-done.8.hx_hi, f32[16,640]{1,0:T(8,128)S(1)} %collective-permute-done.9.after.hy_lo, ...), custom_call_target="tpu_custom_call" | custom-call | flops 3000000000 | bytes 4194304 | tf_op jit(solution)/shard_map/smooth/pallas_call | solution.py:572
  (6 shorter events, 0.1 us)
Async XLA Ops:
  1.7 1.8 %copy-start = (f32[3,10,20,640]{3,2,1,0:T(8,128)S(1)}, f32[3,10,20,640]{3,2,1,0:T(8,128)}, u32[]{:S(2)}) copy-start(f32[3,10,20,640]{3,2,1,0:T(8,128)} %v.5) | copy-start | bytes 4608004
  1.7 13.3 %copy-start.6 = (bf16[1768,256]{1,0:T(8,128)(2,1)S(1)}, bf16[1768,256]{1,0:T(8,128)(2,1)}, u32[]{:S(2)}) copy-start(bf16[1768,256]{1,0:T(8,128)(2,1)} %constant.15.clone.weights) | copy-start | bytes 2715652
  1.7 11.1 %collective-permute-start = (f32[3,24,640]{2,1,0:T(8,128)S(1)}, f32[3,24,640]{2,1,0:T(8,128)S(1)}, u32[]{:S(2)}, u32[]{:S(2)}) collective-permute-start(f32[3,24,640]{2,1,0:T(8,128)S(1)} %get-tuple-element.23), channel_id=1, source_target_pairs={{0,16},{16,32},{32,48},{48,64},{64,80},{80,96},{96,112},{112,0},{1... | collective-permute-start | bytes 552968 | tf_op jit(solution)/shard_map/ppermute | solution.py:563
  3.9 14.5 %collective-permute-start.4 = (f32[24,128]{1,0:T(8,128)S(1)}, f32[24,128]{1,0:T(8,128)S(1)}, u32[]{:S(2)}, u32[]{:S(2)}) collective-permute-start(f32[24,128]{1,0:T(8,128)S(1)} %get-tuple-element.28), channel_id=1, source_target_pairs={{0,1},{1,2},{2,3},{3,0},{4,5},{5,6},{6,7},{7,4},{8,9},{9,10},{10,1... | collective-permute-start | bytes 36872 | tf_op jit(solution)/shard_map/ppermute | solution.py:563
  5.8 12.5 %collective-permute-start.2 = (f32[30,640]{1,0:T(8,128)S(1)}, f32[30,640]{1,0:T(8,128)S(1)}, u32[]{:S(2)}, u32[]{:S(2)}) collective-permute-start(f32[30,640]{1,0:T(8,128)S(1)} %get-tuple-element.26), channel_id=1, source_target_pairs={{0,4},{4,8},{8,12},{12,0},{1,5},{5,9},{9,13},{13,1},{2,6},{6,10},{... | collective-permute-start | bytes 230408 | tf_op jit(solution)/shard_map/ppermute | solution.py:563
  5.8 12.5 %collective-permute-start.3 = (f32[30,640]{1,0:T(8,128)S(1)}, f32[30,640]{1,0:T(8,128)S(1)}, u32[]{:S(2)}, u32[]{:S(2)}) collective-permute-start(f32[30,640]{1,0:T(8,128)S(1)} %get-tuple-element.27), channel_id=1, source_target_pairs={{0,12},{4,0},{8,4},{12,8},{1,13},{5,1},{9,5},{13,9},{2,14},{6,2},{... | collective-permute-start | bytes 230408 | tf_op jit(solution)/shard_map/ppermute | solution.py:563
  9.1 9.3 %collective-permute-start.1 = (f32[3,24,640]{2,1,0:T(8,128)S(1)}, f32[3,24,640]{2,1,0:T(8,128)S(1)}, u32[]{:S(2)}, u32[]{:S(2)}) collective-permute-start(f32[3,24,640]{2,1,0:T(8,128)S(1)} %get-tuple-element.25), channel_id=1, source_target_pairs={{0,112},{16,0},{32,16},{48,32},{64,48},{80,64},{96,80},{112,96},{1... | collective-permute-start | bytes 552968 | tf_op jit(solution)/shard_map/ppermute | solution.py:563
  12.8 5.6 %copy-start.1 = (s32[2,4,128]{2,1,0:T(4,128)S(1)}, s32[2,4,128]{2,1,0:T(4,128)}, u32[]{:S(2)}) copy-start(s32[2,4,128]{2,1,0:T(4,128)} %mask.1) | copy-start | bytes 12292
  12.8 5.6 %copy-start.4 = (bf16[3152,256]{1,0:T(8,128)(2,1)S(1)}, bf16[3152,256]{1,0:T(8,128)(2,1)}, u32[]{:S(2)}) copy-start(bf16[3152,256]{1,0:T(8,128)(2,1)} %constant.16.clone.weights) | copy-start | bytes 4841476
  12.8 5.6 %collective-permute-start.5 = (f32[24,128]{1,0:T(8,128)S(1)}, f32[24,128]{1,0:T(8,128)S(1)}, u32[]{:S(2)}, u32[]{:S(2)}) collective-permute-start(f32[24,128]{1,0:T(8,128)S(1)} %get-tuple-element.29.after), channel_id=1, source_target_pairs={{0,3},{1,0},{2,1},{3,2},{4,7},{5,4},{6,5},{7,6},{8,11},{9,8},{10,9... | collective-permute-start | bytes 36872 | tf_op jit(solution)/shard_map/ppermute | solution.py:563
  18.3 9.8 %copy-start.5 = (bf16[1768,256]{1,0:T(8,128)(2,1)S(1)}, bf16[1768,256]{1,0:T(8,128)(2,1)}, u32[]{:S(2)}) copy-start(bf16[1768,256]{1,0:T(8,128)(2,1)} %constant.17.clone.weights) | copy-start | bytes 2715652
  21.6 6.4 %collective-permute-start.6 = (f32[24,640]{1,0:T(8,128)S(1)}, f32[24,640]{1,0:T(8,128)S(1)}, u32[]{:S(2)}, u32[]{:S(2)}) collective-permute-start(f32[24,640]{1,0:T(8,128)S(1)} %get-tuple-element.33), channel_id=1, source_target_pairs={{0,16},{16,32},{32,48},{48,64},{64,80},{80,96},{96,112},{112,0},{1... | collective-permute-start | bytes 184328 | tf_op jit(solution)/shard_map/ppermute | solution.py:563
  21.7 6.1 %collective-permute-start.7 = (f32[24,128]{1,0:T(8,128)S(1)}, f32[24,128]{1,0:T(8,128)S(1)}, u32[]{:S(2)}, u32[]{:S(2)}) collective-permute-start(f32[24,128]{1,0:T(8,128)S(1)} %get-tuple-element.34), channel_id=1, source_target_pairs={{0,3},{1,0},{2,1},{3,2},{4,7},{5,4},{6,5},{7,6},{8,11},{9,8},{10,9... | collective-permute-start | bytes 36872 | tf_op jit(solution)/shard_map/ppermute | solution.py:563
  23.7 10.5 %collective-permute-start.10 = (f32[16,640]{1,0:T(8,128)S(1)}, f32[16,640]{1,0:T(8,128)S(1)}, u32[]{:S(2)}, u32[]{:S(2)}) collective-permute-start(f32[16,640]{1,0:T(8,128)S(1)} %get-tuple-element.38), channel_id=1, source_target_pairs={{0,12},{4,0},{8,4},{12,8},{1,13},{5,1},{9,5},{13,9},{2,14},{6,2},{... | collective-permute-start | bytes 122888 | tf_op jit(solution)/shard_map/ppermute | solution.py:563
  23.7 10.5 %collective-permute-start.8 = (f32[24,640]{1,0:T(8,128)S(1)}, f32[24,640]{1,0:T(8,128)S(1)}, u32[]{:S(2)}, u32[]{:S(2)}) collective-permute-start(f32[24,640]{1,0:T(8,128)S(1)} %get-tuple-element.36), channel_id=1, source_target_pairs={{0,112},{16,0},{32,16},{48,32},{64,48},{80,64},{96,80},{112,96},{1... | collective-permute-start | bytes 184328 | tf_op jit(solution)/shard_map/ppermute | solution.py:563
  28.0 5.3 %collective-permute-start.9 = (f32[16,640]{1,0:T(8,128)S(1)}, f32[16,640]{1,0:T(8,128)S(1)}, u32[]{:S(2)}, u32[]{:S(2)}) collective-permute-start(f32[16,640]{1,0:T(8,128)S(1)} %pad_add_fusion), channel_id=1, source_target_pairs={{0,4},{4,8},{8,12},{12,0},{1,5},{5,9},{9,13},{13,1},{2,6},{6,10},{... | collective-permute-start | bytes 122888 | tf_op jit(solution)/shard_map/ppermute | solution.py:563
  28.1 5.6 %copy-start.2 = (f32[2,4,128]{2,1,0:T(4,128)S(1)}, f32[2,4,128]{2,1,0:T(4,128)}, u32[]{:S(2)}) copy-start(f32[2,4,128]{2,1,0:T(4,128)} %scale.1) | copy-start | bytes 12292
  28.1 5.6 %copy-start.7 = (bf16[432,256]{1,0:T(8,128)(2,1)S(1)}, bf16[432,256]{1,0:T(8,128)(2,1)}, u32[]{:S(2)}) copy-start(bf16[432,256]{1,0:T(8,128)(2,1)} %constant.18.clone.weights) | copy-start | bytes 663556
  28.1 5.6 %copy-start.8 = (f32[24,640]{1,0:T(8,128)S(1)}, f32[24,640]{1,0:T(8,128)}, u32[]{:S(2)}) copy-start(f32[24,640]{1,0:T(8,128)} %constant.19.clone.modes) | copy-start | bytes 184324
  33.3 5.0 %copy-start.3 = (bf16[3520,256]{1,0:T(8,128)(2,1)S(1)}, bf16[3520,256]{1,0:T(8,128)(2,1)}, u32[]{:S(2)}) copy-start(bf16[3520,256]{1,0:T(8,128)(2,1)} %constant.20.clone.weights) | copy-start | bytes 5406724
  33.3 5.0 %collective-permute-start.11 = (f32[24,128]{1,0:T(8,128)S(1)}, f32[24,128]{1,0:T(8,128)S(1)}, u32[]{:S(2)}, u32[]{:S(2)}) collective-permute-start(f32[24,128]{1,0:T(8,128)S(1)} %pad_add_fusion.1), channel_id=1, source_target_pairs={{0,1},{1,2},{2,3},{3,0},{4,5},{5,6},{6,7},{7,4},{8,9},{9,10},{10,1... | collective-permute-start | bytes 36872 | tf_op jit(solution)/shard_map/ppermute | solution.py:563

commit v4 on v3

--- a/solution.py
+++ b/solution.py
@@ -13,6 +13,7 @@
 LIFT = 10.0
 STEP = 0.05
 PENALTY = 4.0
+LIFT_SCALE = -0.5 * LIFT * STEP
 
 BX, BY, BZ = 10, 20, 640
 EX, EY, EZ = 2, 4, 128
@@ -239,7 +240,13 @@
     return outs
 
 
-def volume_kernel(packed, v, after, weights, conv, V, FH, FL):
+def add_lift(total, a, w, along, face, sign):
+    p = face * jnp.maximum(jnp.abs(a[along]), jnp.abs(w[along]))
+    q = p + sign * w[along]
+    return [total[c] + (p * a[c] - q * w[c]) for c in range(3)]
+
+
+def volume_kernel(packed, v, after, weights, V, conv, FH, FL):
     del after
     for c in range(3):
         for x in range(BX):
@@ -257,7 +264,7 @@
                 FL[f, 2 * PY * q : 2 * PY * (q + 1), dst] = lo
         return carry
 
-    lax.fori_loop(0, TILES, products, 0)
+    lax.fori_loop(0, TILES, products, 0, unroll=True)
 
     for i, (n0, n1, k0, k1) in enumerate(WINDOWS):
         high = FH[2:5, :, k0:k1].reshape(3 * ROWS, k1 - k0)
@@ -282,71 +289,92 @@
                     conv[c, 5 * e + i, :, dst] = conv[c, 5 * e + i, :, dst] + total
         return carry
 
-    lax.fori_loop(0, TILES, along_x, 0)
-
-
-def lift_kernel(
-    packed, v, conv, hx_lo, hx_hi, hy_lo, hy_hi, hz_lo, hz_hi, mask, weights,
-    prov, PH, PL, xp, xm, yp, ym, zp, zm, own, V,
-):
-    for c in range(3):
-        V[c, 0, :, 128:768] = hx_lo[c]
-        V[c, BX + 1, :, 128:768] = hx_hi[c]
-        for x in range(BX):
-            r = BX * c + x
-            V[c, x + 1, 0:BY, 128:768] = v[c, x]
-            V[c, x + 1, 20:22, 128:768] = jnp.broadcast_to(hy_hi[r : r + 1, :], (2, BZ))
-            V[c, x + 1, 22:24, 128:768] = jnp.broadcast_to(hy_lo[r : r + 1, :], (2, BZ))
-            k = 16 * c + x
-            V[c, x + 1, :, 0:128] = jnp.broadcast_to(hz_lo[:, k : k + 1], (PY, 128))
-            V[c, x + 1, :, 768:896] = jnp.broadcast_to(hz_hi[:, k : k + 1], (PY, 128))
-
-    solid = spread_out(packed, weights, [mask[...].astype(F32).reshape(8, EZ).astype(BF16)])
-    solid = jnp.concatenate(solid, axis=1)
-    conv_scale = -0.5 * LIFT * STEP
+    lax.fori_loop(0, TILES, along_x, 0, unroll=True)
+
     lane = lax.broadcasted_iota(jnp.int32, (PY, 128), 1)
     row = lax.broadcasted_iota(jnp.int32, (PY, 128), 0)
-    row_left = (lax.rem(row, 5) == 0) & (row < BY)
-    row_right = (lax.rem(row, 5) == 4) & (row < BY)
-    y_face = jnp.where(row_left | row_right, conv_scale, 0.0)
-    y_sign = jnp.where(row_left, conv_scale, jnp.where(row_right, -conv_scale, 0.0))
-    damp = [1.0 / (1.0 + PENALTY * solid[PY * e : PY * (e + 1)]) for e in range(EX)]
+    row_left = (lax.rem(row, 5) == 0) & (row > 0) & (row < BY)
+    row_right = (lax.rem(row, 5) == 4) & (row < BY - 1)
+    y_face = jnp.where(row_left | row_right, LIFT_SCALE, 0.0)
+    y_sign = jnp.where(row_left, LIFT_SCALE, jnp.where(row_right, -LIFT_SCALE, 0.0))
     for t in range(TILES):
-        point = lax.rem(lane + 128 * t, 5)
-        z_left = point == 0
-        z_face = jnp.where(z_left | (point == 4), conv_scale, 0.0)
-        z_sign = jnp.where(z_left, conv_scale, jnp.where(point == 4, -conv_scale, 0.0))
-        here = slice(128 + 128 * t, 256 + 128 * t)
-        before = slice(128 * t, 128 + 128 * t)
-        after = slice(256 + 128 * t, 384 + 128 * t)
-        out = slice(128 * t, 128 + 128 * t)
+        node = lane + 128 * t
+        z_left = (lax.rem(node, 5) == 0) & (node > 0)
+        z_right = (lax.rem(node, 5) == 4) & (node < BZ - 1)
+        z_face = jnp.where(z_left | z_right, LIFT_SCALE, 0.0)
+        z_sign = jnp.where(z_left, LIFT_SCALE, jnp.where(z_right, -LIFT_SCALE, 0.0))
+        here = slice(128 * t, 128 + 128 * t)
+        before = slice(128 * t - 128, 128 * t)
+        after = slice(128 + 128 * t, 256 + 128 * t)
         for x in range(BX):
-            a = [V[c, x + 1, :, here] for c in range(3)]
-            total = [conv[c, x, :, out] for c in range(3)]
+            a = [V[c, x, :, here] for c in range(3)]
+            total = [conv[c, x, :, here] for c in range(3)]
             w = []
             for c in range(3):
-                lo = pltpu.roll(jnp.where(lane == 127, V[c, x + 1, :, before], a[c]), 1, 1)
-                hi = pltpu.roll(jnp.where(lane == 0, V[c, x + 1, :, after], a[c]), 127, 1)
-                w.append(jnp.where(z_left, lo, hi))
-            p = z_face * jnp.maximum(jnp.abs(a[2]), jnp.abs(w[2]))
-            q = p + z_sign * w[2]
-            total = [total[c] + (p * a[c] - q * w[c]) for c in range(3)]
+                lo, hi = a[c], a[c]
+                if t > 0:
+                    lo = jnp.where(lane == 127, V[c, x, :, before], lo)
+                if t < TILES - 1:
+                    hi = jnp.where(lane == 0, V[c, x, :, after], hi)
+                w.append(jnp.where(z_left, pltpu.roll(lo, 1, 1), pltpu.roll(hi, 127, 1)))
+            total = add_lift(total, a, w, 2, z_face, z_sign)
             w = [
                 jnp.where(row_left, pltpu.roll(a[c], 1, 0), pltpu.roll(a[c], PY - 1, 0))
                 for c in range(3)
             ]
-            p = y_face * jnp.maximum(jnp.abs(a[1]), jnp.abs(w[1]))
-            q = p + y_sign * w[1]
-            total = [total[c] + (p * a[c] - q * w[c]) for c in range(3)]
-            if x % 5 in (0, 4):
-                sign = 1.0 if x % 5 == 0 else -1.0
-                w = [V[c, x if x % 5 == 0 else x + 2, :, here] for c in range(3)]
-                p = conv_scale * jnp.maximum(jnp.abs(a[0]), jnp.abs(w[0]))
-                q = p + (sign * conv_scale) * w[0]
-                total = [total[c] + (p * a[c] - q * w[c]) for c in range(3)]
-            factor = damp[x // 5][:, out]
+            total = add_lift(total, a, w, 1, y_face, y_sign)
+            if x in (4, 5):
+                sign = -1.0 if x == 4 else 1.0
+                w = [V[c, 9 - x, :, here] for c in range(3)]
+                total = add_lift(total, a, w, 0, LIFT_SCALE, sign * LIFT_SCALE)
             for c in range(3):
-                prov[c, x, :, out] = (a[c] + total[c]) * factor
+                conv[c, x, :, here] = total[c]
+
+
+def lift_kernel(
+    packed, V, conv, hx_lo, hx_hi, hy_lo, hy_hi, hz_lo, hz_hi, mask, weights,
+    prov, PH, PL, xp, xm, yp, ym, zp, zm, own,
+):
+    solid = spread_out(packed, weights, [mask[...].astype(F32).reshape(8, EZ).astype(BF16)])
+    solid = jnp.concatenate(solid, axis=1)
+    lane = lax.broadcasted_iota(jnp.int32, (PY, 128), 1)
+    row8 = lax.broadcasted_iota(jnp.int32, (8, 128), 0)
+    first_lane = jnp.where(lane == 0, LIFT_SCALE, 0.0)
+    last_lane = jnp.where(lane == 127, LIFT_SCALE, 0.0)
+    first_row = jnp.where(row8 == 0, LIFT_SCALE, 0.0)
+    last_row = jnp.where(row8 == BY - 17, LIFT_SCALE, 0.0)
+    damp = [1.0 / (1.0 + PENALTY * solid[PY * e : PY * (e + 1)]) for e in range(EX)]
+    for t in range(TILES):
+        here = slice(128 * t, 128 + 128 * t)
+        for x in range(BX):
+            a = [V[c, x, :, here] for c in range(3)]
+            total = [conv[c, x, :, here] for c in range(3)]
+            if t in (0, TILES - 1):
+                edge = hz_lo if t == 0 else hz_hi
+                w = [
+                    jnp.broadcast_to(edge[:, 16 * c + x : 16 * c + x + 1], (PY, 128))
+                    for c in range(3)
+                ]
+                face = first_lane if t == 0 else last_lane
+                total = add_lift(total, a, w, 2, face, face if t == 0 else -face)
+            if x in (0, BX - 1):
+                w = [(hx_lo if x == 0 else hx_hi)[c, :, here] for c in range(3)]
+                sign = 1.0 if x == 0 else -1.0
+                total = add_lift(total, a, w, 0, LIFT_SCALE, sign * LIFT_SCALE)
+            factor = damp[x // 5][:, here]
+            done = [(a[c] + total[c]) * factor for c in range(3)]
+            for c in range(3):
+                prov[c, x, 8:16, here] = done[c][8:16]
+            for r0, edge, face, sign in ((0, hy_lo, first_row, first_row), (16, hy_hi, last_row, -last_row)):
+                w = [
+                    jnp.broadcast_to(edge[BX * c + x : BX * c + x + 1, here], (8, 128))
+                    for c in range(3)
+                ]
+                rows = slice(r0, r0 + 8)
+                zero = [jnp.zeros((8, 128), F32)] * 3
+                more = add_lift(zero, [part[rows] for part in a], w, 1, face, sign)
+                for c in range(3):
+                    prov[c, x, rows, here] = done[c][rows] + more[c] * factor[rows]
 
     for q in range(BX // 2):
         for c in range(3):
@@ -419,7 +447,7 @@
             rhs[x, :, dst] = rhs[x, :, dst] + outs[x]
         return carry
 
-    lax.fori_loop(0, TILES, right_x, 0)
+    lax.fori_loop(0, TILES, right_x, 0, unroll=True)
 
 
 def spread_out(packed, weights, parts):
@@ -608,11 +636,11 @@
     halo.append(shift(last, "gz", -1))
     field = like(3, BX, PY, BZ)
     half = jax.ShapeDtypeStruct((3, ROWS, BZ), BF16)
-    (conv,) = run(
+    v, conv = run(
         functools.partial(volume_kernel, volume),
-        [field],
+        [field, field],
         [velocity, faces[2], volume.array()],
-        scratch=[pltpu.VMEM((3, BX, PY, BZ), F32)] + [pltpu.VMEM((5, ROWS, BZ), BF16)] * 2,
+        scratch=[pltpu.VMEM((5, ROWS, BZ), BF16)] * 2,
         name="volume",
         flops=4 * 10**9,
     )
@@ -621,8 +649,7 @@
         [field, half, half]
         + [like(PY, BZ), like(PY, BZ), like(16, BZ), like(16, BZ), like(PY, 128), like(PY, 128)]
         + [like(16, 128)],
-        [velocity, conv, *halo, obstacle_element_mask, lift.array()],
-        scratch=[pltpu.VMEM((3, BX + 2, PY, 896), F32)],
+        [v, conv, *halo, obstacle_element_mask, lift.array()],
         name="lift",
         flops=4 * 10**9,
     )

time: 41.1 us -> 40.2 us (0.978)
  Pallas kernels: 11 us -> 10 us
    pallas_call x7, Pallas kernels: 11 us -> 10 us  [run(): pl.pallas_call(kernel, out_shape=outs, in_specs=[vmem] * len(operands), o...]
  transfers between devices with their start and end apart: 12 -> 12, of which waited for: 3 -> 3; matrix products, arithmetic and copies ran while one was open for 0% -> 0% of each run, Pallas kernels for 13% -> 14%
where the time goes in v4:
time: 40.2 us; the launch traced here: 40.1 us
  starting transfers between devices  19.4 us (48%)
  Pallas kernels  10 us (25%)
  waiting for transfers between devices  8.68 us (22%)
  local copies, waits for them, and re-layouts  1.11 us (3%)
  between operations  0.83 us (2%)
    ppermute x12, starting transfers between devices, shift(): return lax.ppermute(x, axis, [(i, (i + by) % size) for i in range(size)])  19.4 us
    pallas_call x7, Pallas kernels, run(): pl.pallas_call(kernel, out_shape=outs, in_specs=[vmem] * len(operands), o...  10 us
    ppermute x12, waiting for transfers between devices, shift(): return lax.ppermute(x, axis, [(i, (i + by) % size) for i in range(size)])  8.68 us
    squeeze x1, local copies, waits for them, and re-layouts, shards(): velocity[:, BX - 1]  1.05 us
  transfers between devices with their start and end apart: 12, of which 3 were waited for; matrix products, arithmetic and copies ran while one was open for 0% of the time, Pallas kernels for 14%

profile of v4, /device:TPU:0, one launch (start us, length us, event | category | flops | bytes accessed | tf_op | source)
XLA Modules:
  0.0 40.1 jit_solution(11232537807716616220)
XLA Ops:
  0.6 1.0 %slice_bitcast_fusion = (f32[3,20,640]{2,1,0:T(8,128)S(1)}, f32[3,20,640]{2,1,0:T(8,128)S(1)}) fusion(f32[3,10,20,640]{3,2,1,0:T(8,128)} %v.3), kind=kLoop, calls=%fused_computation | loop fusion | bytes 614400 | tf_op jit(solution)/shard_map/squeeze | solution.py:617
  1.7 0.0 copy-start
  1.7 0.0 copy-start.6
  1.7 1.7 %collective-permute-start = (f32[3,24,640]{2,1,0:T(8,128)S(1)}, f32[3,24,640]{2,1,0:T(8,128)S(1)}, u32[]{:S(2)}, u32[]{:S(2)}) collective-permute-start(f32[3,24,640]{2,1,0:T(8,128)S(1)} %get-tuple-element.27), channel_id=1, source_target_pairs={{0,16},{16,32},{32,48},{48,64},{64,80},{80,96},{96,112},{112,0},{1... | collective-permute-start | bytes 552968 | tf_op jit(solution)/shard_map/ppermute | solution.py:591
  3.5 0.0 copy-done
  3.5 0.4 pack.1
  3.9 2.0 %collective-permute-start.4 = (f32[24,128]{1,0:T(8,128)S(1)}, f32[24,128]{1,0:T(8,128)S(1)}, u32[]{:S(2)}, u32[]{:S(2)}) collective-permute-start(f32[24,128]{1,0:T(8,128)S(1)} %get-tuple-element.32), channel_id=1, source_target_pairs={{0,1},{1,2},{2,3},{3,0},{4,5},{5,6},{6,7},{7,4},{8,9},{9,10},{10,1... | collective-permute-start | bytes 36872 | tf_op jit(solution)/shard_map/ppermute | solution.py:591
  5.8 0.0 collective-permute-start.2
  5.8 3.2 %collective-permute-start.3 = (f32[30,640]{1,0:T(8,128)S(1)}, f32[30,640]{1,0:T(8,128)S(1)}, u32[]{:S(2)}, u32[]{:S(2)}) collective-permute-start(f32[30,640]{1,0:T(8,128)S(1)} %get-tuple-element.31), channel_id=1, source_target_pairs={{0,12},{4,0},{8,4},{12,8},{1,13},{5,1},{9,5},{13,9},{2,14},{6,2},{... | collective-permute-start | bytes 230408 | tf_op jit(solution)/shard_map/ppermute | solution.py:591
  9.1 3.7 %collective-permute-start.1 = (f32[3,24,640]{2,1,0:T(8,128)S(1)}, f32[3,24,640]{2,1,0:T(8,128)S(1)}, u32[]{:S(2)}, u32[]{:S(2)}) collective-permute-start(f32[3,24,640]{2,1,0:T(8,128)S(1)} %get-tuple-element.29), channel_id=1, source_target_pairs={{0,112},{16,0},{32,16},{48,32},{64,48},{80,64},{96,80},{112,96},{1... | collective-permute-start | bytes 552968 | tf_op jit(solution)/shard_map/ppermute | solution.py:591
  12.8 0.0 collective-permute-done.hx_lo
  12.8 0.0 copy-start.1
  12.8 0.0 copy-start.4
  12.8 2.2 %collective-permute-start.5 = (f32[24,128]{1,0:T(8,128)S(1)}, f32[24,128]{1,0:T(8,128)S(1)}, u32[]{:S(2)}, u32[]{:S(2)}) collective-permute-start(f32[24,128]{1,0:T(8,128)S(1)} %get-tuple-element.33.after), channel_id=1, source_target_pairs={{0,3},{1,0},{2,1},{3,2},{4,7},{5,4},{6,5},{7,6},{8,11},{9,8},{10,9... | collective-permute-start | bytes 36872 | tf_op jit(solution)/shard_map/ppermute | solution.py:591
  15.0 0.0 copy-done.6
  15.0 3.9 %volume.1 = (f32[3,10,24,640]{3,2,1,0:T(8,128)S(1)}, f32[3,10,24,640]{3,2,1,0:T(8,128)S(1)}) custom-call(f32[3,10,20,640]{3,2,1,0:T(8,128)S(1)} %copy-done, f32[24,128]{1,0:T(8,128)S(1)} %get-tuple-element.33.after, bf16[1768,256]{1,0:T(8,128)(2,1)S(1)} %copy-done.6), custom_call_target="tpu_custom_call" | custom-call | flops 4000000000 | bytes 4194304 | tf_op jit(solution)/shard_map/volume/pallas_call | solution.py:600
  18.9 0.0 collective-permute-done.4.hz_lo
  18.9 0.0 collective-permute-done.2.hy_lo
  19.0 0.0 collective-permute-done.3.hy_hi
  19.0 0.0 collective-permute-done.1.hx_hi
  19.0 0.0 collective-permute-done.5.hz_hi
  19.0 0.0 copy-done.1
  19.0 0.0 copy-done.4
  19.0 0.0 copy-start.5
  19.0 1.8 %lift.1 = (f32[3,10,24,640]{3,2,1,0:T(8,128)S(1)}, bf16[3,240,640]{2,1,0:T(8,128)(2,1)S(1)}, bf16[3,240,640]{2,1,0:T(8,128)(2,1)S(1)}, f32[24,640]{1,0:T(8,128)S...) custom-call(f32[3,10,24,640]{3,2,1,0:T(8,128)S(1)} %get-tuple-elemen, ...), custom_call_target="tpu_custom_call" | custom-call | flops 4000000000 | bytes 4194304 | tf_op jit(solution)/shard_map/lift/pallas_call | solution.py:600
  20.8 0.0 collective-permute-start.6
  20.8 2.0 %collective-permute-start.7 = (f32[24,128]{1,0:T(8,128)S(1)}, f32[24,128]{1,0:T(8,128)S(1)}, u32[]{:S(2)}, u32[]{:S(2)}) collective-permute-start(f32[24,128]{1,0:T(8,128)S(1)} %get-tuple-element.38), channel_id=1, source_target_pairs={{0,3},{1,0},{2,1},{3,2},{4,7},{5,4},{6,5},{7,6},{8,11},{9,8},{10,9... | collective-permute-start | bytes 36872 | tf_op jit(solution)/shard_map/ppermute | solution.py:591
  22.8 0.0 collective-permute-start.10
  22.8 4.1 %collective-permute-start.8 = (f32[24,640]{1,0:T(8,128)S(1)}, f32[24,640]{1,0:T(8,128)S(1)}, u32[]{:S(2)}, u32[]{:S(2)}) collective-permute-start(f32[24,640]{1,0:T(8,128)S(1)} %get-tuple-element.40), channel_id=1, source_target_pairs={{0,112},{16,0},{32,16},{48,32},{64,48},{80,64},{96,80},{112,96},{1... | collective-permute-start | bytes 184328 | tf_op jit(solution)/shard_map/ppermute | solution.py:591
  26.9 0.0 collective-permute-done.7.hz_hi
  26.9 0.2 collective-permute-done.6.hx_lo
  27.2 0.1 collective-permute-start.9
  27.2 0.0 copy-done.5
  27.3 0.0 copy-start.2
  27.3 0.0 copy-start.7
  27.3 0.0 copy-start.8
  27.3 0.8 %right.1.rhs = f32[10,24,640]{2,1,0:T(8,128)S(1)} custom-call(f32[3,10,24,640]{3,2,1,0:T(8,128)S(1)} %get-tuple-element.34.prov, bf16[3,240,640]{2,1,0:T(8,128)(2,1)S(1)} %get-tuple-element.35.PH, bf16[3,240,640]{2,1,0:T(8,128)(2,1)S(1)} %get-tuple-element.36.PL, bf16[1768,256]{1,0:T(8,128)(2,1)S(1)} %copy-done.5), custom_call_target="tpu_custom_call" | custom-call | flops 2000000000 | bytes 4194304 | tf_op jit(solution)/shard_map/right/pallas_call | solution.py:600
  28.1 4.4 %collective-permute-done.9.after.hy_lo = f32[16,640]{1,0:T(8,128)S(1)} collective-permute-done((f32[16,640]{1,0:T(8,128)S(1)}, f32[16,640]{1,0:T(8,128)S(1)}, u32[]{:S(2)}, u32[]{:S(2)}) %collective-permute-start.9) | collective-permute-done | bytes 40992 | tf_op jit(solution)/shard_map/ppermute | solution.py:591
  32.5 0.0 copy-start.3
  32.5 0.4 collective-permute-start.11
  32.8 0.0 copy-done.2
  32.8 0.0 copy-done.7
  32.8 0.0 copy-done.8
  32.8 0.5 %divisor.1.inverse = f32[10,24,768]{2,1,0:T(8,128)S(1)} custom-call(f32[2,4,128]{2,1,0:T(4,128)S(1)} %copy-done.2, f32[16,640]{1,0:T(8,128)S(1)} %collective-permute-done.9.after.hy_lo, bf16[432,256]{1,0:T(8,128)(2,1)S(1)} %copy-done.7, f32[24,640]{1,0:T(8,128)S(1)} %copy-done.8), custom_call_target="tpu_custom_call" | custom-call | flops 2000000000 | bytes 4194304 | tf_op jit(solution)/shard_map/divisor/pallas_call | solution.py:600
  33.4 0.0 collective-permute-done.10.hy_hi
  33.4 0.0 collective-permute-done.8.hx_hi
  33.4 4.1 %collective-permute-done.11.hz_lo = f32[24,128]{1,0:T(8,128)S(1)} collective-permute-done((f32[24,128]{1,0:T(8,128)S(1)}, f32[24,128]{1,0:T(8,128)S(1)}, u32[]{:S(2)}, u32[]{:S(2)}) %collective-permute-start.11) | collective-permute-done | bytes 12320 | tf_op jit(solution)/shard_map/ppermute | solution.py:591
  37.5 0.0 copy-done.3
  37.5 2.6 %smooth.1 = (f32[10,20,640]{2,1,0:T(8,128)}, f32[2,4,128]{2,1,0:T(4,128)}) custom-call(f32[10,24,640]{2,1,0:T(8,128)S(1)} %right.1.rhs, f32[24,640]{1,0:T(8,128)S(1)} %collective-permute-done.6.hx_lo, f32[24,640]{1,0:T(8,128)S(1)} %collective-permute-done.8.hx_hi, f32[16,640]{1,0:T(8,128)S(1)} %collective-permute-done.9.after.hy_lo, ...), custom_call_target="tpu_custom_call" | custom-call | flops 3000000000 | bytes 4194304 | tf_op jit(solution)/shard_map/smooth/pallas_call | solution.py:600
  (6 shorter events, 0.1 us)
Async XLA Ops:
  1.7 1.8 %copy-start = (f32[3,10,20,640]{3,2,1,0:T(8,128)S(1)}, f32[3,10,20,640]{3,2,1,0:T(8,128)}, u32[]{:S(2)}) copy-start(f32[3,10,20,640]{3,2,1,0:T(8,128)} %v.3) | copy-start | bytes 4608004
  1.7 13.3 %copy-start.6 = (bf16[1768,256]{1,0:T(8,128)(2,1)S(1)}, bf16[1768,256]{1,0:T(8,128)(2,1)}, u32[]{:S(2)}) copy-start(bf16[1768,256]{1,0:T(8,128)(2,1)} %constant.15.clone.weights) | copy-start | bytes 2715652
  1.7 11.1 %collective-permute-start = (f32[3,24,640]{2,1,0:T(8,128)S(1)}, f32[3,24,640]{2,1,0:T(8,128)S(1)}, u32[]{:S(2)}, u32[]{:S(2)}) collective-permute-start(f32[3,24,640]{2,1,0:T(8,128)S(1)} %get-tuple-element.27), channel_id=1, source_target_pairs={{0,16},{16,32},{32,48},{48,64},{64,80},{80,96},{96,112},{112,0},{1... | collective-permute-start | bytes 552968 | tf_op jit(solution)/shard_map/ppermute | solution.py:591
  3.9 15.1 %collective-permute-start.4 = (f32[24,128]{1,0:T(8,128)S(1)}, f32[24,128]{1,0:T(8,128)S(1)}, u32[]{:S(2)}, u32[]{:S(2)}) collective-permute-start(f32[24,128]{1,0:T(8,128)S(1)} %get-tuple-element.32), channel_id=1, source_target_pairs={{0,1},{1,2},{2,3},{3,0},{4,5},{5,6},{6,7},{7,4},{8,9},{9,10},{10,1... | collective-permute-start | bytes 36872 | tf_op jit(solution)/shard_map/ppermute | solution.py:591
  5.8 13.1 %collective-permute-start.2 = (f32[30,640]{1,0:T(8,128)S(1)}, f32[30,640]{1,0:T(8,128)S(1)}, u32[]{:S(2)}, u32[]{:S(2)}) collective-permute-start(f32[30,640]{1,0:T(8,128)S(1)} %get-tuple-element.30), channel_id=1, source_target_pairs={{0,4},{4,8},{8,12},{12,0},{1,5},{5,9},{9,13},{13,1},{2,6},{6,10},{... | collective-permute-start | bytes 230408 | tf_op jit(solution)/shard_map/ppermute | solution.py:591
  5.8 13.1 %collective-permute-start.3 = (f32[30,640]{1,0:T(8,128)S(1)}, f32[30,640]{1,0:T(8,128)S(1)}, u32[]{:S(2)}, u32[]{:S(2)}) collective-permute-start(f32[30,640]{1,0:T(8,128)S(1)} %get-tuple-element.31), channel_id=1, source_target_pairs={{0,12},{4,0},{8,4},{12,8},{1,13},{5,1},{9,5},{13,9},{2,14},{6,2},{... | collective-permute-start | bytes 230408 | tf_op jit(solution)/shard_map/ppermute | solution.py:591
  9.1 9.9 %collective-permute-start.1 = (f32[3,24,640]{2,1,0:T(8,128)S(1)}, f32[3,24,640]{2,1,0:T(8,128)S(1)}, u32[]{:S(2)}, u32[]{:S(2)}) collective-permute-start(f32[3,24,640]{2,1,0:T(8,128)S(1)} %get-tuple-element.29), channel_id=1, source_target_pairs={{0,112},{16,0},{32,16},{48,32},{64,48},{80,64},{96,80},{112,96},{1... | collective-permute-start | bytes 552968 | tf_op jit(solution)/shard_map/ppermute | solution.py:591
  12.8 6.2 %copy-start.1 = (s32[2,4,128]{2,1,0:T(4,128)S(1)}, s32[2,4,128]{2,1,0:T(4,128)}, u32[]{:S(2)}) copy-start(s32[2,4,128]{2,1,0:T(4,128)} %mask.1) | copy-start | bytes 12292
  12.8 6.2 %copy-start.4 = (bf16[3152,256]{1,0:T(8,128)(2,1)S(1)}, bf16[3152,256]{1,0:T(8,128)(2,1)}, u32[]{:S(2)}) copy-start(bf16[3152,256]{1,0:T(8,128)(2,1)} %constant.16.clone.weights) | copy-start | bytes 4841476
  12.8 6.2 %collective-permute-start.5 = (f32[24,128]{1,0:T(8,128)S(1)}, f32[24,128]{1,0:T(8,128)S(1)}, u32[]{:S(2)}, u32[]{:S(2)}) collective-permute-start(f32[24,128]{1,0:T(8,128)S(1)} %get-tuple-element.33.after), channel_id=1, source_target_pairs={{0,3},{1,0},{2,1},{3,2},{4,7},{5,4},{6,5},{7,6},{8,11},{9,8},{10,9... | collective-permute-start | bytes 36872 | tf_op jit(solution)/shard_map/ppermute | solution.py:591
  19.0 8.2 %copy-start.5 = (bf16[1768,256]{1,0:T(8,128)(2,1)S(1)}, bf16[1768,256]{1,0:T(8,128)(2,1)}, u32[]{:S(2)}) copy-start(bf16[1768,256]{1,0:T(8,128)(2,1)} %constant.17.clone.weights) | copy-start | bytes 2715652
  20.8 6.4 %collective-permute-start.6 = (f32[24,640]{1,0:T(8,128)S(1)}, f32[24,640]{1,0:T(8,128)S(1)}, u32[]{:S(2)}, u32[]{:S(2)}) collective-permute-start(f32[24,640]{1,0:T(8,128)S(1)} %get-tuple-element.37), channel_id=1, source_target_pairs={{0,16},{16,32},{32,48},{48,64},{64,80},{80,96},{96,112},{112,0},{1... | collective-permute-start | bytes 184328 | tf_op jit(solution)/shard_map/ppermute | solution.py:591
  20.8 6.1 %collective-permute-start.7 = (f32[24,128]{1,0:T(8,128)S(1)}, f32[24,128]{1,0:T(8,128)S(1)}, u32[]{:S(2)}, u32[]{:S(2)}) collective-permute-start(f32[24,128]{1,0:T(8,128)S(1)} %get-tuple-element.38), channel_id=1, source_target_pairs={{0,3},{1,0},{2,1},{3,2},{4,7},{5,4},{6,5},{7,6},{8,11},{9,8},{10,9... | collective-permute-start | bytes 36872 | tf_op jit(solution)/shard_map/ppermute | solution.py:591
  22.8 10.5 %collective-permute-start.10 = (f32[16,640]{1,0:T(8,128)S(1)}, f32[16,640]{1,0:T(8,128)S(1)}, u32[]{:S(2)}, u32[]{:S(2)}) collective-permute-start(f32[16,640]{1,0:T(8,128)S(1)} %get-tuple-element.42), channel_id=1, source_target_pairs={{0,12},{4,0},{8,4},{12,8},{1,13},{5,1},{9,5},{13,9},{2,14},{6,2},{... | collective-permute-start | bytes 122888 | tf_op jit(solution)/shard_map/ppermute | solution.py:591
  22.8 10.5 %collective-permute-start.8 = (f32[24,640]{1,0:T(8,128)S(1)}, f32[24,640]{1,0:T(8,128)S(1)}, u32[]{:S(2)}, u32[]{:S(2)}) collective-permute-start(f32[24,640]{1,0:T(8,128)S(1)} %get-tuple-element.40), channel_id=1, source_target_pairs={{0,112},{16,0},{32,16},{48,32},{64,48},{80,64},{96,80},{112,96},{1... | collective-permute-start | bytes 184328 | tf_op jit(solution)/shard_map/ppermute | solution.py:591
  27.2 5.3 %collective-permute-start.9 = (f32[16,640]{1,0:T(8,128)S(1)}, f32[16,640]{1,0:T(8,128)S(1)}, u32[]{:S(2)}, u32[]{:S(2)}) collective-permute-start(f32[16,640]{1,0:T(8,128)S(1)} %pad_add_fusion), channel_id=1, source_target_pairs={{0,4},{4,8},{8,12},{12,0},{1,5},{5,9},{9,13},{13,1},{2,6},{6,10},{... | collective-permute-start | bytes 122888 | tf_op jit(solution)/shard_map/ppermute | solution.py:591
  27.3 5.6 %copy-start.2 = (f32[2,4,128]{2,1,0:T(4,128)S(1)}, f32[2,4,128]{2,1,0:T(4,128)}, u32[]{:S(2)}) copy-start(f32[2,4,128]{2,1,0:T(4,128)} %scale.1) | copy-start | bytes 12292
  27.3 5.6 %copy-start.7 = (bf16[432,256]{1,0:T(8,128)(2,1)S(1)}, bf16[432,256]{1,0:T(8,128)(2,1)}, u32[]{:S(2)}) copy-start(bf16[432,256]{1,0:T(8,128)(2,1)} %constant.18.clone.weights) | copy-start | bytes 663556
  27.3 5.6 %copy-start.8 = (f32[24,640]{1,0:T(8,128)S(1)}, f32[24,640]{1,0:T(8,128)}, u32[]{:S(2)}) copy-start(f32[24,640]{1,0:T(8,128)} %constant.19.clone.modes) | copy-start | bytes 184324
  32.5 5.0 %copy-start.3 = (bf16[3520,256]{1,0:T(8,128)(2,1)S(1)}, bf16[3520,256]{1,0:T(8,128)(2,1)}, u32[]{:S(2)}) copy-start(bf16[3520,256]{1,0:T(8,128)(2,1)} %constant.20.clone.weights) | copy-start | bytes 5406724
  32.5 5.0 %collective-permute-start.11 = (f32[24,128]{1,0:T(8,128)S(1)}, f32[24,128]{1,0:T(8,128)S(1)}, u32[]{:S(2)}, u32[]{:S(2)}) collective-permute-start(f32[24,128]{1,0:T(8,128)S(1)} %pad_add_fusion.1), channel_id=1, source_target_pairs={{0,1},{1,2},{2,3},{3,0},{4,5},{5,6},{6,7},{7,4},{8,9},{9,10},{10,1... | collective-permute-start | bytes 36872 | tf_op jit(solution)/shard_map/ppermute | solution.py:591

commit v5 on v4

--- a/solution.py
+++ b/solution.py
@@ -253,8 +253,8 @@
             V[c, x, 0:BY, :] = v[c, x]
             V[c, x, BY:PY, :] = jnp.zeros((PY - BY, BZ), F32)
 
-    def products(t, carry):
-        dst = pl.ds(pl.multiple_of(128 * t, 128), 128)
+    def products(t):
+        dst = slice(128 * t, 128 * t + 128)
         for q in range(BX // 2):
             a = [V[c, 2 * q : 2 * q + 2, :, dst].reshape(2 * PY, 128) for c in range(3)]
             pairs = (a[0] * a[1], a[1] * a[1], a[1] * a[2], a[0] * a[2], a[2] * a[2])
@@ -262,34 +262,31 @@
                 hi, lo = split(value)
                 FH[f, 2 * PY * q : 2 * PY * (q + 1), dst] = hi
                 FL[f, 2 * PY * q : 2 * PY * (q + 1), dst] = lo
-        return carry
-
-    lax.fori_loop(0, TILES, products, 0, unroll=True)
-
-    for i, (n0, n1, k0, k1) in enumerate(WINDOWS):
+
+    def along_z(i):
+        n0, n1, k0, k1 = WINDOWS[i]
         high = FH[2:5, :, k0:k1].reshape(3 * ROWS, k1 - k0)
         low = FL[2:5, :, k0:k1].reshape(3 * ROWS, k1 - k0)
         z = right_dot(high, low, packed.get(weights, "bz" + str(i)))
         for c in range(3):
-            along_z = ROWS * (1, 0, 2)[c]
-            conv[c, :, :, n0:n1] = z[along_z : along_z + ROWS].reshape(BX, PY, n1 - n0)
+            place = ROWS * (1, 0, 2)[c]
+            conv[c, :, :, n0:n1] = z[place : place + ROWS].reshape(BX, PY, n1 - n0)
     my = packed.both(weights, "my")
-    for n0, n1 in LANES:
-        for c in range(3):
-            y = left_dot(my, FH[c, :, n0:n1], FL[c, :, n0:n1]).reshape(BX, PY, n1 - n0)
-            conv[c, :, :, n0:n1] = conv[c, :, :, n0:n1] + y
-
-    def along_x(t, carry):
-        dst = pl.ds(pl.multiple_of(128 * t, 128), 128)
+
+    def along_y(i, c):
+        n0, n1 = LANES[i]
+        y = left_dot(my, FH[c, :, n0:n1], FL[c, :, n0:n1]).reshape(BX, PY, n1 - n0)
+        conv[c, :, :, n0:n1] = conv[c, :, :, n0:n1] + y
+
+    def along_x(t):
+        dst = slice(128 * t, 128 * t + 128)
         for e in range(EX):
             v0 = [V[0, 5 * e + i, :, dst] for i in range(5)]
             for c in range(3):
                 flux = [v0[i] * V[c, 5 * e + i, :, dst] for i in range(5)]
                 for i, total in enumerate(plane_sums(flux, -STEP)):
                     conv[c, 5 * e + i, :, dst] = conv[c, 5 * e + i, :, dst] + total
-        return carry
-
-    lax.fori_loop(0, TILES, along_x, 0, unroll=True)
+
 
     lane = lax.broadcasted_iota(jnp.int32, (PY, 128), 1)
     row = lax.broadcasted_iota(jnp.int32, (PY, 128), 0)
@@ -297,7 +294,8 @@
     row_right = (lax.rem(row, 5) == 4) & (row < BY - 1)
     y_face = jnp.where(row_left | row_right, LIFT_SCALE, 0.0)
     y_sign = jnp.where(row_left, LIFT_SCALE, jnp.where(row_right, -LIFT_SCALE, 0.0))
-    for t in range(TILES):
+
+    def inner_lifts(t):
         node = lane + 128 * t
         z_left = (lax.rem(node, 5) == 0) & (node > 0)
         z_right = (lax.rem(node, 5) == 4) & (node < BZ - 1)
@@ -329,6 +327,16 @@
                 total = add_lift(total, a, w, 0, LIFT_SCALE, sign * LIFT_SCALE)
             for c in range(3):
                 conv[c, x, :, here] = total[c]
+
+    for t in range(TILES):
+        products(t)
+        if t in (1, 3, 4):
+            along_z((1, 3, 4).index(t))
+    for t in range(TILES):
+        inner_lifts(t)
+        for job in range(2 * t, min(2 * t + 2, 9)):
+            along_y(job // 3, job % 3)
+        along_x(t)
 
 
 def lift_kernel(

time: 40.2 us -> 40.1 us (level)
  no operation moved by 1% of the time
where the time goes in v5:
time: 40.1 us; the launch traced here: 40 us
  starting transfers between devices  19.4 us (48%)
  Pallas kernels  9.96 us (25%)
  waiting for transfers between devices  8.68 us (22%)
  local copies, waits for them, and re-layouts  1.11 us (3%)
  between operations  0.83 us (2%)
    ppermute x12, starting transfers between devices, shift(): return lax.ppermute(x, axis, [(i, (i + by) % size) for i in range(size)])  19.4 us
    pallas_call x7, Pallas kernels, run(): pl.pallas_call(kernel, out_shape=outs, in_specs=[vmem] * len(operands), o...  9.96 us
    ppermute x12, waiting for transfers between devices, shift(): return lax.ppermute(x, axis, [(i, (i + by) % size) for i in range(size)])  8.68 us
    squeeze x1, local copies, waits for them, and re-layouts, shards(): velocity[:, BX - 1]  1.05 us
  transfers between devices with their start and end apart: 12, of which 3 were waited for; matrix products, arithmetic and copies ran while one was open for 0% of the time, Pallas kernels for 14%

profile of v5, /device:TPU:0, one launch (start us, length us, event | category | flops | bytes accessed | tf_op | source)
XLA Modules:
  0.0 40.0 jit_solution(14756597760768854724)
XLA Ops:
  0.6 1.0 %slice_bitcast_fusion = (f32[3,20,640]{2,1,0:T(8,128)S(1)}, f32[3,20,640]{2,1,0:T(8,128)S(1)}) fusion(f32[3,10,20,640]{3,2,1,0:T(8,128)} %v.3), kind=kLoop, calls=%fused_computation | loop fusion | bytes 614400 | tf_op jit(solution)/shard_map/squeeze | solution.py:625
  1.7 0.0 copy-start
  1.7 0.0 copy-start.6
  1.7 1.7 %collective-permute-start = (f32[3,24,640]{2,1,0:T(8,128)S(1)}, f32[3,24,640]{2,1,0:T(8,128)S(1)}, u32[]{:S(2)}, u32[]{:S(2)}) collective-permute-start(f32[3,24,640]{2,1,0:T(8,128)S(1)} %get-tuple-element.27), channel_id=1, source_target_pairs={{0,16},{16,32},{32,48},{48,64},{64,80},{80,96},{96,112},{112,0},{1... | collective-permute-start | bytes 552968 | tf_op jit(solution)/shard_map/ppermute | solution.py:599
  3.5 0.0 copy-done
  3.5 0.4 pack.1
  3.9 2.0 %collective-permute-start.4 = (f32[24,128]{1,0:T(8,128)S(1)}, f32[24,128]{1,0:T(8,128)S(1)}, u32[]{:S(2)}, u32[]{:S(2)}) collective-permute-start(f32[24,128]{1,0:T(8,128)S(1)} %get-tuple-element.32), channel_id=1, source_target_pairs={{0,1},{1,2},{2,3},{3,0},{4,5},{5,6},{6,7},{7,4},{8,9},{9,10},{10,1... | collective-permute-start | bytes 36872 | tf_op jit(solution)/shard_map/ppermute | solution.py:599
  5.8 0.0 collective-permute-start.2
  5.8 3.2 %collective-permute-start.3 = (f32[30,640]{1,0:T(8,128)S(1)}, f32[30,640]{1,0:T(8,128)S(1)}, u32[]{:S(2)}, u32[]{:S(2)}) collective-permute-start(f32[30,640]{1,0:T(8,128)S(1)} %get-tuple-element.31), channel_id=1, source_target_pairs={{0,12},{4,0},{8,4},{12,8},{1,13},{5,1},{9,5},{13,9},{2,14},{6,2},{... | collective-permute-start | bytes 230408 | tf_op jit(solution)/shard_map/ppermute | solution.py:599
  9.1 3.7 %collective-permute-start.1 = (f32[3,24,640]{2,1,0:T(8,128)S(1)}, f32[3,24,640]{2,1,0:T(8,128)S(1)}, u32[]{:S(2)}, u32[]{:S(2)}) collective-permute-start(f32[3,24,640]{2,1,0:T(8,128)S(1)} %get-tuple-element.29), channel_id=1, source_target_pairs={{0,112},{16,0},{32,16},{48,32},{64,48},{80,64},{96,80},{112,96},{1... | collective-permute-start | bytes 552968 | tf_op jit(solution)/shard_map/ppermute | solution.py:599
  12.8 0.0 collective-permute-done.hx_lo
  12.8 0.0 copy-start.1
  12.8 0.0 copy-start.4
  12.8 2.2 %collective-permute-start.5 = (f32[24,128]{1,0:T(8,128)S(1)}, f32[24,128]{1,0:T(8,128)S(1)}, u32[]{:S(2)}, u32[]{:S(2)}) collective-permute-start(f32[24,128]{1,0:T(8,128)S(1)} %get-tuple-element.33.after), channel_id=1, source_target_pairs={{0,3},{1,0},{2,1},{3,2},{4,7},{5,4},{6,5},{7,6},{8,11},{9,8},{10,9... | collective-permute-start | bytes 36872 | tf_op jit(solution)/shard_map/ppermute | solution.py:599
  15.0 0.0 copy-done.6
  15.0 3.8 %volume.1 = (f32[3,10,24,640]{3,2,1,0:T(8,128)S(1)}, f32[3,10,24,640]{3,2,1,0:T(8,128)S(1)}) custom-call(f32[3,10,20,640]{3,2,1,0:T(8,128)S(1)} %copy-done, f32[24,128]{1,0:T(8,128)S(1)} %get-tuple-element.33.after, bf16[1768,256]{1,0:T(8,128)(2,1)S(1)} %copy-done.6), custom_call_target="tpu_custom_call" | custom-call | flops 4000000000 | bytes 4194304 | tf_op jit(solution)/shard_map/volume/pallas_call | solution.py:608
  18.9 0.0 collective-permute-done.4.hz_lo
  18.9 0.0 collective-permute-done.2.hy_lo
  18.9 0.0 collective-permute-done.3.hy_hi
  18.9 0.0 collective-permute-done.1.hx_hi
  18.9 0.0 collective-permute-done.5.hz_hi
  18.9 0.0 copy-done.1
  18.9 0.0 copy-done.4
  18.9 0.0 copy-start.5
  19.0 1.8 %lift.1 = (f32[3,10,24,640]{3,2,1,0:T(8,128)S(1)}, bf16[3,240,640]{2,1,0:T(8,128)(2,1)S(1)}, bf16[3,240,640]{2,1,0:T(8,128)(2,1)S(1)}, f32[24,640]{1,0:T(8,128)S...) custom-call(f32[3,10,24,640]{3,2,1,0:T(8,128)S(1)} %get-tuple-elemen, ...), custom_call_target="tpu_custom_call" | custom-call | flops 4000000000 | bytes 4194304 | tf_op jit(solution)/shard_map/lift/pallas_call | solution.py:608
  20.7 0.0 collective-permute-start.6
  20.8 2.0 %collective-permute-start.7 = (f32[24,128]{1,0:T(8,128)S(1)}, f32[24,128]{1,0:T(8,128)S(1)}, u32[]{:S(2)}, u32[]{:S(2)}) collective-permute-start(f32[24,128]{1,0:T(8,128)S(1)} %get-tuple-element.38), channel_id=1, source_target_pairs={{0,3},{1,0},{2,1},{3,2},{4,7},{5,4},{6,5},{7,6},{8,11},{9,8},{10,9... | collective-permute-start | bytes 36872 | tf_op jit(solution)/shard_map/ppermute | solution.py:599
  22.8 0.0 collective-permute-start.10
  22.8 4.1 %collective-permute-start.8 = (f32[24,640]{1,0:T(8,128)S(1)}, f32[24,640]{1,0:T(8,128)S(1)}, u32[]{:S(2)}, u32[]{:S(2)}) collective-permute-start(f32[24,640]{1,0:T(8,128)S(1)} %get-tuple-element.40), channel_id=1, source_target_pairs={{0,112},{16,0},{32,16},{48,32},{64,48},{80,64},{96,80},{112,96},{1... | collective-permute-start | bytes 184328 | tf_op jit(solution)/shard_map/ppermute | solution.py:599
  26.8 0.0 collective-permute-done.7.hz_hi
  26.8 0.2 collective-permute-done.6.hx_lo
  27.1 0.1 collective-permute-start.9
  27.2 0.0 copy-done.5
  27.2 0.0 copy-start.2
  27.2 0.0 copy-start.7
  27.2 0.0 copy-start.8
  27.2 0.8 %right.1.rhs = f32[10,24,640]{2,1,0:T(8,128)S(1)} custom-call(f32[3,10,24,640]{3,2,1,0:T(8,128)S(1)} %get-tuple-element.34.prov, bf16[3,240,640]{2,1,0:T(8,128)(2,1)S(1)} %get-tuple-element.35.PH, bf16[3,240,640]{2,1,0:T(8,128)(2,1)S(1)} %get-tuple-element.36.PL, bf16[1768,256]{1,0:T(8,128)(2,1)S(1)} %copy-done.5), custom_call_target="tpu_custom_call" | custom-call | flops 2000000000 | bytes 4194304 | tf_op jit(solution)/shard_map/right/pallas_call | solution.py:608
  28.0 4.4 %collective-permute-done.9.after.hy_lo = f32[16,640]{1,0:T(8,128)S(1)} collective-permute-done((f32[16,640]{1,0:T(8,128)S(1)}, f32[16,640]{1,0:T(8,128)S(1)}, u32[]{:S(2)}, u32[]{:S(2)}) %collective-permute-start.9) | collective-permute-done | bytes 40992 | tf_op jit(solution)/shard_map/ppermute | solution.py:599
  32.4 0.0 copy-start.3
  32.4 0.4 collective-permute-start.11
  32.8 0.0 copy-done.2
  32.8 0.0 copy-done.7
  32.8 0.0 copy-done.8
  32.8 0.5 %divisor.1.inverse = f32[10,24,768]{2,1,0:T(8,128)S(1)} custom-call(f32[2,4,128]{2,1,0:T(4,128)S(1)} %copy-done.2, f32[16,640]{1,0:T(8,128)S(1)} %collective-permute-done.9.after.hy_lo, bf16[432,256]{1,0:T(8,128)(2,1)S(1)} %copy-done.7, f32[24,640]{1,0:T(8,128)S(1)} %copy-done.8), custom_call_target="tpu_custom_call" | custom-call | flops 2000000000 | bytes 4194304 | tf_op jit(solution)/shard_map/divisor/pallas_call | solution.py:608
  33.3 0.0 collective-permute-done.10.hy_hi
  33.3 0.0 collective-permute-done.8.hx_hi
  33.3 4.1 %collective-permute-done.11.hz_lo = f32[24,128]{1,0:T(8,128)S(1)} collective-permute-done((f32[24,128]{1,0:T(8,128)S(1)}, f32[24,128]{1,0:T(8,128)S(1)}, u32[]{:S(2)}, u32[]{:S(2)}) %collective-permute-start.11) | collective-permute-done | bytes 12320 | tf_op jit(solution)/shard_map/ppermute | solution.py:599
  37.4 0.0 copy-done.3
  37.4 2.6 %smooth.1 = (f32[10,20,640]{2,1,0:T(8,128)}, f32[2,4,128]{2,1,0:T(4,128)}) custom-call(f32[10,24,640]{2,1,0:T(8,128)S(1)} %right.1.rhs, f32[24,640]{1,0:T(8,128)S(1)} %collective-permute-done.6.hx_lo, f32[24,640]{1,0:T(8,128)S(1)} %collective-permute-done.8.hx_hi, f32[16,640]{1,0:T(8,128)S(1)} %collective-permute-done.9.after.hy_lo, ...), custom_call_target="tpu_custom_call" | custom-call | flops 3000000000 | bytes 4194304 | tf_op jit(solution)/shard_map/smooth/pallas_call | solution.py:608
  (6 shorter events, 0.1 us)
Async XLA Ops:
  1.7 1.8 %copy-start = (f32[3,10,20,640]{3,2,1,0:T(8,128)S(1)}, f32[3,10,20,640]{3,2,1,0:T(8,128)}, u32[]{:S(2)}) copy-start(f32[3,10,20,640]{3,2,1,0:T(8,128)} %v.3) | copy-start | bytes 4608004
  1.7 13.3 %copy-start.6 = (bf16[1768,256]{1,0:T(8,128)(2,1)S(1)}, bf16[1768,256]{1,0:T(8,128)(2,1)}, u32[]{:S(2)}) copy-start(bf16[1768,256]{1,0:T(8,128)(2,1)} %constant.15.clone.weights) | copy-start | bytes 2715652
  1.7 11.1 %collective-permute-start = (f32[3,24,640]{2,1,0:T(8,128)S(1)}, f32[3,24,640]{2,1,0:T(8,128)S(1)}, u32[]{:S(2)}, u32[]{:S(2)}) collective-permute-start(f32[3,24,640]{2,1,0:T(8,128)S(1)} %get-tuple-element.27), channel_id=1, source_target_pairs={{0,16},{16,32},{32,48},{48,64},{64,80},{80,96},{96,112},{112,0},{1... | collective-permute-start | bytes 552968 | tf_op jit(solution)/shard_map/ppermute | solution.py:599
  3.9 15.0 %collective-permute-start.4 = (f32[24,128]{1,0:T(8,128)S(1)}, f32[24,128]{1,0:T(8,128)S(1)}, u32[]{:S(2)}, u32[]{:S(2)}) collective-permute-start(f32[24,128]{1,0:T(8,128)S(1)} %get-tuple-element.32), channel_id=1, source_target_pairs={{0,1},{1,2},{2,3},{3,0},{4,5},{5,6},{6,7},{7,4},{8,9},{9,10},{10,1... | collective-permute-start | bytes 36872 | tf_op jit(solution)/shard_map/ppermute | solution.py:599
  5.8 13.0 %collective-permute-start.2 = (f32[30,640]{1,0:T(8,128)S(1)}, f32[30,640]{1,0:T(8,128)S(1)}, u32[]{:S(2)}, u32[]{:S(2)}) collective-permute-start(f32[30,640]{1,0:T(8,128)S(1)} %get-tuple-element.30), channel_id=1, source_target_pairs={{0,4},{4,8},{8,12},{12,0},{1,5},{5,9},{9,13},{13,1},{2,6},{6,10},{... | collective-permute-start | bytes 230408 | tf_op jit(solution)/shard_map/ppermute | solution.py:599
  5.8 13.1 %collective-permute-start.3 = (f32[30,640]{1,0:T(8,128)S(1)}, f32[30,640]{1,0:T(8,128)S(1)}, u32[]{:S(2)}, u32[]{:S(2)}) collective-permute-start(f32[30,640]{1,0:T(8,128)S(1)} %get-tuple-element.31), channel_id=1, source_target_pairs={{0,12},{4,0},{8,4},{12,8},{1,13},{5,1},{9,5},{13,9},{2,14},{6,2},{... | collective-permute-start | bytes 230408 | tf_op jit(solution)/shard_map/ppermute | solution.py:599
  9.1 9.8 %collective-permute-start.1 = (f32[3,24,640]{2,1,0:T(8,128)S(1)}, f32[3,24,640]{2,1,0:T(8,128)S(1)}, u32[]{:S(2)}, u32[]{:S(2)}) collective-permute-start(f32[3,24,640]{2,1,0:T(8,128)S(1)} %get-tuple-element.29), channel_id=1, source_target_pairs={{0,112},{16,0},{32,16},{48,32},{64,48},{80,64},{96,80},{112,96},{1... | collective-permute-start | bytes 552968 | tf_op jit(solution)/shard_map/ppermute | solution.py:599
  12.8 6.1 %copy-start.1 = (s32[2,4,128]{2,1,0:T(4,128)S(1)}, s32[2,4,128]{2,1,0:T(4,128)}, u32[]{:S(2)}) copy-start(s32[2,4,128]{2,1,0:T(4,128)} %mask.1) | copy-start | bytes 12292
  12.8 6.1 %copy-start.4 = (bf16[3152,256]{1,0:T(8,128)(2,1)S(1)}, bf16[3152,256]{1,0:T(8,128)(2,1)}, u32[]{:S(2)}) copy-start(bf16[3152,256]{1,0:T(8,128)(2,1)} %constant.16.clone.weights) | copy-start | bytes 4841476
  12.8 6.1 %collective-permute-start.5 = (f32[24,128]{1,0:T(8,128)S(1)}, f32[24,128]{1,0:T(8,128)S(1)}, u32[]{:S(2)}, u32[]{:S(2)}) collective-permute-start(f32[24,128]{1,0:T(8,128)S(1)} %get-tuple-element.33.after), channel_id=1, source_target_pairs={{0,3},{1,0},{2,1},{3,2},{4,7},{5,4},{6,5},{7,6},{8,11},{9,8},{10,9... | collective-permute-start | bytes 36872 | tf_op jit(solution)/shard_map/ppermute | solution.py:599
  18.9 8.2 %copy-start.5 = (bf16[1768,256]{1,0:T(8,128)(2,1)S(1)}, bf16[1768,256]{1,0:T(8,128)(2,1)}, u32[]{:S(2)}) copy-start(bf16[1768,256]{1,0:T(8,128)(2,1)} %constant.17.clone.weights) | copy-start | bytes 2715652
  20.7 6.4 %collective-permute-start.6 = (f32[24,640]{1,0:T(8,128)S(1)}, f32[24,640]{1,0:T(8,128)S(1)}, u32[]{:S(2)}, u32[]{:S(2)}) collective-permute-start(f32[24,640]{1,0:T(8,128)S(1)} %get-tuple-element.37), channel_id=1, source_target_pairs={{0,16},{16,32},{32,48},{48,64},{64,80},{80,96},{96,112},{112,0},{1... | collective-permute-start | bytes 184328 | tf_op jit(solution)/shard_map/ppermute | solution.py:599
  20.8 6.1 %collective-permute-start.7 = (f32[24,128]{1,0:T(8,128)S(1)}, f32[24,128]{1,0:T(8,128)S(1)}, u32[]{:S(2)}, u32[]{:S(2)}) collective-permute-start(f32[24,128]{1,0:T(8,128)S(1)} %get-tuple-element.38), channel_id=1, source_target_pairs={{0,3},{1,0},{2,1},{3,2},{4,7},{5,4},{6,5},{7,6},{8,11},{9,8},{10,9... | collective-permute-start | bytes 36872 | tf_op jit(solution)/shard_map/ppermute | solution.py:599
  22.8 10.5 %collective-permute-start.10 = (f32[16,640]{1,0:T(8,128)S(1)}, f32[16,640]{1,0:T(8,128)S(1)}, u32[]{:S(2)}, u32[]{:S(2)}) collective-permute-start(f32[16,640]{1,0:T(8,128)S(1)} %get-tuple-element.42), channel_id=1, source_target_pairs={{0,12},{4,0},{8,4},{12,8},{1,13},{5,1},{9,5},{13,9},{2,14},{6,2},{... | collective-permute-start | bytes 122888 | tf_op jit(solution)/shard_map/ppermute | solution.py:599
  22.8 10.5 %collective-permute-start.8 = (f32[24,640]{1,0:T(8,128)S(1)}, f32[24,640]{1,0:T(8,128)S(1)}, u32[]{:S(2)}, u32[]{:S(2)}) collective-permute-start(f32[24,640]{1,0:T(8,128)S(1)} %get-tuple-element.40), channel_id=1, source_target_pairs={{0,112},{16,0},{32,16},{48,32},{64,48},{80,64},{96,80},{112,96},{1... | collective-permute-start | bytes 184328 | tf_op jit(solution)/shard_map/ppermute | solution.py:599
  27.1 5.3 %collective-permute-start.9 = (f32[16,640]{1,0:T(8,128)S(1)}, f32[16,640]{1,0:T(8,128)S(1)}, u32[]{:S(2)}, u32[]{:S(2)}) collective-permute-start(f32[16,640]{1,0:T(8,128)S(1)} %pad_add_fusion), channel_id=1, source_target_pairs={{0,4},{4,8},{8,12},{12,0},{1,5},{5,9},{9,13},{13,1},{2,6},{6,10},{... | collective-permute-start | bytes 122888 | tf_op jit(solution)/shard_map/ppermute | solution.py:599
  27.2 5.6 %copy-start.2 = (f32[2,4,128]{2,1,0:T(4,128)S(1)}, f32[2,4,128]{2,1,0:T(4,128)}, u32[]{:S(2)}) copy-start(f32[2,4,128]{2,1,0:T(4,128)} %scale.1) | copy-start | bytes 12292
  27.2 5.6 %copy-start.7 = (bf16[432,256]{1,0:T(8,128)(2,1)S(1)}, bf16[432,256]{1,0:T(8,128)(2,1)}, u32[]{:S(2)}) copy-start(bf16[432,256]{1,0:T(8,128)(2,1)} %constant.18.clone.weights) | copy-start | bytes 663556
  27.2 5.6 %copy-start.8 = (f32[24,640]{1,0:T(8,128)S(1)}, f32[24,640]{1,0:T(8,128)}, u32[]{:S(2)}) copy-start(f32[24,640]{1,0:T(8,128)} %constant.19.clone.modes) | copy-start | bytes 184324
  32.4 5.0 %copy-start.3 = (bf16[3520,256]{1,0:T(8,128)(2,1)S(1)}, bf16[3520,256]{1,0:T(8,128)(2,1)}, u32[]{:S(2)}) copy-start(bf16[3520,256]{1,0:T(8,128)(2,1)} %constant.20.clone.weights) | copy-start | bytes 5406724
  32.4 5.0 %collective-permute-start.11 = (f32[24,128]{1,0:T(8,128)S(1)}, f32[24,128]{1,0:T(8,128)S(1)}, u32[]{:S(2)}, u32[]{:S(2)}) collective-permute-start(f32[24,128]{1,0:T(8,128)S(1)} %pad_add_fusion.1), channel_id=1, source_target_pairs={{0,1},{1,2},{2,3},{3,0},{4,5},{5,6},{6,7},{7,4},{8,9},{9,10},{10,1... | collective-permute-start | bytes 36872 | tf_op jit(solution)/shard_map/ppermute | solution.py:599

commit v6 on v5

--- a/solution.py
+++ b/solution.py
@@ -511,18 +511,16 @@
         A[ROWS + 2 * PY * q : ROWS + 2 * PY * (q + 1), 0:BZ] = lo
 
     tf = packed.both(weights, "tf")
-    for n0, n1 in LANES:
-        B[:, n0:n1] = stacked(left_dot(tf, A[0:ROWS, n0:n1], A[ROWS:, n0:n1]))
-
+
+    tb = packed.both(weights, "tb")
     for i, (n0, n1, _, _) in enumerate(WINDOWS):
+        l0, l1 = LANES[i]
+        B[:, l0:l1] = stacked(left_dot(tf, A[0:ROWS, l0:l1], A[ROWS:, l0:l1]))
         size = n1 - n0
         c = stack_dot(B[:, n0:n1], packed.get(weights, "sf" + str(i))).reshape(BX, PY, size)
         c = (c * inverse[:, :, 256 * i : 256 * i + size]).reshape(ROWS, size)
         c = stack_dot(stacked(c), packed.get(weights, "sb" + str(i)))
         A[:, 256 * i : 256 * i + size] = stacked(c)
-
-    tb = packed.both(weights, "tb")
-    for i, (n0, n1, _, _) in enumerate(WINDOWS):
         here = slice(256 * i, 256 * i + n1 - n0)
         c = left_dot(tb, A[0:ROWS, here], A[ROWS:, here]).reshape(BX, PY, n1 - n0)
         smoothed[:, :, n0:n1] = c[:, 0:BY]

time: 40.1 us -> 41.3 us (1.030)
  Pallas kernels: 9.96 us -> 11.1 us
    pallas_call x7, Pallas kernels: 9.96 us -> 11.1 us  [run(): pl.pallas_call(kernel, out_shape=outs, in_specs=[vmem] * len(operands), o...]
  transfers between devices with their start and end apart: 12 -> 12, of which waited for: 3 -> 3; matrix products, arithmetic and copies ran while one was open for 0% -> 0% of each run, Pallas kernels for 14% -> 13%
where the time goes in v6:
time: 41.3 us; the launch traced here: 41.2 us
  starting transfers between devices  19.4 us (47%)
  Pallas kernels  11.1 us (27%)
  waiting for transfers between devices  8.68 us (21%)
  local copies, waits for them, and re-layouts  1.11 us (3%)
  between operations  0.83 us (2%)
    ppermute x12, starting transfers between devices, shift(): return lax.ppermute(x, axis, [(i, (i + by) % size) for i in range(size)])  19.4 us
    pallas_call x7, Pallas kernels, run(): pl.pallas_call(kernel, out_shape=outs, in_specs=[vmem] * len(operands), o...  11.1 us
    ppermute x12, waiting for transfers between devices, shift(): return lax.ppermute(x, axis, [(i, (i + by) % size) for i in range(size)])  8.68 us
    squeeze x1, local copies, waits for them, and re-layouts, shards(): velocity[:, BX - 1]  1.05 us
  transfers between devices with their start and end apart: 12, of which 3 were waited for; matrix products, arithmetic and copies ran while one was open for 0% of the time, Pallas kernels for 13%

profile of v6, /device:TPU:0, one launch (start us, length us, event | category | flops | bytes accessed | tf_op | source)
XLA Modules:
  0.0 41.2 jit_solution(17480283368953796435)
XLA Ops:
  0.6 1.0 %slice_bitcast_fusion = (f32[3,20,640]{2,1,0:T(8,128)S(1)}, f32[3,20,640]{2,1,0:T(8,128)S(1)}) fusion(f32[3,10,20,640]{3,2,1,0:T(8,128)} %v.3), kind=kLoop, calls=%fused_computation | loop fusion | bytes 614400 | tf_op jit(solution)/shard_map/squeeze | solution.py:623
  1.7 0.0 copy-start
  1.7 0.0 copy-start.6
  1.7 1.7 %collective-permute-start = (f32[3,24,640]{2,1,0:T(8,128)S(1)}, f32[3,24,640]{2,1,0:T(8,128)S(1)}, u32[]{:S(2)}, u32[]{:S(2)}) collective-permute-start(f32[3,24,640]{2,1,0:T(8,128)S(1)} %get-tuple-element.27), channel_id=1, source_target_pairs={{0,16},{16,32},{32,48},{48,64},{64,80},{80,96},{96,112},{112,0},{1... | collective-permute-start | bytes 552968 | tf_op jit(solution)/shard_map/ppermute | solution.py:597
  3.5 0.0 copy-done
  3.5 0.4 pack.1
  3.9 2.0 %collective-permute-start.4 = (f32[24,128]{1,0:T(8,128)S(1)}, f32[24,128]{1,0:T(8,128)S(1)}, u32[]{:S(2)}, u32[]{:S(2)}) collective-permute-start(f32[24,128]{1,0:T(8,128)S(1)} %get-tuple-element.32), channel_id=1, source_target_pairs={{0,1},{1,2},{2,3},{3,0},{4,5},{5,6},{6,7},{7,4},{8,9},{9,10},{10,1... | collective-permute-start | bytes 36872 | tf_op jit(solution)/shard_map/ppermute | solution.py:597
  5.8 0.0 collective-permute-start.2
  5.8 3.2 %collective-permute-start.3 = (f32[30,640]{1,0:T(8,128)S(1)}, f32[30,640]{1,0:T(8,128)S(1)}, u32[]{:S(2)}, u32[]{:S(2)}) collective-permute-start(f32[30,640]{1,0:T(8,128)S(1)} %get-tuple-element.31), channel_id=1, source_target_pairs={{0,12},{4,0},{8,4},{12,8},{1,13},{5,1},{9,5},{13,9},{2,14},{6,2},{... | collective-permute-start | bytes 230408 | tf_op jit(solution)/shard_map/ppermute | solution.py:597
  9.1 3.7 %collective-permute-start.1 = (f32[3,24,640]{2,1,0:T(8,128)S(1)}, f32[3,24,640]{2,1,0:T(8,128)S(1)}, u32[]{:S(2)}, u32[]{:S(2)}) collective-permute-start(f32[3,24,640]{2,1,0:T(8,128)S(1)} %get-tuple-element.29), channel_id=1, source_target_pairs={{0,112},{16,0},{32,16},{48,32},{64,48},{80,64},{96,80},{112,96},{1... | collective-permute-start | bytes 552968 | tf_op jit(solution)/shard_map/ppermute | solution.py:597
  12.8 0.0 collective-permute-done.hx_lo
  12.8 0.0 copy-start.1
  12.8 0.0 copy-start.4
  12.8 2.2 %collective-permute-start.5 = (f32[24,128]{1,0:T(8,128)S(1)}, f32[24,128]{1,0:T(8,128)S(1)}, u32[]{:S(2)}, u32[]{:S(2)}) collective-permute-start(f32[24,128]{1,0:T(8,128)S(1)} %get-tuple-element.33.after), channel_id=1, source_target_pairs={{0,3},{1,0},{2,1},{3,2},{4,7},{5,4},{6,5},{7,6},{8,11},{9,8},{10,9... | collective-permute-start | bytes 36872 | tf_op jit(solution)/shard_map/ppermute | solution.py:597
  15.0 0.0 copy-done.6
  15.0 3.8 %volume.1 = (f32[3,10,24,640]{3,2,1,0:T(8,128)S(1)}, f32[3,10,24,640]{3,2,1,0:T(8,128)S(1)}) custom-call(f32[3,10,20,640]{3,2,1,0:T(8,128)S(1)} %copy-done, f32[24,128]{1,0:T(8,128)S(1)} %get-tuple-element.33.after, bf16[1768,256]{1,0:T(8,128)(2,1)S(1)} %copy-done.6), custom_call_target="tpu_custom_call" | custom-call | flops 4000000000 | bytes 4194304 | tf_op jit(solution)/shard_map/volume/pallas_call | solution.py:606
  18.9 0.0 collective-permute-done.4.hz_lo
  18.9 0.0 collective-permute-done.2.hy_lo
  18.9 0.0 collective-permute-done.3.hy_hi
  18.9 0.0 collective-permute-done.1.hx_hi
  18.9 0.0 collective-permute-done.5.hz_hi
  18.9 0.0 copy-done.1
  18.9 0.0 copy-done.4
  18.9 0.0 copy-start.5
  19.0 1.8 %lift.1 = (f32[3,10,24,640]{3,2,1,0:T(8,128)S(1)}, bf16[3,240,640]{2,1,0:T(8,128)(2,1)S(1)}, bf16[3,240,640]{2,1,0:T(8,128)(2,1)S(1)}, f32[24,640]{1,0:T(8,128)S...) custom-call(f32[3,10,24,640]{3,2,1,0:T(8,128)S(1)} %get-tuple-elemen, ...), custom_call_target="tpu_custom_call" | custom-call | flops 4000000000 | bytes 4194304 | tf_op jit(solution)/shard_map/lift/pallas_call | solution.py:606
  20.7 0.0 collective-permute-start.6
  20.8 2.0 %collective-permute-start.7 = (f32[24,128]{1,0:T(8,128)S(1)}, f32[24,128]{1,0:T(8,128)S(1)}, u32[]{:S(2)}, u32[]{:S(2)}) collective-permute-start(f32[24,128]{1,0:T(8,128)S(1)} %get-tuple-element.38), channel_id=1, source_target_pairs={{0,3},{1,0},{2,1},{3,2},{4,7},{5,4},{6,5},{7,6},{8,11},{9,8},{10,9... | collective-permute-start | bytes 36872 | tf_op jit(solution)/shard_map/ppermute | solution.py:597
  22.8 0.0 collective-permute-start.10
  22.8 4.1 %collective-permute-start.8 = (f32[24,640]{1,0:T(8,128)S(1)}, f32[24,640]{1,0:T(8,128)S(1)}, u32[]{:S(2)}, u32[]{:S(2)}) collective-permute-start(f32[24,640]{1,0:T(8,128)S(1)} %get-tuple-element.40), channel_id=1, source_target_pairs={{0,112},{16,0},{32,16},{48,32},{64,48},{80,64},{96,80},{112,96},{1... | collective-permute-start | bytes 184328 | tf_op jit(solution)/shard_map/ppermute | solution.py:597
  26.8 0.0 collective-permute-done.7.hz_hi
  26.8 0.2 collective-permute-done.6.hx_lo
  27.1 0.1 collective-permute-start.9
  27.2 0.0 copy-done.5
  27.2 0.0 copy-start.2
  27.2 0.0 copy-start.7
  27.2 0.0 copy-start.8
  27.2 0.8 %right.1.rhs = f32[10,24,640]{2,1,0:T(8,128)S(1)} custom-call(f32[3,10,24,640]{3,2,1,0:T(8,128)S(1)} %get-tuple-element.34.prov, bf16[3,240,640]{2,1,0:T(8,128)(2,1)S(1)} %get-tuple-element.35.PH, bf16[3,240,640]{2,1,0:T(8,128)(2,1)S(1)} %get-tuple-element.36.PL, bf16[1768,256]{1,0:T(8,128)(2,1)S(1)} %copy-done.5), custom_call_target="tpu_custom_call" | custom-call | flops 2000000000 | bytes 4194304 | tf_op jit(solution)/shard_map/right/pallas_call | solution.py:606
  28.0 4.4 %collective-permute-done.9.after.hy_lo = f32[16,640]{1,0:T(8,128)S(1)} collective-permute-done((f32[16,640]{1,0:T(8,128)S(1)}, f32[16,640]{1,0:T(8,128)S(1)}, u32[]{:S(2)}, u32[]{:S(2)}) %collective-permute-start.9) | collective-permute-done | bytes 40992 | tf_op jit(solution)/shard_map/ppermute | solution.py:597
  32.4 0.0 copy-start.3
  32.4 0.4 collective-permute-start.11
  32.8 0.0 copy-done.2
  32.8 0.0 copy-done.7
  32.8 0.0 copy-done.8
  32.8 0.5 %divisor.1.inverse = f32[10,24,768]{2,1,0:T(8,128)S(1)} custom-call(f32[2,4,128]{2,1,0:T(4,128)S(1)} %copy-done.2, f32[16,640]{1,0:T(8,128)S(1)} %collective-permute-done.9.after.hy_lo, bf16[432,256]{1,0:T(8,128)(2,1)S(1)} %copy-done.7, f32[24,640]{1,0:T(8,128)S(1)} %copy-done.8), custom_call_target="tpu_custom_call" | custom-call | flops 2000000000 | bytes 4194304 | tf_op jit(solution)/shard_map/divisor/pallas_call | solution.py:606
  33.3 0.0 collective-permute-done.10.hy_hi
  33.3 0.0 collective-permute-done.8.hx_hi
  33.3 4.1 %collective-permute-done.11.hz_lo = f32[24,128]{1,0:T(8,128)S(1)} collective-permute-done((f32[24,128]{1,0:T(8,128)S(1)}, f32[24,128]{1,0:T(8,128)S(1)}, u32[]{:S(2)}, u32[]{:S(2)}) %collective-permute-start.11) | collective-permute-done | bytes 12320 | tf_op jit(solution)/shard_map/ppermute | solution.py:597
  37.4 0.0 copy-done.3
  37.4 3.8 %smooth.1 = (f32[10,20,640]{2,1,0:T(8,128)}, f32[2,4,128]{2,1,0:T(4,128)}) custom-call(f32[10,24,640]{2,1,0:T(8,128)S(1)} %right.1.rhs, f32[24,640]{1,0:T(8,128)S(1)} %collective-permute-done.6.hx_lo, f32[24,640]{1,0:T(8,128)S(1)} %collective-permute-done.8.hx_hi, f32[16,640]{1,0:T(8,128)S(1)} %collective-permute-done.9.after.hy_lo, ...), custom_call_target="tpu_custom_call" | custom-call | flops 3000000000 | bytes 4194304 | tf_op jit(solution)/shard_map/smooth/pallas_call | solution.py:606
  (6 shorter events, 0.1 us)
Async XLA Ops:
  1.7 1.8 %copy-start = (f32[3,10,20,640]{3,2,1,0:T(8,128)S(1)}, f32[3,10,20,640]{3,2,1,0:T(8,128)}, u32[]{:S(2)}) copy-start(f32[3,10,20,640]{3,2,1,0:T(8,128)} %v.3) | copy-start | bytes 4608004
  1.7 13.3 %copy-start.6 = (bf16[1768,256]{1,0:T(8,128)(2,1)S(1)}, bf16[1768,256]{1,0:T(8,128)(2,1)}, u32[]{:S(2)}) copy-start(bf16[1768,256]{1,0:T(8,128)(2,1)} %constant.15.clone.weights) | copy-start | bytes 2715652
  1.7 11.1 %collective-permute-start = (f32[3,24,640]{2,1,0:T(8,128)S(1)}, f32[3,24,640]{2,1,0:T(8,128)S(1)}, u32[]{:S(2)}, u32[]{:S(2)}) collective-permute-start(f32[3,24,640]{2,1,0:T(8,128)S(1)} %get-tuple-element.27), channel_id=1, source_target_pairs={{0,16},{16,32},{32,48},{48,64},{64,80},{80,96},{96,112},{112,0},{1... | collective-permute-start | bytes 552968 | tf_op jit(solution)/shard_map/ppermute | solution.py:597
  3.9 15.0 %collective-permute-start.4 = (f32[24,128]{1,0:T(8,128)S(1)}, f32[24,128]{1,0:T(8,128)S(1)}, u32[]{:S(2)}, u32[]{:S(2)}) collective-permute-start(f32[24,128]{1,0:T(8,128)S(1)} %get-tuple-element.32), channel_id=1, source_target_pairs={{0,1},{1,2},{2,3},{3,0},{4,5},{5,6},{6,7},{7,4},{8,9},{9,10},{10,1... | collective-permute-start | bytes 36872 | tf_op jit(solution)/shard_map/ppermute | solution.py:597
  5.8 13.0 %collective-permute-start.2 = (f32[30,640]{1,0:T(8,128)S(1)}, f32[30,640]{1,0:T(8,128)S(1)}, u32[]{:S(2)}, u32[]{:S(2)}) collective-permute-start(f32[30,640]{1,0:T(8,128)S(1)} %get-tuple-element.30), channel_id=1, source_target_pairs={{0,4},{4,8},{8,12},{12,0},{1,5},{5,9},{9,13},{13,1},{2,6},{6,10},{... | collective-permute-start | bytes 230408 | tf_op jit(solution)/shard_map/ppermute | solution.py:597
  5.8 13.1 %collective-permute-start.3 = (f32[30,640]{1,0:T(8,128)S(1)}, f32[30,640]{1,0:T(8,128)S(1)}, u32[]{:S(2)}, u32[]{:S(2)}) collective-permute-start(f32[30,640]{1,0:T(8,128)S(1)} %get-tuple-element.31), channel_id=1, source_target_pairs={{0,12},{4,0},{8,4},{12,8},{1,13},{5,1},{9,5},{13,9},{2,14},{6,2},{... | collective-permute-start | bytes 230408 | tf_op jit(solution)/shard_map/ppermute | solution.py:597
  9.1 9.8 %collective-permute-start.1 = (f32[3,24,640]{2,1,0:T(8,128)S(1)}, f32[3,24,640]{2,1,0:T(8,128)S(1)}, u32[]{:S(2)}, u32[]{:S(2)}) collective-permute-start(f32[3,24,640]{2,1,0:T(8,128)S(1)} %get-tuple-element.29), channel_id=1, source_target_pairs={{0,112},{16,0},{32,16},{48,32},{64,48},{80,64},{96,80},{112,96},{1... | collective-permute-start | bytes 552968 | tf_op jit(solution)/shard_map/ppermute | solution.py:597
  12.8 6.1 %copy-start.1 = (s32[2,4,128]{2,1,0:T(4,128)S(1)}, s32[2,4,128]{2,1,0:T(4,128)}, u32[]{:S(2)}) copy-start(s32[2,4,128]{2,1,0:T(4,128)} %mask.1) | copy-start | bytes 12292
  12.8 6.1 %copy-start.4 = (bf16[3152,256]{1,0:T(8,128)(2,1)S(1)}, bf16[3152,256]{1,0:T(8,128)(2,1)}, u32[]{:S(2)}) copy-start(bf16[3152,256]{1,0:T(8,128)(2,1)} %constant.16.clone.weights) | copy-start | bytes 4841476
  12.8 6.1 %collective-permute-start.5 = (f32[24,128]{1,0:T(8,128)S(1)}, f32[24,128]{1,0:T(8,128)S(1)}, u32[]{:S(2)}, u32[]{:S(2)}) collective-permute-start(f32[24,128]{1,0:T(8,128)S(1)} %get-tuple-element.33.after), channel_id=1, source_target_pairs={{0,3},{1,0},{2,1},{3,2},{4,7},{5,4},{6,5},{7,6},{8,11},{9,8},{10,9... | collective-permute-start | bytes 36872 | tf_op jit(solution)/shard_map/ppermute | solution.py:597
  18.9 8.2 %copy-start.5 = (bf16[1768,256]{1,0:T(8,128)(2,1)S(1)}, bf16[1768,256]{1,0:T(8,128)(2,1)}, u32[]{:S(2)}) copy-start(bf16[1768,256]{1,0:T(8,128)(2,1)} %constant.17.clone.weights) | copy-start | bytes 2715652
  20.7 6.4 %collective-permute-start.6 = (f32[24,640]{1,0:T(8,128)S(1)}, f32[24,640]{1,0:T(8,128)S(1)}, u32[]{:S(2)}, u32[]{:S(2)}) collective-permute-start(f32[24,640]{1,0:T(8,128)S(1)} %get-tuple-element.37), channel_id=1, source_target_pairs={{0,16},{16,32},{32,48},{48,64},{64,80},{80,96},{96,112},{112,0},{1... | collective-permute-start | bytes 184328 | tf_op jit(solution)/shard_map/ppermute | solution.py:597
  20.8 6.1 %collective-permute-start.7 = (f32[24,128]{1,0:T(8,128)S(1)}, f32[24,128]{1,0:T(8,128)S(1)}, u32[]{:S(2)}, u32[]{:S(2)}) collective-permute-start(f32[24,128]{1,0:T(8,128)S(1)} %get-tuple-element.38), channel_id=1, source_target_pairs={{0,3},{1,0},{2,1},{3,2},{4,7},{5,4},{6,5},{7,6},{8,11},{9,8},{10,9... | collective-permute-start | bytes 36872 | tf_op jit(solution)/shard_map/ppermute | solution.py:597
  22.8 10.5 %collective-permute-start.10 = (f32[16,640]{1,0:T(8,128)S(1)}, f32[16,640]{1,0:T(8,128)S(1)}, u32[]{:S(2)}, u32[]{:S(2)}) collective-permute-start(f32[16,640]{1,0:T(8,128)S(1)} %get-tuple-element.42), channel_id=1, source_target_pairs={{0,12},{4,0},{8,4},{12,8},{1,13},{5,1},{9,5},{13,9},{2,14},{6,2},{... | collective-permute-start | bytes 122888 | tf_op jit(solution)/shard_map/ppermute | solution.py:597
  22.8 10.5 %collective-permute-start.8 = (f32[24,640]{1,0:T(8,128)S(1)}, f32[24,640]{1,0:T(8,128)S(1)}, u32[]{:S(2)}, u32[]{:S(2)}) collective-permute-start(f32[24,640]{1,0:T(8,128)S(1)} %get-tuple-element.40), channel_id=1, source_target_pairs={{0,112},{16,0},{32,16},{48,32},{64,48},{80,64},{96,80},{112,96},{1... | collective-permute-start | bytes 184328 | tf_op jit(solution)/shard_map/ppermute | solution.py:597
  27.1 5.3 %collective-permute-start.9 = (f32[16,640]{1,0:T(8,128)S(1)}, f32[16,640]{1,0:T(8,128)S(1)}, u32[]{:S(2)}, u32[]{:S(2)}) collective-permute-start(f32[16,640]{1,0:T(8,128)S(1)} %pad_add_fusion), channel_id=1, source_target_pairs={{0,4},{4,8},{8,12},{12,0},{1,5},{5,9},{9,13},{13,1},{2,6},{6,10},{... | collective-permute-start | bytes 122888 | tf_op jit(solution)/shard_map/ppermute | solution.py:597
  27.2 5.6 %copy-start.2 = (f32[2,4,128]{2,1,0:T(4,128)S(1)}, f32[2,4,128]{2,1,0:T(4,128)}, u32[]{:S(2)}) copy-start(f32[2,4,128]{2,1,0:T(4,128)} %scale.1) | copy-start | bytes 12292
  27.2 5.6 %copy-start.7 = (bf16[432,256]{1,0:T(8,128)(2,1)S(1)}, bf16[432,256]{1,0:T(8,128)(2,1)}, u32[]{:S(2)}) copy-start(bf16[432,256]{1,0:T(8,128)(2,1)} %constant.18.clone.weights) | copy-start | bytes 663556
  27.2 5.6 %copy-start.8 = (f32[24,640]{1,0:T(8,128)S(1)}, f32[24,640]{1,0:T(8,128)}, u32[]{:S(2)}) copy-start(f32[24,640]{1,0:T(8,128)} %constant.19.clone.modes) | copy-start | bytes 184324
  32.4 5.0 %copy-start.3 = (bf16[3520,256]{1,0:T(8,128)(2,1)S(1)}, bf16[3520,256]{1,0:T(8,128)(2,1)}, u32[]{:S(2)}) copy-start(bf16[3520,256]{1,0:T(8,128)(2,1)} %constant.20.clone.weights) | copy-start | bytes 5406724
  32.4 5.0 %collective-permute-start.11 = (f32[24,128]{1,0:T(8,128)S(1)}, f32[24,128]{1,0:T(8,128)S(1)}, u32[]{:S(2)}, u32[]{:S(2)}) collective-permute-start(f32[24,128]{1,0:T(8,128)S(1)} %pad_add_fusion.1), channel_id=1, source_target_pairs={{0,1},{1,2},{2,3},{3,0},{4,5},{5,6},{6,7},{7,4},{8,9},{9,10},{10,1... | collective-permute-start | bytes 36872 | tf_op jit(solution)/shard_map/ppermute | solution.py:597
